TPU v7x, 32 devices: a whole 2x2x4 slice. The times are simulated.
32 devices in a mesh: dp: 8 (over z, y), expert: 4 (over x, core).
Axes of the slice: x: 2, y: 2, z: 4, core: 2. Of those that a mesh axis runs over, the one named last changes fastest.
Arguments:
- hidden: bfloat16 [2, 4, 1024, 768], P(None, 'expert', 'dp'), may hold values from -6 to 6
- routes: int32 [2, 4, 1024, 2], P(None, 'expert', 'dp'), may hold values from 0 to 3, all different within a row
- prefix: int32 [2, 4], P(None, 'expert'), may hold values from 102 to 512, as said below
- cotangent: bfloat16 [2, 4, 1024, 768], P(None, 'expert', 'dp'), may hold values from -6 to 6
- attn_gain: bfloat16 [768], P(('dp', 'expert')), may hold values from 0.5 to 1.5
- w_query: bfloat16 [768, 768], P(('dp', 'expert')), may hold values from -0.21875 to 0.21875
- w_key: bfloat16 [768, 768], P(('dp', 'expert')), may hold values from -0.21875 to 0.21875
- w_value: bfloat16 [768, 768], P(('dp', 'expert')), may hold values from -0.21875 to 0.21875
- w_output: bfloat16 [768, 768], P(('dp', 'expert')), may hold values from -1.25 to 1.25
- ffn_gain: bfloat16 [768], P(('dp', 'expert')), may hold values from 0.5 to 1.5
- router: bfloat16 [768, 4], P(('dp', 'expert')), may hold values from -0.15625 to 0.15625
- shared_gate: bfloat16 [768, 2048], P(('dp', 'expert')), may hold values from -0.21875 to 0.21875
- shared_up: bfloat16 [768, 2048], P(('dp', 'expert')), may hold values from -0.21875 to 0.21875
- shared_down: bfloat16 [2048, 768], P(('dp', 'expert')), may hold values from -0.125 to 0.125
- expert_gate: bfloat16 [4, 768, 2048], P('expert', 'dp'), may hold values from -0.21875 to 0.21875
- expert_up: bfloat16 [4, 768, 2048], P('expert', 'dp'), may hold values from -0.21875 to 0.21875
- expert_down: bfloat16 [4, 2048, 768], P('expert', 'dp'), may hold values from -0.125 to 0.125
Outputs:
- block_out: bfloat16 [2, 4, 1024, 768], P(None, 'expert', 'dp')
- grad_hidden: bfloat16 [2, 4, 1024, 768], P(None, 'expert', 'dp')
- grad_attn_gain: float32 [768], P(('dp', 'expert'))
- grad_w_query: float32 [768, 768], P(('dp', 'expert'))
- grad_w_key: float32 [768, 768], P(('dp', 'expert'))
- grad_w_value: float32 [768, 768], P(('dp', 'expert'))
- grad_w_output: float32 [768, 768], P(('dp', 'expert'))
- grad_ffn_gain: float32 [768], P(('dp', 'expert'))
- grad_router: float32 [768, 4], P(('dp', 'expert'))
- grad_shared_gate: float32 [768, 2048], P(('dp', 'expert'))
- grad_shared_up: float32 [768, 2048], P(('dp', 'expert'))
- grad_shared_down: float32 [2048, 768], P(('dp', 'expert'))
- grad_expert_gate: float32 [4, 768, 2048], P('expert', 'dp')
- grad_expert_up: float32 [4, 768, 2048], P('expert', 'dp')
- grad_expert_down: float32 [4, 2048, 768], P('expert', 'dp')
Inputs may be any that keep to these rules, and one draw needn't show every extreme that they name: `routes`: each token names 2 different experts; every expert is named by some token. Each sequence's prefix length is drawn evenly from 102 to 512; in every draw one sequence has exactly 102 and another exactly 512.
All inputs are finite; a program needn't handle non-finite values.
Results may differ from a plain program's by a relative error of at most 0.024.
Values may be sent and summed in bfloat16 or wider, within the bound.
A program may use at most 320 MiB of HBM per device.

v0:
```python
import math

import jax
import jax.numpy as jnp
from jax import lax
from jax.sharding import PartitionSpec as P

HEAD_DIM = 64
EXPERT_FF = 2048
SHARED_FF = 2048
TOP_K = 2


eps = 1e-06
highest = lax.Precision.HIGHEST
neg_fill = -1e30


def rms_scale(values):
    return lax.rsqrt(jnp.mean(values * values, axis=-1, keepdims=True) + eps)


def rotary_tables(positions, head_size):
    halfway = head_size // 2
    frequency = jnp.exp(
        jnp.arange(halfway, dtype=jnp.float32) * (-math.log(10000.0) * 2.0 / head_size)
    )
    angles = positions.astype(jnp.float32)[:, None] * frequency[None, :]
    return (jnp.cos(angles)[:, None, :], jnp.sin(angles)[:, None, :])


def rotate(values, cosine, sine_tab):
    halfway = values.shape[-1] // 2
    first_part = values[..., :halfway]
    second_part = values[..., halfway:]
    return jnp.concatenate(
        [
            first_part * cosine - second_part * sine_tab,
            second_part * cosine + first_part * sine_tab,
        ],
        axis=-1,
    )


def unrotate(gradient, cosine, sine_tab):
    halfway = gradient.shape[-1] // 2
    first_part = gradient[..., :halfway]
    second_part = gradient[..., halfway:]
    return jnp.concatenate(
        [
            first_part * cosine + second_part * sine_tab,
            second_part * cosine - first_part * sine_tab,
        ],
        axis=-1,
    )


def silu_grad(values):
    sigmoid_of = jax.nn.sigmoid(values)
    return sigmoid_of * (1.0 + values * (1.0 - sigmoid_of))


def visible(query_pos, key_pos, prefix_len):
    return (key_pos[None, :] <= query_pos[:, None]) | (query_pos[:, None] < prefix_len) & (
        key_pos[None, :] < prefix_len
    )


def shards(
    hidden,
    routes,
    prefix,
    cotangent,
    attn_gain,
    w_query,
    w_key,
    w_value,
    w_output,
    ffn_gain,
    router,
    shared_gate,
    shared_up,
    shared_down,
    expert_gate,
    expert_up,
    expert_down,
):
    tok_rows = hidden.shape[2]
    model_width = hidden.shape[3]
    head_count = model_width // HEAD_DIM
    expert_total = router.shape[1]
    local_experts = expert_gate.shape[0]
    capacity = (5 * tok_rows * TOP_K + 4 * expert_total - 1) // (4 * expert_total)
    slot_total = expert_total * capacity
    seq_rows = tok_rows * lax.axis_size("dp")
    first_row = lax.axis_index("dp") * tok_rows
    query_pos = first_row + jnp.arange(tok_rows, dtype=jnp.int32)
    cosine, sine_tab = rotary_tables(query_pos, HEAD_DIM)
    key_all_pos = jnp.arange(seq_rows, dtype=jnp.int32)
    expert_ids = jnp.arange(expert_total, dtype=jnp.int32)
    slot_ids = jnp.arange(slot_total, dtype=jnp.int32)
    inv_root = 1.0 / math.sqrt(HEAD_DIM)

    def one_batch(totals, packed):
        batch_hidden, batch_routes, batch_prefix, batch_cot = packed
        dense_fwd = (
            lax.all_gather(attn_gain, ("dp", "expert"), axis=0, tiled=True),
            lax.all_gather(w_query, ("dp", "expert"), axis=0, tiled=True),
            lax.all_gather(w_key, ("dp", "expert"), axis=0, tiled=True),
            lax.all_gather(w_value, ("dp", "expert"), axis=0, tiled=True),
            lax.all_gather(w_output, ("dp", "expert"), axis=0, tiled=True),
            lax.all_gather(ffn_gain, ("dp", "expert"), axis=0, tiled=True),
            lax.all_gather(router, ("dp", "expert"), axis=0, tiled=True),
            lax.all_gather(shared_gate, ("dp", "expert"), axis=0, tiled=True),
            lax.all_gather(shared_up, ("dp", "expert"), axis=0, tiled=True),
            lax.all_gather(shared_down, ("dp", "expert"), axis=0, tiled=True),
        )
        expert_forward_pass = (
            lax.all_gather(expert_gate, "dp", axis=1, tiled=True),
            lax.all_gather(expert_up, "dp", axis=1, tiled=True),
            lax.all_gather(expert_down, "dp", axis=1, tiled=True),
        )
        (
            gain_attn,
            query_w,
            key_w,
            value_w,
            output_w,
            gain_ffn,
            router_w,
            sgate_w,
            sup_w,
            sdown_w,
        ) = dense_fwd
        expert_gate_matrix, expert_up_matrix, expert_down_matrix = expert_forward_pass
        prefix_len = batch_prefix[0]
        residual_in = batch_hidden[0].astype(jnp.float32)
        attn_scale = rms_scale(residual_in)
        attn_norm = residual_in * attn_scale
        normed = (attn_norm * gain_attn).astype(jnp.bfloat16)

        def heads_of(matrix):
            return jnp.dot(normed, matrix, preferred_element_type=jnp.float32).reshape(
                tok_rows, head_count, HEAD_DIM
            )

        queries = rotate(heads_of(query_w), cosine, sine_tab).astype(jnp.bfloat16)
        key_rows = (
            rotate(heads_of(key_w), cosine, sine_tab)
            .astype(jnp.bfloat16)
            .reshape(tok_rows, model_width)
        )
        value_rows = jnp.dot(normed, value_w, preferred_element_type=jnp.float32).astype(
            jnp.bfloat16
        )
        initial_state = (
            jnp.full((head_count, tok_rows), neg_fill, jnp.float32),
            jnp.zeros((head_count, tok_rows), jnp.float32),
            jnp.zeros((head_count, tok_rows, HEAD_DIM), jnp.float32),
        )
        offset = jnp.int32(0)
        key_part = lax.all_gather(key_rows, "dp", axis=0, tiled=True)
        value_part = lax.all_gather(value_rows, "dp", axis=0, tiled=True)
        piece_rows = key_part.shape[0]
        key_heads = key_part.reshape(piece_rows, head_count, HEAD_DIM)
        value_heads = value_part.reshape(piece_rows, head_count, HEAD_DIM)
        key_pos = jnp.arange(piece_rows, dtype=jnp.int32)

        def update(current):
            run_max, run_sum, run_acc = current
            allowed = visible(query_pos, key_pos, prefix_len)[None]
            scores = (
                jnp.einsum("qhd,khd->hqk", queries, key_heads, preferred_element_type=jnp.float32)
                * inv_root
            )
            scores = jnp.where(allowed, scores, neg_fill)
            new_max = jnp.maximum(run_max, jnp.max(scores, axis=-1))
            weights = jnp.where(allowed, jnp.exp(scores - new_max[..., None]), 0.0)
            new_sum = jnp.sum(weights, axis=-1)
            new_acc = jnp.einsum(
                "hqk,khd->hqd",
                weights.astype(jnp.bfloat16),
                value_heads,
                preferred_element_type=jnp.float32,
            )
            return (new_max, new_sum, new_acc)

        def unchanged(current):
            return current

        live = (offset <= first_row + tok_rows - 1) | (offset < prefix_len)
        run_max, run_sum, run_acc = lax.cond(live, update, unchanged, initial_state)
        log_total = run_max + jnp.log(run_sum)
        context = (
            jnp.transpose(run_acc / run_sum[..., None], (1, 0, 2))
            .reshape(tok_rows, model_width)
            .astype(jnp.bfloat16)
        )
        attended = residual_in + jnp.dot(context, output_w, preferred_element_type=jnp.float32)
        ffn_scale = rms_scale(attended)
        ffn_norm = attended * ffn_scale
        mixed = (ffn_norm * gain_ffn).astype(jnp.bfloat16)
        logits = jnp.dot(mixed, router_w, preferred_element_type=jnp.float32)
        pair_ids = batch_routes[0]
        route_match = pair_ids[..., None] == expert_ids
        route_hot = route_match.astype(jnp.float32)
        gate_probs = jax.nn.softmax(jnp.sum(route_hot * logits[:, None, :], axis=-1), axis=-1)
        hot_int = route_match.astype(jnp.int32).reshape(tok_rows * TOP_K, expert_total)
        earlier = jnp.cumsum(hot_int, axis=0) - hot_int
        pair_rank = jnp.sum(earlier * hot_int, axis=-1).reshape(tok_rows, TOP_K)
        slot_index = jnp.where(pair_rank < capacity, pair_ids * capacity + pair_rank, slot_total)
        slot_hot = (slot_index[..., None] == slot_ids).astype(jnp.bfloat16)
        send_rows = (
            jnp.einsum("tks,td->sd", slot_hot, mixed, preferred_element_type=jnp.float32)
            .astype(jnp.bfloat16)
            .reshape(expert_total, capacity, model_width)
        )
        arrived_rows = lax.all_to_all(send_rows, "expert", split_axis=0, concat_axis=1, tiled=True)
        gate_activation = jnp.einsum(
            "zno,zog->zng", arrived_rows, expert_gate_matrix, preferred_element_type=jnp.float32
        )
        up_activation = jnp.einsum(
            "zno,zog->zng", arrived_rows, expert_up_matrix, preferred_element_type=jnp.float32
        )
        expert_hidden = (jax.nn.silu(gate_activation) * up_activation).astype(jnp.bfloat16)
        expert_out = jnp.einsum(
            "erf,efd->erd", expert_hidden, expert_down_matrix, preferred_element_type=jnp.float32
        ).astype(jnp.bfloat16)
        returned = lax.all_to_all(
            expert_out, "expert", split_axis=1, concat_axis=0, tiled=True
        ).reshape(slot_total, model_width)
        pair_rows = jnp.einsum(
            "tks,sd->tkd", slot_hot, returned, preferred_element_type=jnp.float32
        )
        expert_sum = jnp.sum(gate_probs[..., None] * pair_rows, axis=1)
        shared_in = jnp.dot(mixed, sgate_w, preferred_element_type=jnp.float32)
        shared_lift = jnp.dot(mixed, sup_w, preferred_element_type=jnp.float32)
        shared_hidden = (jax.nn.silu(shared_in) * shared_lift).astype(jnp.bfloat16)
        shared_out = jnp.dot(shared_hidden, sdown_w, preferred_element_type=jnp.float32)
        block_rows = (attended + shared_out + expert_sum).astype(jnp.bfloat16)
        dense_bwd = (
            lax.all_gather(attn_gain, ("dp", "expert"), axis=0, tiled=True),
            lax.all_gather(w_query, ("dp", "expert"), axis=0, tiled=True),
            lax.all_gather(w_key, ("dp", "expert"), axis=0, tiled=True),
            lax.all_gather(w_value, ("dp", "expert"), axis=0, tiled=True),
            lax.all_gather(w_output, ("dp", "expert"), axis=0, tiled=True),
            lax.all_gather(ffn_gain, ("dp", "expert"), axis=0, tiled=True),
            lax.all_gather(router, ("dp", "expert"), axis=0, tiled=True),
            lax.all_gather(shared_gate, ("dp", "expert"), axis=0, tiled=True),
            lax.all_gather(shared_up, ("dp", "expert"), axis=0, tiled=True),
            lax.all_gather(shared_down, ("dp", "expert"), axis=0, tiled=True),
        )
        expert_backward_pass = (
            lax.all_gather(expert_gate, "dp", axis=1, tiled=True),
            lax.all_gather(expert_up, "dp", axis=1, tiled=True),
            lax.all_gather(expert_down, "dp", axis=1, tiled=True),
        )
        (
            gain_attn,
            query_w,
            key_w,
            value_w,
            output_w,
            gain_ffn,
            router_w,
            sgate_w,
            sup_w,
            sdown_w,
        ) = dense_bwd
        expert_gate_matrix, expert_up_matrix, expert_down_matrix = expert_backward_pass
        cot_low = batch_cot[0]
        cot_wide = cot_low.astype(jnp.float32)
        pair_grads = (gate_probs[..., None] * cot_wide[:, None, :]).astype(jnp.bfloat16)
        gate_grads = jnp.sum(pair_rows * cot_wide[:, None, :], axis=-1)
        slot_grads = (
            jnp.einsum("tks,tkd->sd", slot_hot, pair_grads, preferred_element_type=jnp.float32)
            .astype(jnp.bfloat16)
            .reshape(expert_total, capacity, model_width)
        )
        expert_grads_in = lax.all_to_all(
            slot_grads, "expert", split_axis=0, concat_axis=1, tiled=True
        )
        hidden_gradient_rows = jnp.einsum(
            "erd,efd->erf", expert_grads_in, expert_down_matrix, preferred_element_type=jnp.float32
        )
        expert_down_gradient = jnp.einsum(
            "erf,erd->efd", expert_hidden, expert_grads_in, preferred_element_type=jnp.float32
        )
        egate_grads = (hidden_gradient_rows * up_activation * silu_grad(gate_activation)).astype(
            jnp.bfloat16
        )
        expert_up_grad_sums = (hidden_gradient_rows * jax.nn.silu(gate_activation)).astype(
            jnp.bfloat16
        )
        expert_gate_gradient = jnp.einsum(
            "jlw,jls->jws", arrived_rows, egate_grads, preferred_element_type=jnp.float32
        )
        expert_up_gradient = jnp.einsum(
            "jlw,jls->jws", arrived_rows, expert_up_grad_sums, preferred_element_type=jnp.float32
        )
        slot_back = (
            jnp.einsum(
                "nmh,nzh->nmz", egate_grads, expert_gate_matrix, preferred_element_type=jnp.float32
            )
            + jnp.einsum(
                "nmh,nzh->nmz",
                expert_up_grad_sums,
                expert_up_matrix,
                preferred_element_type=jnp.float32,
            )
        ).astype(jnp.bfloat16)
        returned_grads = lax.all_to_all(
            slot_back, "expert", split_axis=1, concat_axis=0, tiled=True
        ).reshape(slot_total, model_width)
        mixed_grads = jnp.einsum(
            "tks,sd->td", slot_hot, returned_grads, preferred_element_type=jnp.float32
        )
        weighted_sum = jnp.sum(gate_probs * gate_grads, axis=-1, keepdims=True)
        picked_grads = gate_probs * (gate_grads - weighted_sum)
        logit_grads = jnp.sum(route_hot * picked_grads[..., None], axis=1)
        grad_router = jnp.dot(mixed.astype(jnp.float32).T, logit_grads, precision=highest)
        mixed_grads = mixed_grads + jnp.dot(
            logit_grads, router_w.astype(jnp.float32).T, precision=highest
        )
        shared_hidden_grads = jnp.dot(cot_low, sdown_w.T, preferred_element_type=jnp.float32)
        grad_sdown = jnp.dot(shared_hidden.T, cot_low, preferred_element_type=jnp.float32)
        sgate_grads = (shared_hidden_grads * shared_lift * silu_grad(shared_in)).astype(
            jnp.bfloat16
        )
        sup_grads = (shared_hidden_grads * jax.nn.silu(shared_in)).astype(jnp.bfloat16)
        grad_sgate = jnp.dot(mixed.T, sgate_grads, preferred_element_type=jnp.float32)
        grad_sup = jnp.dot(mixed.T, sup_grads, preferred_element_type=jnp.float32)
        mixed_grads = (
            mixed_grads
            + jnp.dot(sgate_grads, sgate_w.T, preferred_element_type=jnp.float32)
            + jnp.dot(sup_grads, sup_w.T, preferred_element_type=jnp.float32)
        )
        ffn_inner = mixed_grads * gain_ffn
        grad_gffn = jnp.sum(mixed_grads * ffn_norm, axis=0)
        attended_grads = cot_wide + ffn_scale * (
            ffn_inner - ffn_norm * jnp.mean(ffn_inner * ffn_norm, axis=-1, keepdims=True)
        )
        attn_out_grads = attended_grads.astype(jnp.bfloat16)
        grad_wout = jnp.dot(context.T, attn_out_grads, preferred_element_type=jnp.float32)
        context_grads = (
            jnp.dot(attn_out_grads, output_w.T, preferred_element_type=jnp.float32)
            .astype(jnp.bfloat16)
            .reshape(tok_rows, head_count, HEAD_DIM)
        )
        key_all, value_all = (
            lax.all_gather(key_rows, "dp", axis=0, tiled=True),
            lax.all_gather(value_rows, "dp", axis=0, tiled=True),
        )
        key_heads = key_all.reshape(seq_rows, head_count, HEAD_DIM)
        value_heads = value_all.reshape(seq_rows, head_count, HEAD_DIM)
        allowed = visible(query_pos, key_all_pos, prefix_len)[None]
        scores = (
            jnp.einsum("qhd,khd->hqk", queries, key_heads, preferred_element_type=jnp.float32)
            * inv_root
        )
        probs = jnp.where(allowed, jnp.exp(scores - log_total[..., None]), 0.0)
        prob_grads = jnp.einsum(
            "qhd,khd->hqk", context_grads, value_heads, preferred_element_type=jnp.float32
        )
        row_delta = jnp.sum(probs * prob_grads, axis=-1, keepdims=True)
        score_grads = (probs * (prob_grads - row_delta)).astype(jnp.bfloat16)
        query_rot_grads = (
            jnp.einsum("hqk,khd->qhd", score_grads, key_heads, preferred_element_type=jnp.float32)
            * inv_root
        )
        probs_low = probs.astype(jnp.bfloat16)
        key_part = (
            jnp.einsum("hqk,qhd->khd", score_grads, queries, preferred_element_type=jnp.float32)
            * inv_root
        )
        value_part = jnp.einsum(
            "hqk,qhd->khd", probs_low, context_grads, preferred_element_type=jnp.float32
        )
        key_value_grads = lax.psum_scatter(
            jnp.concatenate(
                [
                    key_part.reshape(tok_rows * lax.axis_size("dp"), model_width),
                    value_part.reshape(tok_rows * lax.axis_size("dp"), model_width),
                ],
                axis=1,
            ).astype(jnp.bfloat16),
            "dp",
            scatter_dimension=0,
            tiled=True,
        ).astype(jnp.float32)
        key_rot_sum = key_value_grads[:, :model_width].reshape(tok_rows, head_count, HEAD_DIM)
        value_sum = key_value_grads[:, model_width:]
        key_grads = (
            unrotate(key_rot_sum, cosine, sine_tab)
            .astype(jnp.bfloat16)
            .reshape(tok_rows, model_width)
        )
        value_grads = value_sum.astype(jnp.bfloat16)
        query_grads = (
            unrotate(query_rot_grads, cosine, sine_tab)
            .astype(jnp.bfloat16)
            .reshape(tok_rows, model_width)
        )
        grad_wq = jnp.dot(normed.T, query_grads, preferred_element_type=jnp.float32)
        grad_wk = jnp.dot(normed.T, key_grads, preferred_element_type=jnp.float32)
        grad_wv = jnp.dot(normed.T, value_grads, preferred_element_type=jnp.float32)
        normed_grads = (
            jnp.dot(query_grads, query_w.T, preferred_element_type=jnp.float32)
            + jnp.dot(key_grads, key_w.T, preferred_element_type=jnp.float32)
            + jnp.dot(value_grads, value_w.T, preferred_element_type=jnp.float32)
        )
        grad_gattn = jnp.sum(normed_grads * attn_norm, axis=0)
        attn_inner = normed_grads * gain_attn
        input_grads = (
            attended_grads
            + attn_scale
            * (attn_inner - attn_norm * jnp.mean(attn_inner * attn_norm, axis=-1, keepdims=True))
        ).astype(jnp.bfloat16)
        dense_terms = (
            grad_gattn,
            grad_wq,
            grad_wk,
            grad_wv,
            grad_wout,
            grad_gffn,
            grad_router,
            grad_sgate,
            grad_sup,
            grad_sdown,
        )
        expert_branch_terms = (expert_gate_gradient, expert_up_gradient, expert_down_gradient)
        totals = jax.tree.map(jnp.add, totals, (dense_terms, expert_branch_terms))
        return (totals, (block_rows, input_grads))

    square_shape = (model_width, model_width)
    dense_shapes = (
        (model_width,),
        square_shape,
        square_shape,
        square_shape,
        square_shape,
        (model_width,),
        (model_width, expert_total),
        (model_width, SHARED_FF),
        (model_width, SHARED_FF),
        (SHARED_FF, model_width),
    )
    expert_shapes = (
        (local_experts, model_width, EXPERT_FF),
        (local_experts, model_width, EXPERT_FF),
        (local_experts, EXPERT_FF, model_width),
    )
    initial = (
        tuple((jnp.zeros(shape_one, jnp.float32) for shape_one in dense_shapes)),
        tuple((jnp.zeros(shape_one, jnp.float32) for shape_one in expert_shapes)),
    )
    totals, (block_rows, input_grads) = lax.scan(
        one_batch, initial, (hidden, routes, prefix, cotangent)
    )
    dense_sum, expert_total_grads = totals
    dense_shares = (
        lax.psum_scatter(dense_sum[0], ("dp", "expert"), scatter_dimension=0, tiled=True),
        lax.psum_scatter(dense_sum[1], ("dp", "expert"), scatter_dimension=0, tiled=True),
        lax.psum_scatter(dense_sum[2], ("dp", "expert"), scatter_dimension=0, tiled=True),
        lax.psum_scatter(dense_sum[3], ("dp", "expert"), scatter_dimension=0, tiled=True),
        lax.psum_scatter(dense_sum[4], ("dp", "expert"), scatter_dimension=0, tiled=True),
        lax.psum_scatter(dense_sum[5], ("dp", "expert"), scatter_dimension=0, tiled=True),
        lax.psum_scatter(dense_sum[6], ("dp", "expert"), scatter_dimension=0, tiled=True),
        lax.psum_scatter(dense_sum[7], ("dp", "expert"), scatter_dimension=0, tiled=True),
        lax.psum_scatter(dense_sum[8], ("dp", "expert"), scatter_dimension=0, tiled=True),
        lax.psum_scatter(dense_sum[9], ("dp", "expert"), scatter_dimension=0, tiled=True),
    )
    expert_shares = (
        lax.psum_scatter(
            expert_total_grads[0].astype(jnp.bfloat16), "dp", scatter_dimension=1, tiled=True
        ).astype(jnp.float32),
        lax.psum_scatter(
            expert_total_grads[1].astype(jnp.bfloat16), "dp", scatter_dimension=1, tiled=True
        ).astype(jnp.float32),
        lax.psum_scatter(
            expert_total_grads[2].astype(jnp.bfloat16), "dp", scatter_dimension=1, tiled=True
        ).astype(jnp.float32),
    )
    dense_sum = tuple(dense_shares)
    expert_total_grads = tuple(expert_shares)
    return (
        block_rows[:, None],
        input_grads[:, None],
        dense_sum[0],
        dense_sum[1],
        dense_sum[2],
        dense_sum[3],
        dense_sum[4],
        dense_sum[5],
        dense_sum[6],
        dense_sum[7],
        dense_sum[8],
        dense_sum[9],
        expert_total_grads[0],
        expert_total_grads[1],
        expert_total_grads[2],
    )


def solution(mesh):
    return jax.shard_map(
        shards,
        mesh=mesh,
        in_specs=(
            P(None, "expert", "dp", None),
            P(None, "expert", "dp", None),
            P(None, "expert"),
            P(None, "expert", "dp", None),
            P(("dp", "expert")),
            P(("dp", "expert"), None),
            P(("dp", "expert"), None),
            P(("dp", "expert"), None),
            P(("dp", "expert"), None),
            P(("dp", "expert")),
            P(("dp", "expert"), None),
            P(("dp", "expert"), None),
            P(("dp", "expert"), None),
            P(("dp", "expert"), None),
            P("expert", "dp", None),
            P("expert", "dp", None),
            P("expert", "dp", None),
        ),
        out_specs=(
            P(None, "expert", "dp", None),
            P(None, "expert", "dp", None),
            P(("dp", "expert")),
            P(("dp", "expert"), None),
            P(("dp", "expert"), None),
            P(("dp", "expert"), None),
            P(("dp", "expert"), None),
            P(("dp", "expert")),
            P(("dp", "expert"), None),
            P(("dp", "expert"), None),
            P(("dp", "expert"), None),
            P(("dp", "expert"), None),
            P("expert", "dp", None),
            P("expert", "dp", None),
            P("expert", "dp", None),
        ),
        check_vma=False,
    )
```

profile of v0, /device:TPU:0, one launch (start us, length us, event | category | flops | bytes accessed | tf_op | source)
XLA Modules:
  0.0 2635.3 jit_solution(18292688072209404209)
XLA Ops:
  8.2 1611.6 %while.44 = (s32[]{:T(128)}, f32[768]{0:T(1024)}, f32[768,768]{1,0:T(8,128)}, f32[768,768]{1,0:T(8,128)}, f32[768,768]{1,0:T(8,128)}, /*index=5*/f32[768,768]{1,...) while((s32[]{:T(128)}, f32[768]{0:T(1024)}, ...), condition=%wide.region_24.25_spmd.clone.clone.clone.clone, body=%wide.region_0.24_spmd.clone.clone.clone.clone.sunk | while | flops 16397719552 | bytes 770416000 | solution.py:457
  72.0 53.7 %all-gather.21.cloned.1.call-done = bf16[768,768]{1,0:T(8,128)(2,1)} async-done(((bf16[24,768]{1,0:T(8,128)(2,1)}), bf16[768,768]{1,0:T(8,128)(2,1)}) %all-gather.21.cloned.1.call-update) | async-done | bytes 1179664 | tf_op jit(solution)/shard_map/while/body/eval_jaxpr/all_gather | solution.py:108
  127.2 54.7 %all-gather.23.cloned.1.call-done = bf16[768,768]{1,0:T(8,128)(2,1)} async-done(((bf16[24,768]{1,0:T(8,128)(2,1)}), bf16[768,768]{1,0:T(8,128)(2,1)}) %all-gather.23.cloned.1.call-update) | async-done | bytes 1179664 | tf_op jit(solution)/shard_map/while/body/eval_jaxpr/all_gather | solution.py:109
  287.7 42.6 %all-gather.19.cloned.1.call-done = bf16[768,768]{1,0:T(8,128)(2,1)} async-done(((bf16[24,768]{1,0:T(8,128)(2,1)}), bf16[768,768]{1,0:T(8,128)(2,1)}) %all-gather.19.cloned.1.call-update) | async-done | bytes 1179664 | tf_op jit(solution)/shard_map/while/body/eval_jaxpr/all_gather | solution.py:111
  396.7 56.9 %all-gather.37.cloned.1.call-done = bf16[1,768,2048]{2,1,0:T(8,128)(2,1)} async-done(((bf16[1,96,2048]{2,1,0:T(8,128)(2,1)}), bf16[1,768,2048]{2,1,0:T(8,128)(2,1)}) %all-gather.37.cloned.1.call-update) | async-done | bytes 3145744 | tf_op jit(solution)/shard_map/while/body/eval_jaxpr/all_gather | solution.py:119
  458.2 57.0 %all-gather.41.cloned.1.call-done = bf16[1,768,2048]{2,1,0:T(8,128)(2,1)} async-done(((bf16[1,96,2048]{2,1,0:T(8,128)(2,1)}), bf16[1,768,2048]{2,1,0:T(8,128)(2,1)}) %all-gather.41.cloned.1.call-update) | async-done | bytes 3145744 | tf_op jit(solution)/shard_map/while/body/eval_jaxpr/all_gather | solution.py:120
  579.8 57.1 %all-gather.31.cloned.1.call-done = bf16[768,2048]{1,0:T(8,128)(2,1)} async-done(((bf16[24,2048]{1,0:T(8,128)(2,1)}), bf16[768,2048]{1,0:T(8,128)(2,1)}) %all-gather.31.cloned.1.call-update) | async-done | bytes 3145744 | tf_op jit(solution)/shard_map/while/body/eval_jaxpr/all_gather | solution.py:114
  640.4 57.5 %all-gather.35.cloned.1.call-done = bf16[768,2048]{1,0:T(8,128)(2,1)} async-done(((bf16[24,2048]{1,0:T(8,128)(2,1)}), bf16[768,2048]{1,0:T(8,128)(2,1)}) %all-gather.35.cloned.1.call-update) | async-done | bytes 3145744 | tf_op jit(solution)/shard_map/while/body/eval_jaxpr/all_gather | solution.py:115
  874.4 53.4 %all-gather.21.cloned.1.call-done = bf16[768,768]{1,0:T(8,128)(2,1)} async-done(((bf16[24,768]{1,0:T(8,128)(2,1)}), bf16[768,768]{1,0:T(8,128)(2,1)}) %all-gather.21.cloned.1.call-update) | async-done | bytes 1179664 | tf_op jit(solution)/shard_map/while/body/eval_jaxpr/all_gather | solution.py:108
  929.4 54.6 %all-gather.23.cloned.1.call-done = bf16[768,768]{1,0:T(8,128)(2,1)} async-done(((bf16[24,768]{1,0:T(8,128)(2,1)}), bf16[768,768]{1,0:T(8,128)(2,1)}) %all-gather.23.cloned.1.call-update) | async-done | bytes 1179664 | tf_op jit(solution)/shard_map/while/body/eval_jaxpr/all_gather | solution.py:109
  1089.7 42.8 %all-gather.19.cloned.1.call-done = bf16[768,768]{1,0:T(8,128)(2,1)} async-done(((bf16[24,768]{1,0:T(8,128)(2,1)}), bf16[768,768]{1,0:T(8,128)(2,1)}) %all-gather.19.cloned.1.call-update) | async-done | bytes 1179664 | tf_op jit(solution)/shard_map/while/body/eval_jaxpr/all_gather | solution.py:111
  1198.8 56.9 %all-gather.37.cloned.1.call-done = bf16[1,768,2048]{2,1,0:T(8,128)(2,1)} async-done(((bf16[1,96,2048]{2,1,0:T(8,128)(2,1)}), bf16[1,768,2048]{2,1,0:T(8,128)(2,1)}) %all-gather.37.cloned.1.call-update) | async-done | bytes 3145744 | tf_op jit(solution)/shard_map/while/body/eval_jaxpr/all_gather | solution.py:119
  1260.3 57.0 %all-gather.41.cloned.1.call-done = bf16[1,768,2048]{2,1,0:T(8,128)(2,1)} async-done(((bf16[1,96,2048]{2,1,0:T(8,128)(2,1)}), bf16[1,768,2048]{2,1,0:T(8,128)(2,1)}) %all-gather.41.cloned.1.call-update) | async-done | bytes 3145744 | tf_op jit(solution)/shard_map/while/body/eval_jaxpr/all_gather | solution.py:120
  1382.1 56.9 %all-gather.31.cloned.1.call-done = bf16[768,2048]{1,0:T(8,128)(2,1)} async-done(((bf16[24,2048]{1,0:T(8,128)(2,1)}), bf16[768,2048]{1,0:T(8,128)(2,1)}) %all-gather.31.cloned.1.call-update) | async-done | bytes 3145744 | tf_op jit(solution)/shard_map/while/body/eval_jaxpr/all_gather | solution.py:114
  1442.5 57.6 %all-gather.35.cloned.1.call-done = bf16[768,2048]{1,0:T(8,128)(2,1)} async-done(((bf16[24,2048]{1,0:T(8,128)(2,1)}), bf16[768,2048]{1,0:T(8,128)(2,1)}) %all-gather.35.cloned.1.call-update) | async-done | bytes 3145744 | tf_op jit(solution)/shard_map/while/body/eval_jaxpr/all_gather | solution.py:115
  1700.2 74.6 %reduce-scatter.33.cloned.1.call-done = bf16[1,96,2048]{2,1,0:T(8,128)(2,1)} async-done(((bf16[1,768,2048]{2,1,0:T(8,128)(2,1)}), bf16[1,96,2048]{2,1,0:T(8,128)(2,1)}) %reduce-scatter.33.cloned.1.call-update) | async-done | bytes 393232 | tf_op jit(solution)/shard_map/reduce_scatter | solution.py:477
  1776.7 74.5 %reduce-scatter.35.cloned.1.call-done = bf16[1,256,768]{2,1,0:T(8,128)(2,1)} async-done(((bf16[1,2048,768]{2,1,0:T(8,128)(2,1)}), bf16[1,256,768]{2,1,0:T(8,128)(2,1)}) %reduce-scatter.35.cloned.1.call-update) | async-done | bytes 393232 | tf_op jit(solution)/shard_map/reduce_scatter | solution.py:480
  1853.2 101.9 %reduce-scatter.17.cloned.1.call-done = f32[24,768]{1,0:T(8,128)} async-done(((f32[768,768]{1,0:T(8,128)}), f32[24,768]{1,0:T(8,128)}) %reduce-scatter.17.cloned.1.call-update) | async-done | bytes 73744 | tf_op jit(solution)/shard_map/reduce_scatter | solution.py:463
  1955.0 104.7 %reduce-scatter.19.cloned.1.call-done = f32[24,768]{1,0:T(8,128)} async-done(((f32[768,768]{1,0:T(8,128)}), f32[24,768]{1,0:T(8,128)}) %reduce-scatter.19.cloned.1.call-update) | async-done | bytes 73744 | tf_op jit(solution)/shard_map/reduce_scatter | solution.py:464
  2059.7 103.8 %reduce-scatter.21.cloned.1.call-done = f32[24,768]{1,0:T(8,128)} async-done(((f32[768,768]{1,0:T(8,128)}), f32[24,768]{1,0:T(8,128)}) %reduce-scatter.21.cloned.1.call-update) | async-done | bytes 73744 | tf_op jit(solution)/shard_map/reduce_scatter | solution.py:465
  2163.5 104.6 %reduce-scatter.23.cloned.1.call-done = f32[24,768]{1,0:T(8,128)} async-done(((f32[768,768]{1,0:T(8,128)}), f32[24,768]{1,0:T(8,128)}) %reduce-scatter.23.cloned.1.call-update) | async-done | bytes 73744 | tf_op jit(solution)/shard_map/reduce_scatter | solution.py:466
  2268.2 119.4 %reduce-scatter.25.cloned.1.call-done = f32[24,2048]{1,0:T(8,128)} async-done(((f32[768,2048]{1,0:T(8,128)}), f32[24,2048]{1,0:T(8,128)}) %reduce-scatter.25.cloned.1.call-update) | async-done | bytes 196624 | tf_op jit(solution)/shard_map/reduce_scatter | solution.py:469
  2387.5 120.6 %reduce-scatter.27.cloned.1.call-done = f32[24,2048]{1,0:T(8,128)} async-done(((f32[768,2048]{1,0:T(8,128)}), f32[24,2048]{1,0:T(8,128)}) %reduce-scatter.27.cloned.1.call-update) | async-done | bytes 196624 | tf_op jit(solution)/shard_map/reduce_scatter | solution.py:470
  2508.1 119.8 %reduce-scatter.29.cloned.1.call-done = f32[64,768]{1,0:T(8,128)} async-done(((f32[2048,768]{1,0:T(8,128)}), f32[64,768]{1,0:T(8,128)}) %reduce-scatter.29.cloned.1.call-update) | async-done | bytes 196624 | tf_op jit(solution)/shard_map/reduce_scatter | solution.py:471
  (722 shorter events, 952.5 us)
Async XLA Ops:
  10.7 224.4 %all-gather.29.cloned.1.call-start = ((), (), s32[]{:S(2)}) async-start(), calls=%async_computation.30 | async-start | bytes 1769472 | tf_op jit(solution)/shard_map/while/body/eval_jaxpr/all_gather | solution.py:163
  186.2 205.9 %all-gather.39.cloned.1.call-start = ((), (), s32[]{:S(2)}) async-start(), calls=%async_computation.35 | async-start | bytes 3538944 | tf_op jit(solution)/shard_map/while/body/eval_jaxpr/all_gather | solution.py:256
  186.9 266.7 %all-gather.37.cloned.1.call-start = ((), (), s32[]{:S(2)}) async-start(), calls=%async_computation.34 | async-start | bytes 3538944 | tf_op jit(solution)/shard_map/while/body/eval_jaxpr/all_gather | solution.py:119
  187.7 327.5 %all-gather.41.cloned.1.call-start = ((), (), s32[]{:S(2)}) async-start(), calls=%async_computation.36 | async-start | bytes 3538944 | tf_op jit(solution)/shard_map/while/body/eval_jaxpr/all_gather | solution.py:120
  188.4 387.5 %all-gather.33.cloned.1.call-start = ((), (), s32[]{:S(2)}) async-start(), calls=%async_computation.32 | async-start | bytes 3244032 | tf_op jit(solution)/shard_map/while/body/eval_jaxpr/all_gather | solution.py:251
  189.0 447.9 %all-gather.31.cloned.1.call-start = ((), (), s32[]{:S(2)}) async-start(), calls=%async_computation.31 | async-start | bytes 3244032 | tf_op jit(solution)/shard_map/while/body/eval_jaxpr/all_gather | solution.py:114
  189.7 508.1 %all-gather.35.cloned.1.call-start = ((), (), s32[]{:S(2)}) async-start(), calls=%async_computation.33 | async-start | bytes 3244032 | tf_op jit(solution)/shard_map/while/body/eval_jaxpr/all_gather | solution.py:115
  552.6 249.5 %reduce-scatter.37.cloned.1.call-start = ((), (), s32[]{:S(2)}) async-start(), calls=%async_computation.37 | async-start | bytes 3538944 | tf_op jit(solution)/shard_map/while
  816.3 221.1 %all-gather.29.cloned.1.call-start = ((), (), s32[]{:S(2)}) async-start(), calls=%async_computation.30 | async-start | bytes 1769472 | tf_op jit(solution)/shard_map/while/body/eval_jaxpr/all_gather | solution.py:163
  988.4 205.8 %all-gather.39.cloned.1.call-start = ((), (), s32[]{:S(2)}) async-start(), calls=%async_computation.35 | async-start | bytes 3538944 | tf_op jit(solution)/shard_map/while/body/eval_jaxpr/all_gather | solution.py:256
  989.0 266.7 %all-gather.37.cloned.1.call-start = ((), (), s32[]{:S(2)}) async-start(), calls=%async_computation.34 | async-start | bytes 3538944 | tf_op jit(solution)/shard_map/while/body/eval_jaxpr/all_gather | solution.py:119
  989.7 327.5 %all-gather.41.cloned.1.call-start = ((), (), s32[]{:S(2)}) async-start(), calls=%async_computation.36 | async-start | bytes 3538944 | tf_op jit(solution)/shard_map/while/body/eval_jaxpr/all_gather | solution.py:120
  990.5 387.6 %all-gather.33.cloned.1.call-start = ((), (), s32[]{:S(2)}) async-start(), calls=%async_computation.32 | async-start | bytes 3244032 | tf_op jit(solution)/shard_map/while/body/eval_jaxpr/all_gather | solution.py:251
  991.2 447.8 %all-gather.31.cloned.1.call-start = ((), (), s32[]{:S(2)}) async-start(), calls=%async_computation.31 | async-start | bytes 3244032 | tf_op jit(solution)/shard_map/while/body/eval_jaxpr/all_gather | solution.py:114
  991.8 508.3 %all-gather.35.cloned.1.call-start = ((), (), s32[]{:S(2)}) async-start(), calls=%async_computation.33 | async-start | bytes 3244032 | tf_op jit(solution)/shard_map/while/body/eval_jaxpr/all_gather | solution.py:115
  1354.5 250.0 %reduce-scatter.37.cloned.1.call-start = ((), (), s32[]{:S(2)}) async-start(), calls=%async_computation.37 | async-start | bytes 3538944 | tf_op jit(solution)/shard_map/while
  1629.8 221.4 %reduce-scatter.35.cloned.1.call-start = ((), (), s32[]{:S(2)}) async-start(), calls=%async_computation.24 | async-start | bytes 3538944 | tf_op jit(solution)/shard_map/reduce_scatter | solution.py:480
  1635.0 320.0 %reduce-scatter.17.cloned.1.call-start = ((), (), s32[]{:S(2)}) async-start(), calls=%async_computation.15 | async-start | bytes 2433024 | tf_op jit(solution)/shard_map/reduce_scatter | solution.py:463
  1635.7 424.0 %reduce-scatter.19.cloned.1.call-start = ((), (), s32[]{:S(2)}) async-start(), calls=%async_computation.16 | async-start | bytes 2433024 | tf_op jit(solution)/shard_map/reduce_scatter | solution.py:464
  1636.5 527.0 %reduce-scatter.21.cloned.1.call-start = ((), (), s32[]{:S(2)}) async-start(), calls=%async_computation.17 | async-start | bytes 2433024 | tf_op jit(solution)/shard_map/reduce_scatter | solution.py:465
  1637.2 630.9 %reduce-scatter.23.cloned.1.call-start = ((), (), s32[]{:S(2)}) async-start(), calls=%async_computation.18 | async-start | bytes 2433024 | tf_op jit(solution)/shard_map/reduce_scatter | solution.py:466
  1637.8 749.7 %reduce-scatter.25.cloned.1.call-start = ((), (), s32[]{:S(2)}) async-start(), calls=%async_computation.19 | async-start | bytes 6488064 | tf_op jit(solution)/shard_map/reduce_scatter | solution.py:469
  1638.4 869.7 %reduce-scatter.27.cloned.1.call-start = ((), (), s32[]{:S(2)}) async-start(), calls=%async_computation.20 | async-start | bytes 6488064 | tf_op jit(solution)/shard_map/reduce_scatter | solution.py:470
  1639.0 988.9 %reduce-scatter.29.cloned.1.call-start = ((), (), s32[]{:S(2)}) async-start(), calls=%async_computation.21 | async-start | bytes 6488064 | tf_op jit(solution)/shard_map/reduce_scatter | solution.py:471
  (182 other events, 5636.5 us)
Sparse Core Ops, SparseCore 0:
  12.6 56.7 all-gather.26
  72.7 52.9 all-gather.20
  129.0 52.9 all-gather.22
  230.7 44.1 all-gather.24
  278.0 52.2 all-gather.18
  332.7 59.4 all-gather.38
  394.5 59.0 all-gather.36
  456.1 59.0 all-gather.40
  518.3 57.5 all-gather.32
  579.2 57.7 all-gather.30
  640.1 57.7 all-gather.34
  728.9 73.1 reduce-scatter.36
  818.4 53.2 all-gather.26
  874.9 52.8 all-gather.20
  931.0 52.9 all-gather.22
  1032.7 44.1 all-gather.24
  1080.2 52.2 all-gather.18
  1134.8 59.3 all-gather.38
  1196.6 59.0 all-gather.36
  1258.1 59.0 all-gather.40
  1320.5 57.5 all-gather.32
  1381.2 57.7 all-gather.30
  1442.3 57.7 all-gather.34
  1531.1 73.3 reduce-scatter.36
  (2 shorter events, 86.2 us)
Sparse Core Ops, SparseCore 1:
  1624.9 73.3 reduce-scatter.30
  1701.7 73.0 reduce-scatter.32
  1778.2 73.0 reduce-scatter.34
  1857.1 97.9 reduce-scatter.16
  1961.8 97.9 reduce-scatter.18
  2065.6 97.9 reduce-scatter.20
  2170.1 98.0 reduce-scatter.22
  2274.2 113.3 reduce-scatter.24
  2394.6 113.5 reduce-scatter.26
  2514.4 113.5 reduce-scatter.28
where the time goes:
time: 2640 us
  waiting for transfers between devices  2010 us (76%)
  matrix products  216 us (8%)
  blocking collectives  201 us (8%)
  local copies, waits for them, and re-layouts  81.1 us (3%)
  other arithmetic  73.5 us (3%)
  starting transfers between devices  33.4 us (1%)
    reduce_scatter x1, waiting for transfers between devices, shards(): lax.psum_scatter(dense_sum[8], ('dp', 'expert'), scatter_dimension=0, til...  121 us
    reduce_scatter x1, waiting for transfers between devices, shards(): lax.psum_scatter(dense_sum[9], ('dp', 'expert'), scatter_dimension=0, til...  120 us
    reduce_scatter x1, waiting for transfers between devices, shards(): lax.psum_scatter(dense_sum[7], ('dp', 'expert'), scatter_dimension=0, til...  119 us
    all_gather x2, waiting for transfers between devices, one_batch(): lax.all_gather(shared_up, ('dp', 'expert'), axis=0, tiled=True)  115 us
    all_gather x2, waiting for transfers between devices, one_batch(): lax.all_gather(shared_gate, ('dp', 'expert'), axis=0, tiled=True)  114 us
    all_gather x2, waiting for transfers between devices, one_batch(): lax.all_gather(expert_up, 'dp', axis=1, tiled=True)  114 us
    all_gather x2, waiting for transfers between devices, one_batch(): lax.all_gather(expert_gate, 'dp', axis=1, tiled=True)  114 us
    all_gather x2, waiting for transfers between devices, one_batch(): lax.all_gather(w_key, ('dp', 'expert'), axis=0, tiled=True)  109 us
  transfers between devices with their start and end apart: 44, of which 38 were waited for; matrix products, arithmetic and copies ran while one was open for 10% of the time, Pallas kernels for 0%

commit v1 on v0

v1 whole, which is shorter than its diff:
```python
import math

import jax
import jax.numpy as jnp
from jax import lax
from jax.sharding import Mesh
from jax.sharding import PartitionSpec as P

HEAD_DIM = 64
TOP_K = 2
MISC = 128

eps = 1e-06
highest = lax.Precision.HIGHEST
neg_fill = -1e30
f32 = jnp.float32
bf16 = jnp.bfloat16

ALL = ("z", "y", "x", "c")
PLANE = ("y", "x", "c")
DP = ("z", "y")
EXPERT = ("x", "c")


def rms_scale(values):
    return lax.rsqrt(jnp.mean(values * values, axis=-1, keepdims=True) + eps)


def silu_grad(values):
    sig = jax.nn.sigmoid(values)
    return sig * (1.0 + values * (1.0 - sig))


def dot(a, b, dims, batch=((), ())):
    return lax.dot_general(a, b, (dims, batch), preferred_element_type=f32)


def rotary_tables(positions):
    half = HEAD_DIM // 2
    frequency = jnp.exp(jnp.arange(half, dtype=f32) * (-math.log(10000.0) * 2.0 / HEAD_DIM))
    angles = frequency[:, None] * positions.astype(f32)[None, :]
    return jnp.cos(angles), jnp.sin(angles)


def rotate_t(values, cosine, sine, sign):
    rows = values.shape[-1]
    halves = values.reshape(-1, 2, HEAD_DIM // 2, rows)
    first, second = halves[:, 0], halves[:, 1]
    turned = jnp.stack([first * cosine - sign * second * sine, second * cosine + sign * first * sine], axis=1)
    return turned.reshape(values.shape)


def gather_all(shard):
    return lax.all_gather(shard, ALL, axis=0, tiled=True)


def gather_weights(egu, sgu, ed, sd):
    nz, ny, ne = lax.axis_size("z"), lax.axis_size("y"), lax.axis_size(EXPERT)

    def spread(blocks):
        mine = lax.all_to_all(blocks, "z", 0, 0, tiled=True)
        return lax.all_gather(mine, PLANE, axis=0).reshape(ny, ne, nz, *blocks.shape[1:])

    egu_all = jnp.transpose(spread(egu), (1, 2, 0, 3, 4)).reshape(ne, -1, egu.shape[-1])
    sgu_all = jnp.transpose(spread(sgu), (2, 0, 1, 3, 4)).reshape(-1, sgu.shape[-1])
    ed_all = lax.all_gather(ed, PLANE, axis=0).reshape(ny, ne, *ed.shape)
    ed_all = jnp.transpose(ed_all, (1, 0, 2, 3)).reshape(ne, -1, ed.shape[-1])
    sd_all = lax.all_gather(sd, PLANE, axis=0, tiled=True)
    return egu_all, sgu_all, ed_all, sd_all


def gather_line(rows):
    return lax.all_gather(rows, "z", axis=0, tiled=True)


def sum_line(rows):
    return lax.psum_scatter(rows, "z", scatter_dimension=0, tiled=True)


def sum_weights(egu, sgu, ed, sd):
    nz, ny, ne = lax.axis_size("z"), lax.axis_size("y"), lax.axis_size(EXPERT)

    def collect(parts):
        mine = lax.psum_scatter(parts, PLANE, scatter_dimension=0, tiled=True)
        return lax.all_to_all(mine.reshape(nz, *mine.shape[1:]), "z", 0, 0, tiled=True)

    wide = egu.shape[-1]
    egu = jnp.transpose(egu.reshape(ne, nz, ny, -1, wide), (2, 0, 1, 3, 4))
    sgu = jnp.transpose(sgu.reshape(nz, ny, ne, -1, wide), (1, 2, 0, 3, 4))
    egu = collect(egu.reshape(ny * ne * nz, -1, wide))
    sgu = collect(sgu.reshape(ny * ne * nz, -1, wide))
    ed = jnp.transpose(ed.reshape(ne, ny, -1, ed.shape[-1]), (1, 0, 2, 3)).reshape(ny * ne, -1, ed.shape[-1])
    ed = lax.psum_scatter(ed, PLANE, scatter_dimension=0, tiled=True)[0]
    sd = lax.psum_scatter(sd, PLANE, scatter_dimension=0, tiled=True)
    return egu, sgu, ed, sd


def sum_all(parts):
    return lax.psum_scatter(parts, ALL, scatter_dimension=0, tiled=True)


def units_here(batches, heads):
    return -(-batches * heads // lax.axis_size(DP))


def to_units(tensor):
    kinds, batches, width, rows = tensor.shape
    n_dp = lax.axis_size(DP)
    heads = width // HEAD_DIM
    here = units_here(batches, heads)
    units = tensor.reshape(kinds, batches * heads, HEAD_DIM, rows)
    units = jnp.pad(units, ((0, 0), (0, here * n_dp - batches * heads), (0, 0), (0, 0)))
    units = jnp.transpose(units.reshape(kinds, n_dp, here, HEAD_DIM, rows), (1, 2, 0, 3, 4))
    units = lax.all_to_all(units, DP, 0, 0, tiled=True)
    return jnp.transpose(units, (1, 2, 3, 0, 4)).reshape(here, kinds, HEAD_DIM, n_dp * rows)


def from_units(units, batches, heads):
    here, kinds, _, length = units.shape
    n_dp = lax.axis_size(DP)
    rows = length // n_dp
    parts = jnp.transpose(units.reshape(here, kinds, HEAD_DIM, n_dp, rows), (3, 0, 1, 2, 4))
    parts = lax.all_to_all(parts, DP, 0, 0, tiled=True)
    parts = parts.reshape(n_dp * here, kinds, HEAD_DIM, rows)[: batches * heads]
    return jnp.transpose(parts, (1, 0, 2, 3)).reshape(kinds, batches, heads * HEAD_DIM, rows)


def visible_units(prefix, heads, here, length):
    unit = lax.axis_index(DP) * here + jnp.arange(here)
    lengths = prefix[jnp.minimum(unit // heads, prefix.shape[0] - 1), 0]
    pos = jnp.arange(length, dtype=jnp.int32)
    low = pos[None, :] < lengths[:, None]
    return (pos[None, None, :] <= pos[None, :, None]) | (low[:, :, None] & low[:, None, :])


def attention_forward(qkv, batches, heads, prefix):
    units = to_units(qkv)
    q, k, v = units[:, 0], units[:, 1], units[:, 2]
    allowed = visible_units(prefix, heads, q.shape[0], q.shape[-1])
    scores = dot(q, k, ((1,), (1,)), ((0,), (0,))) * (1.0 / math.sqrt(HEAD_DIM))
    scores = jnp.where(allowed, scores, neg_fill)
    top = jnp.max(scores, axis=-1, keepdims=True)
    weights = jnp.exp(scores - top)
    total = jnp.sum(weights, axis=-1, keepdims=True)
    lse = top + jnp.log(total)
    probs = (weights / total).astype(bf16)
    context = dot(v, probs, ((2,), (2,)), ((0,), (0,))).astype(bf16)
    return from_units(context[:, None], batches, heads)[0], (q, k, v, lse)


def attention_backward(context_grad, saved, batches, heads, prefix):
    q, k, v, lse = saved
    grad = to_units(context_grad[None])[:, 0]
    allowed = visible_units(prefix, heads, q.shape[0], q.shape[-1])
    inv = 1.0 / math.sqrt(HEAD_DIM)
    scores = dot(q, k, ((1,), (1,)), ((0,), (0,))) * inv
    probs = jnp.where(allowed, jnp.exp(scores - lse), 0.0)
    prob_grad = dot(grad, v, ((1,), (1,)), ((0,), (0,)))
    delta = jnp.sum(probs * prob_grad, axis=-1, keepdims=True)
    score_grad = (probs * (prob_grad - delta)).astype(bf16)
    dq = dot(k, score_grad, ((2,), (2,)), ((0,), (0,))) * inv
    dk = dot(q, score_grad, ((2,), (1,)), ((0,), (0,))) * inv
    dv = dot(grad, probs.astype(bf16), ((2,), (1,)), ((0,), (0,)))
    return from_units(jnp.stack([dq, dk, dv], axis=1).astype(bf16), batches, heads)


def shards(
    hidden,
    routes,
    prefix,
    cotangent,
    attn_gain,
    w_query,
    w_key,
    w_value,
    w_output,
    ffn_gain,
    router,
    shared_gate,
    shared_up,
    shared_down,
    expert_gate,
    expert_up,
    expert_down,
):
    nz = lax.axis_size("z")
    batches, _, rows, width = hidden.shape
    count = batches * rows
    heads = width // HEAD_DIM
    experts = router.shape[1]
    own = router.shape[0]
    capacity = (5 * rows * TOP_K + 4 * experts - 1) // (4 * experts)
    slice_ff = shared_gate.shape[1] // nz

    misc = jnp.concatenate(
        [router, attn_gain[:, None], ffn_gain[:, None], jnp.zeros((own, MISC - experts - 2), bf16)], axis=1
    )
    attn_shard = jnp.concatenate([w_query, w_key, w_value, w_output, misc], axis=1)

    def slices(gate, up):
        both = jnp.stack([gate.reshape(-1, nz, slice_ff), up.reshape(-1, nz, slice_ff)], axis=2)
        return jnp.transpose(both.reshape(-1, nz, 2 * slice_ff), (1, 0, 2))

    cot = cotangent.reshape(count, width)
    pair_ids = routes.reshape(count, TOP_K)
    cot_routes = jnp.concatenate(
        [cot, pair_ids.astype(bf16), jnp.zeros((count, MISC - TOP_K), bf16)], axis=1
    )
    attn_full = gather_all(attn_shard)
    egu, sgu, ed, sd = gather_weights(
        slices(expert_gate[0], expert_up[0]), slices(shared_gate, shared_up), expert_down[0], shared_down
    )
    cot_line = gather_line(cot_routes)

    w_qkv = attn_full[:, : 3 * width]
    w_out = attn_full[:, 3 * width : 4 * width]
    misc_full = attn_full[:, 4 * width :]
    router_w = misc_full[:, :experts]
    gain_attn = misc_full[:, experts].astype(f32)
    gain_ffn = misc_full[:, experts + 1].astype(f32)

    x_in = hidden.reshape(count, width).astype(f32)
    attn_scale = rms_scale(x_in)
    attn_norm = x_in * attn_scale
    normed = (attn_norm * gain_attn).astype(bf16)
    positions = lax.axis_index(DP) * rows + jnp.arange(rows, dtype=jnp.int32)
    cosine, sine = rotary_tables(jnp.tile(positions, batches))
    projected = dot(w_qkv, normed, ((0,), (1,)))
    turned = rotate_t(projected[: 2 * width], cosine, sine, 1.0)
    qkv = jnp.concatenate([turned, projected[2 * width :]], axis=0).astype(bf16)
    qkv = jnp.transpose(qkv.reshape(3, width, batches, rows), (0, 2, 1, 3))
    context, saved = attention_forward(qkv, batches, heads, prefix)
    context = jnp.transpose(context, (1, 0, 2)).reshape(width, count)
    attended = x_in + dot(context, w_out, ((0,), (0,)))
    ffn_scale = rms_scale(attended)
    ffn_norm = attended * ffn_scale
    mixed = (ffn_norm * gain_ffn).astype(bf16)

    mixed_line = gather_line(mixed)
    cot_rows = cot_line[:, :width]
    ids = cot_line[:, width : width + TOP_K].astype(jnp.int32)
    lines = mixed_line.shape[0]
    groups = lines // rows

    def gates(mixed_rows, pair_ids):
        hot = (pair_ids[..., None] == jnp.arange(experts, dtype=jnp.int32)).astype(f32)
        logits = dot(mixed_rows, router_w, ((1,), (0,)))
        return hot, jax.nn.softmax(jnp.sum(hot * logits[:, None, :], axis=-1), axis=-1)

    hot, probs = gates(mixed_line, ids)
    hot_int = hot.astype(jnp.int32).reshape(groups, rows * TOP_K, experts)
    earlier = jnp.cumsum(hot_int, axis=1) - hot_int
    rank = jnp.sum(earlier * hot_int, axis=-1).reshape(groups, rows, TOP_K)
    group_ids = ids.reshape(groups, rows, TOP_K)
    slot = jnp.where(rank < capacity, group_ids * capacity + rank, experts * capacity)
    slot_hot = (slot[..., None] == jnp.arange(experts * capacity, dtype=jnp.int32)).astype(bf16)
    token_hot = jnp.sum(slot_hot, axis=2)
    slot_probs = jnp.sum(slot_hot.astype(f32) * probs.reshape(groups, rows, TOP_K, 1), axis=(1, 2))

    def dispatch(values):
        per_group = dot(token_hot, values.reshape(groups, rows, width), ((1,), (1,)), ((0,), (0,)))
        per_group = per_group.reshape(groups, experts, capacity, width)
        return jnp.transpose(per_group, (1, 0, 2, 3)).reshape(experts, groups * capacity, width)

    def per_slot(values):
        return jnp.transpose(values.reshape(groups, experts, capacity), (1, 0, 2)).reshape(experts, -1, 1)

    def combine(slots):
        per_group = jnp.transpose(slots.reshape(experts, groups, capacity, width), (1, 0, 2, 3))
        per_group = per_group.reshape(groups, experts * capacity, width)
        return dot(token_hot, per_group, ((2,), (1,)), ((0,), (0,))).reshape(lines, width)

    slot_p = per_slot(slot_probs)
    arrived = dispatch(mixed_line).astype(bf16)
    cot_slots = dispatch(cot_rows)
    pair_grad = (cot_slots * slot_p).astype(bf16)
    batch = ((0,), (0,))
    act = dot(arrived, egu, ((2,), (1,)), batch)
    gate_act, up_act = act[..., :slice_ff], act[..., slice_ff:]
    sig = jax.nn.sigmoid(gate_act)
    silu_act = gate_act * sig
    expert_hidden = (silu_act * up_act).astype(bf16)
    expert_out = dot(expert_hidden, ed, ((2,), (1,)), batch)
    hidden_grad = dot(pair_grad, ed, ((2,), (2,)), batch)
    gate_up_grad = jnp.concatenate(
        [hidden_grad * up_act * sig * (1.0 + gate_act * (1.0 - sig)), hidden_grad * silu_act], axis=-1
    ).astype(bf16)
    grad_egu = dot(arrived, gate_up_grad, ((1,), (1,)), batch).astype(bf16)
    grad_ed = dot(expert_hidden, pair_grad, ((1,), (1,)), batch).astype(bf16)
    slot_grad = dot(gate_up_grad, egu, ((2,), (2,)), batch).astype(bf16)
    gate_dot = jnp.sum(cot_slots * expert_out, axis=-1)
    gate_dot = jnp.transpose(gate_dot.reshape(experts, groups, capacity), (1, 0, 2)).reshape(groups, 1, 1, -1)
    pair_dot = jnp.sum(slot_hot.astype(f32) * gate_dot, axis=-1).reshape(lines, TOP_K)
    expert_sum = combine((expert_out * slot_p).astype(bf16))

    s_act = dot(mixed_line, sgu, ((1,), (0,)))
    s_in, s_lift = s_act[:, :slice_ff], s_act[:, slice_ff:]
    s_sig = jax.nn.sigmoid(s_in)
    s_silu = s_in * s_sig
    s_hidden = (s_silu * s_lift).astype(bf16)
    s_hidden_grad = dot(cot_rows, sd, ((1,), (1,)))
    s_grad = jnp.concatenate(
        [s_hidden_grad * s_lift * s_sig * (1.0 + s_in * (1.0 - s_sig)), s_hidden_grad * s_silu], axis=-1
    ).astype(bf16)
    grad_sgu = dot(mixed_line, s_grad, ((0,), (0,))).astype(bf16)
    grad_sd = dot(s_hidden, cot_rows, ((0,), (0,))).astype(bf16)
    out_part = (dot(s_hidden, sd, ((1,), (0,))) + expert_sum).astype(bf16)
    mixed_part = combine(slot_grad) + dot(s_grad, sgu, ((1,), (1,)))
    mixed_part = jnp.concatenate(
        [mixed_part.astype(bf16), pair_dot.astype(bf16), jnp.zeros((lines, MISC - TOP_K), bf16)], axis=1
    )
    mixed_sum = sum_line(mixed_part).astype(f32)
    out_sum = sum_line(out_part).astype(f32)
    block_rows = (attended + out_sum).astype(bf16)

    hot, probs = gates(mixed, pair_ids)
    gate_grads = mixed_sum[:, width : width + TOP_K]
    picked = probs * (gate_grads - jnp.sum(probs * gate_grads, axis=-1, keepdims=True))
    logit_grad = jnp.sum(hot * picked[..., None], axis=1)
    grad_router = jnp.dot(mixed.astype(f32).T, logit_grad, precision=highest)
    mixed_grad = mixed_sum[:, :width] + jnp.dot(logit_grad, router_w.astype(f32).T, precision=highest)
    cot_wide = cot.astype(f32)
    inner = mixed_grad * gain_ffn
    grad_gffn = jnp.sum(mixed_grad * ffn_norm, axis=0)
    attended_grad = cot_wide + ffn_scale * (inner - ffn_norm * jnp.mean(inner * ffn_norm, axis=-1, keepdims=True))
    out_grad = attended_grad.astype(bf16)
    grad_wout = dot(context, out_grad, ((1,), (0,)))
    context_grad = dot(w_out, out_grad, ((1,), (1,))).astype(bf16)
    context_grad = jnp.transpose(context_grad.reshape(width, batches, rows), (1, 0, 2))

    rot_grad = attention_backward(context_grad, saved, batches, heads, prefix)
    rot_grad = jnp.transpose(rot_grad, (0, 2, 1, 3)).reshape(3 * width, count).astype(f32)
    turned = rotate_t(rot_grad[: 2 * width], cosine, sine, -1.0)
    qkv_grad = jnp.concatenate([turned, rot_grad[2 * width :]], axis=0).astype(bf16)
    grad_wqkv = dot(normed, qkv_grad, ((0,), (1,)))
    normed_grad = dot(qkv_grad, w_qkv, ((0,), (1,)))
    grad_gattn = jnp.sum(normed_grad * attn_norm, axis=0)
    inner = normed_grad * gain_attn
    input_grad = (
        attended_grad + attn_scale * (inner - attn_norm * jnp.mean(inner * attn_norm, axis=-1, keepdims=True))
    ).astype(bf16)

    grad_misc = jnp.concatenate(
        [grad_router, grad_gattn[:, None], grad_gffn[:, None], jnp.zeros((width, MISC - experts - 2), f32)], axis=1
    )
    attn_parts = jnp.concatenate([grad_wqkv, grad_wout, grad_misc], axis=1).astype(bf16)
    attn_sums = sum_all(attn_parts).astype(f32)
    egu_sum, sgu_sum, ed_sum, sd_sum = sum_weights(grad_egu, grad_sgu, grad_ed, grad_sd)

    def joined(blocks):
        both = jnp.transpose(blocks.reshape(nz, -1, 2, slice_ff), (2, 1, 0, 3)).astype(f32)
        return both.reshape(2, -1, nz * slice_ff)

    egu_sum, sgu_sum = joined(egu_sum), joined(sgu_sum)
    return (
        block_rows.reshape(batches, 1, rows, width),
        input_grad.reshape(batches, 1, rows, width),
        attn_sums[:, 4 * width + experts],
        attn_sums[:, :width],
        attn_sums[:, width : 2 * width],
        attn_sums[:, 2 * width : 3 * width],
        attn_sums[:, 3 * width : 4 * width],
        attn_sums[:, 4 * width + experts + 1],
        attn_sums[:, 4 * width : 4 * width + experts],
        sgu_sum[0],
        sgu_sum[1],
        sd_sum.astype(f32),
        egu_sum[0][None],
        egu_sum[1][None],
        ed_sum.astype(f32)[None],
    )


def solution(mesh):
    n_dp, n_expert = mesh.shape["dp"], mesh.shape["expert"]
    nz = 4 if n_dp % 4 == 0 else 1
    grid = Mesh(mesh.devices.reshape(nz, n_dp // nz, n_expert // 2, 2), ALL)
    rows = P(None, EXPERT, DP, None)
    line = P(ALL)
    dense = P(ALL, None)
    expert = P(EXPERT, DP, None)
    return jax.shard_map(
        shards,
        mesh=grid,
        in_specs=(rows, rows, P(None, EXPERT), rows, line)
        + (dense,) * 4
        + (line,)
        + (dense,) * 4
        + (expert,) * 3,
        out_specs=(rows, rows, line) + (dense,) * 4 + (line,) + (dense,) * 4 + (expert,) * 3,
        check_vma=False,
    )
```

time: 2640 us -> 776 us (0.29)
  waiting for transfers between devices: 2010 us -> 384 us
  blocking collectives: 201 us -> 82.1 us
  matrix products: 216 us -> 120 us
    all_gather x24 -> x6, waiting for transfers between devices: 962 us -> 96.7 us  [the longest x2 43.5 us: spread(): lax.all_gather(mine, PLANE, axis=0).reshape(ny, ne, nz, *blocks.shape[1:])]
    reduce_scatter x10 -> x6, waiting for transfers between devices: 940 us -> 108 us  [the longest x1 44.9 us: sum_weights(): ed = lax.psum_scatter(ed, PLANE, scatter_dimension=0, tiled=True)[0]]
    dot_general x88 -> x32, matrix products: 216 us -> 120 us  [the longest x30 117 us: dot(): return lax.dot_general(a, b, (dims, batch), preferred_element_type=f32)]
    unnamed x10 -> x14, waiting for transfers between devices: 4.37 us -> 99.5 us
    while x28 -> x0, waiting for transfers between devices: 85.1 us -> none
    while x2 -> x0, blocking collectives: 81.8 us -> none
    all_to_all x0 -> x4, blocking collectives: none -> 70.3 us  [the longest x2 44.1 us: spread(): mine = lax.all_to_all(blocks, 'z', 0, 0, tiled=True)]
    all_gather x2 -> x1, blocking collectives: 79.1 us -> 11.8 us  [gather_weights(): sd_all = lax.all_gather(sd, PLANE, axis=0, tiled=True)]
  transfers between devices with their start and end apart: 44 -> 17, of which waited for: 38 -> 12; matrix products, arithmetic and copies ran while one was open for 10% -> 24% of each run, Pallas kernels for 0% -> 0%
where the time goes in v1:
time: 776 us; the launch traced here: 767 us
  waiting for transfers between devices  384 us (49%)
  matrix products  120 us (15%)
  local copies, waits for them, and re-layouts  96.6 us (12%)
  blocking collectives  82.1 us (11%)
  other arithmetic  51.7 us (7%)
  starting transfers between devices  17.5 us (2%)
  between operations  15.5 us (2%)
    dot_general x30, matrix products, dot(): return lax.dot_general(a, b, (dims, batch), preferred_element_type=f32)  117 us
    unnamed x14, waiting for transfers between devices  99.5 us
    all_to_all x2, waiting for transfers between devices, to_units(): units = lax.all_to_all(units, DP, 0, 0, tiled=True)  55.6 us
    reduce_scatter x1, waiting for transfers between devices, sum_weights(): ed = lax.psum_scatter(ed, PLANE, scatter_dimension=0, tiled=True)[0]  44.9 us
    all_to_all x2, blocking collectives, spread(): mine = lax.all_to_all(blocks, 'z', 0, 0, tiled=True)  44.1 us
    all_gather x2, waiting for transfers between devices, spread(): lax.all_gather(mine, PLANE, axis=0).reshape(ny, ne, nz, *blocks.shape[1:])  43.5 us
    reduce_scatter x2, waiting for transfers between devices, sum_line(): return lax.psum_scatter(rows, 'z', scatter_dimension=0, tiled=True)  36.7 us
    all_gather x2, waiting for transfers between devices, gather_line(): return lax.all_gather(rows, 'z', axis=0, tiled=True)  33.2 us
  transfers between devices with their start and end apart: 17, of which 12 were waited for; matrix products, arithmetic and copies ran while one was open for 24% of the time, Pallas kernels for 0%

profile of v1, /device:TPU:0, one launch (start us, length us, event | category | flops | bytes accessed | tf_op | source)
XLA Modules:
  0.0 767.4 jit_solution(3532242303437003346)
XLA Ops:
  16.3 15.8 %all_to_all.40 = bf16[4,24,1024]{2,1,0:T(8,128)(2,1)} all-to-all(bf16[4,24,1024]{2,1,0:T(8,128)(2,1)S(1)} %bitcast.286), channel_id=1, replica_groups=mesh['z'=4,'y'=2,'x'=2,'c'=2] {'z'}, dimensions={0} | all-to-all | bytes 393216 | tf_op jit(solution)/shard_map/all_to_all | solution.py:61
  36.7 28.4 %all_to_all.41 = bf16[4,96,1024]{2,1,0:T(8,128)(2,1)} all-to-all(bf16[4,96,1024]{2,1,0:T(8,128)(2,1)S(1)} %bitcast.267), channel_id=1, replica_groups=mesh['z'=4,'y'=2,'x'=2,'c'=2] {'z'}, dimensions={0} | all-to-all | bytes 1572864 | tf_op jit(solution)/shard_map/all_to_all | solution.py:61
  66.4 19.6 %all-gather.9.cloned.1.call-done = bf16[768,3200]{1,0:T(8,128)(2,1)} async-done(((bf16[24,3200]{1,0:T(8,128)(2,1)}), bf16[768,3200]{1,0:T(8,128)(2,1)}) %all-gather.9.cloned.1.call-update) | async-done | bytes 4915216 | tf_op jit(solution)/shard_map/all_gather | solution.py:54
  98.6 52.0 %all-to-all-done = bf16[8,3,3,64,128]{4,3,1,2,0:T(8,128)(2,1)S(1)} async-done(((bf16[8,3,3,64,128]{4,3,1,2,0:T(8,128)(2,1)}), bf16[8,3,3,64,128]{4,3,1,2,0:T(8,128)(2,1)S(1)}, u32[]{:S(2)}, u32[]{:S(2)}) %all-to-all-start) | async-done | bytes 1179680 | tf_op jit(solution)/shard_map/all_to_all | solution.py:114
  163.6 15.8 %all_to_all.42 = bf16[8,3,1,64,128]{4,3,1,2,0:T(8,128)(2,1)S(1)} all-to-all(bf16[8,3,1,64,128]{4,3,1,2,0:T(8,128)(2,1)S(1)} %bitcast.277), channel_id=1, replica_groups=mesh['z'=4,'y'=2,'x'=2,'c'=2] {'z','y'}, dimensions={0} | all-to-all | bytes 786432 | tf_op jit(solution)/shard_map/all_to_all | solution.py:123
  183.6 11.8 %all_gather.31 = bf16[512,768]{1,0:T(8,128)(2,1)S(1)} all-gather(bf16[64,768]{1,0:T(8,128)(2,1)S(1)} %copy-done.41), channel_id=1, replica_groups=mesh['z'=4,'y'=2,'x'=2,'c'=2] {'y','x','c'}, dimensions={0}, use_global_device_ids=true | all-gather | bytes 884736 | tf_op jit(solution)/shard_map/all_gather | solution.py:68
  218.2 43.5 %all-gather.19.cloned.1.call-done = bf16[32,96,1024]{2,1,0:T(8,128)(2,1)} async-done(((bf16[4,96,1024]{2,1,0:T(8,128)(2,1)}), bf16[32,96,1024]{2,1,0:T(8,128)(2,1)}) %all-gather.19.cloned.1.call-update) | async-done | bytes 6291472 | tf_op jit(solution)/shard_map/all_gather | solution.py:62
  261.8 6.5 copy.387
  268.3 33.2 %all-gather.11.cloned.1.call-done = bf16[1024,768]{0,1:T(8,128)(2,1)} async-done(((bf16[256,768]{0,1:T(8,128)(2,1)}), bf16[1024,768]{0,1:T(8,128)(2,1)}) %all-gather.11.cloned.1.call-update) | async-done | bytes 1572880 | tf_op jit(solution)/shard_map/all_gather | solution.py:73
  306.7 7.8 %fusion.64 = f32[4,640,1024]{2,1,0:T(8,128)S(1)} fusion(bf16[4,640,768]{2,1,0:T(8,128)(2,1)} %bitcast.258, bf16[4,768,1024]{2,1,0:T(8,128)(2,1)} %bitcast.246), kind=kOutput, calls=%fused_computation.172 | convolution fusion | flops 4026531840 | bytes 20709376 | tf_op jit(solution)/shard_map/dot_general | solution.py:35
  327.5 8.2 %fusion.2 = (bf16[4,640,768]{2,1,0:T(8,128)(2,1)S(1)}, bf16[4,640,768]{2,1,0:T(8,128)(2,1)}) fusion(f32[8,4,80,768]{3,2,0,1:T(8,128)} %copy.395, f32[4,640]{1,0:T(4,128)S(1)} %mul.375, f32[4,640,768]{2,1,0:T(8,128)} %get-tuple-element.161), kind=kLoop, calls=%fused_computation.11 | loop fusion | flops 7864320 | bytes 23603200 | tf_op jit(solution)/shard_map/convert_element_type | solution.py:276
  335.7 9.5 %multiply_convert_fusion.3 = (bf16[4,640,512]{2,1,0:T(8,128)(2,1)}, bf16[4,640,512]{2,1,0:T(8,128)(2,1)}) fusion(f32[4,640,1024]{2,1,0:T(8,128)} %copy-done.13, bf16[4,640,768]{2,1,0:T(8,128)(2,1)S(1)} %get-tuple-element.151, bf16[4,512,768]{2,1,0:T(8,128)(2,1)S(1)} %bitcast.241), kind=kOutput, calls=%fused_computation.20 | convolution fusion | flops 2030305280 | bytes 22806528 | tf_op jit(solution)/shard_map/dot_general | solution.py:35
  345.2 10.5 %fusion.17 = bf16[4,640,768]{2,1,0:T(8,128)(2,1)} fusion(bf16[4,768,1024]{2,1,0:T(8,128)(2,1)} %bitcast.247, bf16[4,640,512]{2,1,0:T(8,128)(2,1)} %get-tuple-element.133, bf16[4,640,512]{2,1,0:T(8,128)(2,1)} %get-tuple-element.132), kind=kOutput, calls=%fused_computation.40 | convolution fusion | flops 4038983680 | bytes 15466496 | tf_op jit(solution)/shard_map/dot_general | solution.py:35
  391.9 7.6 convolution_convert_fusion.1
  415.4 33.3 %reduce-scatter.10.cloned.1.call-done = bf16[256,768]{0,1:T(8,128)(2,1)} async-done(((bf16[1024,768]{0,1:T(8,128)(2,1)}), bf16[256,768]{0,1:T(8,128)(2,1)}) %reduce-scatter.10.cloned.1.call-update) | async-done | bytes 393232 | tf_op jit(solution)/shard_map/reduce_scatter | solution.py:77
  458.0 5.8 convolution_convert_fusion.3
  469.7 11.1 %multiply_reduce_fusion = (f32[3,1024]{1,0:T(4,128)S(1)}, f32[3,1024,1024]{1,2,0:T(8,128)}) fusion(f32[3,1024]{1,0:T(4,128)S(1)} %log_add_fusion, f32[3,1024,1024]{1,2,0:T(8,128)} %copy-done.2, pred[3,1024]{1,0:T(4,128)(4,1)S(1)} %iota_compare_fusion.5, pred[1024,1024]{0,1:T(8,128)(4,1)S(1)} %copy-done.16, bf16[3,64,1024]{2,1,0:T(8,128)(2,1)S(1)} %squeeze_reshape.3, ...), kind=kOutput, calls=%fused_computation.2 | convolution fusion | flops 424670208 | bytes 27037696 | tf_op jit(solution)/shard_map/dot_general | solution.py:35
  480.9 10.7 %multiply_convert_fusion = bf16[3,1024,1024]{1,2,0:T(8,128)(2,1)S(1)} fusion(f32[3,1024,1024]{1,2,0:T(8,128)} %get-tuple-element.164, f32[3,1024]{1,0:T(4,128)S(1)} %get-tuple-element.163, f32[3,1024]{1,0:T(4,128)S(1)} %log_add_fusion, f32[3,1024,1024]{1,2,0:T(8,128)} %copy-done.2, pred[3,1024]{1,0:T(4,128)(4,1)S(1)} %iota_compare_fusion.5, ...), kind=kLoop, calls=%fused_computation.1 | loop fusion | flops 25165824 | bytes 32533504 | tf_op jit(solution)/shard_map/convert_element_type | solution.py:160
  509.0 24.1 %all-to-all-done.5 = bf16[8,3,3,64,128]{4,3,2,1,0:T(8,128)(2,1)} async-done(((bf16[8,3,3,64,128]{4,3,2,1,0:T(8,128)(2,1)}), bf16[8,3,3,64,128]{4,3,2,1,0:T(8,128)(2,1)}, u32[]{:S(2)}, u32[]{:S(2)}) %all-to-all-start.5) | async-done | bytes 1179680 | tf_op jit(solution)/shard_map/all_to_all | solution.py:123
  548.2 7.8 %concatenate.43 = bf16[768,3200]{1,0:T(8,128)(2,1)} concatenate(bf16[768,2304]{1,0:T(8,128)(2,1)S(1)} %convolution_convert_fusion, bf16[768,768]{1,0:T(8,128)(2,1)} %convolution_convert_fusion.5, bf16[768,4]{1,0:T(8,128)(2,1)} %copy.418, bf16[768,1]{1,0:T(8,128)(2,1)} %broadcast_in_dim.40, bf16[768,1]{1,0:T(8,128)(2,1)} %broadcast_in_dim.41, bf16[768,122]{1,0:T(8,128)(2,1)} %broadcast_in_dim.39), dimensions={1} | concatenate | bytes 9830400 | tf_op jit(solution)/shard_map/concatenate | solution.py:346
  556.1 10.3 %all_to_all.43 = bf16[4,24,1024]{2,1,0:T(8,128)(2,1)S(1)} all-to-all(bf16[4,24,1024]{2,1,0:T(8,128)(2,1)} %reduce-scatter.14.cloned.1.call-done), channel_id=1, replica_groups=mesh['z'=4,'y'=2,'x'=2,'c'=2] {'z'}, dimensions={0} | all-to-all | bytes 393216 | tf_op jit(solution)/shard_map/all_to_all | solution.py:85
  570.2 26.4 %reduce-scatter.16.cloned.1.call-done = bf16[64,768]{1,0:T(8,128)(2,1)} async-done(((bf16[512,768]{1,0:T(8,128)(2,1)}), bf16[64,768]{1,0:T(8,128)(2,1)}) %reduce-scatter.16.cloned.1.call-update) | async-done | bytes 98320 | tf_op jit(solution)/shard_map/reduce_scatter | solution.py:94
  601.6 44.9 %reduce-scatter.20.cloned.1.call-done = bf16[1,256,768]{2,1,0:T(8,128)(2,1)} async-done(((bf16[8,256,768]{2,1,0:T(8,128)(2,1)}), bf16[1,256,768]{2,1,0:T(8,128)(2,1)}) %reduce-scatter.20.cloned.1.call-update) | async-done | bytes 393232 | tf_op jit(solution)/shard_map/reduce_scatter | solution.py:93
  657.4 98.7 %reduce-scatter.22.cloned.1.call-done = bf16[24,3200]{1,0:T(8,128)(2,1)} async-done(((bf16[768,3200]{1,0:T(8,128)(2,1)}), bf16[24,3200]{1,0:T(8,128)(2,1)}) %reduce-scatter.22.cloned.1.call-update) | async-done | bytes 153616
  (325 shorter events, 208.5 us)
Async XLA Ops:
  7.2 90.4 %copy-start = (s32[2,1]{0,1:T(1,128)S(1)}, s32[2,1]{0,1:T(1,128)}, u32[]{:S(2)}) copy-start(s32[2,1]{0,1:T(1,128)} %param.19) | copy-start | bytes 28
  7.2 78.8 %all-gather.9.cloned.1.call-start = ((), (), s32[]{:S(2)}) async-start(), calls=%async_computation.15 | async-start | bytes 5068800 | tf_op jit(solution)/shard_map/all_gather | solution.py:54
  11.2 184.2 %all-gather.13.cloned.1.call-start = ((), (), s32[]{:S(2)}) async-start(), calls=%async_computation.17 | async-start | bytes 2293760 | tf_op jit(solution)/shard_map/all_gather | solution.py:73
  14.4 197.0 %all-gather.17.cloned.1.call-start = ((), (), s32[]{:S(2)}) async-start(), calls=%async_computation.25 | async-start | bytes 1769472 | tf_op jit(solution)/shard_map/all_gather | solution.py:62
  32.1 182.4 %all-gather.15.cloned.1.call-start = ((), (), s32[]{:S(2)}) async-start(), calls=%async_computation.18 | async-start | bytes 3538944 | tf_op jit(solution)/shard_map/all_gather | solution.py:66
  32.6 229.1 %all-gather.19.cloned.1.call-start = ((), (), s32[]{:S(2)}) async-start(), calls=%async_computation.26 | async-start | bytes 7077888 | tf_op jit(solution)/shard_map/all_gather | solution.py:62
  65.3 114.4 %copy-start.3 = (f32[256,768]{0,1:T(8,128)}, f32[256,768]{0,1:T(8,128)S(1)}, u32[]{:S(2)}) copy-start(f32[256,768]{0,1:T(8,128)S(1)} %copy.445) | copy-start | bytes 2359300
  93.0 57.6 %all-to-all-start = ((bf16[8,3,3,64,128]{4,3,1,2,0:T(8,128)(2,1)}), bf16[8,3,3,64,128]{4,3,1,2,0:T(8,128)(2,1)S(1)}, u32[]{:S(2)}, u32[]{:S(2)}) async-start(bf16[8,3,3,64,128]{4,3,1,2,0:T(8,128)(2,1)} %copy.365), calls=%async_computation | async-start | bytes 2359296 | tf_op jit(solution)/shard_map/all_to_all | solution.py:114
  97.3 204.2 %all-gather.11.cloned.1.call-start = ((), (), s32[]{:S(2)}) async-start(), calls=%async_computation.16 | async-start | bytes 1966080 | tf_op jit(solution)/shard_map/all_gather | solution.py:73
  98.5 60.3 %copy-start.15 = (pred[1024,1024]{0,1:T(8,128)(4,1)}, pred[1024,1024]{0,1:T(8,128)(4,1)S(1)}, u32[]{:S(2)}) copy-start(pred[1024,1024]{0,1:T(8,128)(4,1)S(1)} %iota_compare_fusion) | copy-start | bytes 3145732
  183.5 228.4 %reduce-scatter.12.cloned.1.call-start = ((), (), s32[]{:S(2)}) async-start(), calls=%async_computation.20 | async-start | bytes 2293760 | tf_op jit(solution)/shard_map/reduce_scatter | solution.py:77
  195.4 172.4 %copy-start.26 = (bf16[512,768]{1,0:T(8,128)(2,1)}, bf16[512,768]{1,0:T(8,128)(2,1)S(1)}, u32[]{:S(2)}) copy-start(bf16[512,768]{1,0:T(8,128)(2,1)S(1)} %all_gather.31) | copy-start | bytes 2359300
  374.1 74.6 %reduce-scatter.10.cloned.1.call-start = ((), (), s32[]{:S(2)}) async-start(), calls=%async_computation.19 | async-start | bytes 1966080 | tf_op jit(solution)/shard_map/reduce_scatter | solution.py:77
  385.7 170.4 %reduce-scatter.14.cloned.1.call-start = ((), (), s32[]{:S(2)}) async-start(), calls=%async_computation.21 | async-start | bytes 1769472 | tf_op jit(solution)/shard_map/reduce_scatter | solution.py:84
  390.9 175.5 %reduce-scatter.18.cloned.1.call-start = ((), (), s32[]{:S(2)}) async-start(), calls=%async_computation.23 | async-start | bytes 7077888 | tf_op jit(solution)/shard_map/reduce_scatter | solution.py:84
  403.0 193.6 %reduce-scatter.16.cloned.1.call-start = ((), (), s32[]{:S(2)}) async-start(), calls=%async_computation.22 | async-start | bytes 884736 | tf_op jit(solution)/shard_map/reduce_scatter | solution.py:94
  454.0 15.3 %all-to-all-start.4 = ((bf16[8,3,1,64,128]{4,3,1,2,0:T(8,128)(2,1)}), bf16[8,3,1,64,128]{4,3,1,2,0:T(8,128)(2,1)S(1)}, u32[]{:S(2)}, u32[]{:S(2)}) async-start(bf16[8,3,1,64,128]{4,3,1,2,0:T(8,128)(2,1)} %bitcast.61), calls=%async_computation.6 | async-start | bytes 786432 | tf_op jit(solution)/shard_map/all_to_all | solution.py:114
  457.5 189.0 %reduce-scatter.20.cloned.1.call-start = ((), (), s32[]{:S(2)}) async-start(), calls=%async_computation.24 | async-start | bytes 3538944 | tf_op jit(solution)/shard_map/reduce_scatter | solution.py:93
  500.8 32.3 %all-to-all-start.5 = ((bf16[8,3,3,64,128]{4,3,2,1,0:T(8,128)(2,1)}), bf16[8,3,3,64,128]{4,3,2,1,0:T(8,128)(2,1)}, u32[]{:S(2)}, u32[]{:S(2)}) async-start(bf16[8,3,3,64,128]{4,3,2,1,0:T(8,128)(2,1)} %maximum_bitcast_fusion), calls=%async_computation.7 | async-start | bytes 2359296 | tf_op jit(solution)/shard_map/all_to_all | solution.py:123
  505.1 251.1 %reduce-scatter.22.cloned.1.call-start = ((), (), s32[]{:S(2)}) async-start(), calls=%async_computation.27 | async-start | bytes 5068800
  566.4 82.1 %copy-start.6 = (f32[256,768]{0,1:T(8,128)S(1)}, f32[256,768]{0,1:T(8,128)}, u32[]{:S(2)}) copy-start(f32[256,768]{0,1:T(8,128)} %copy-done.3) | copy-start | bytes 2359300
  566.4 82.1 %copy-start.12 = (f32[256,768]{0,1:T(8,128)S(1)}, f32[256,768]{0,1:T(8,128)}, u32[]{:S(2)}) copy-start(f32[256,768]{0,1:T(8,128)} %copy-done.11) | copy-start | bytes 2359300
  566.4 84.4 %all-to-all-start.7 = ((bf16[4,96,1024]{2,1,0:T(8,128)(2,1)}), bf16[4,96,1024]{2,1,0:T(8,128)(2,1)S(1)}, u32[]{:S(2)}, u32[]{:S(2)}) async-start(bf16[4,96,1024]{2,1,0:T(8,128)(2,1)} %reduce-scatter.18.cloned.1.call-done), calls=%async_computation.12 | async-start | bytes 1572864 | tf_op jit(solution)/shard_map/all_to_all | solution.py:85
  653.5 107.1 %copy-start.1 = (s32[2,1]{0,1:T(1,128)S(1)}, s32[2,1]{0,1:T(1,128)}, u32[]{:S(2)}) copy-start(s32[2,1]{0,1:T(1,128)} %param.19) | copy-start | bytes 28
  (47 other events, 546.1 us)
Sparse Core Ops, SparseCore 0:
  11.5 74.4 all-gather.8
  87.6 65.3 all-gather.12
  154.9 26.0 all-gather.16
  182.6 31.7 all-gather.14
  216.2 45.4 all-gather.18
  263.7 37.6 all-gather.10
  374.2 37.6 reduce-scatter.11
  414.2 34.4 reduce-scatter.9
  452.0 37.4 reduce-scatter.13
  492.7 65.4 reduce-scatter.17
  561.7 34.9 reduce-scatter.15
  600.3 46.2 reduce-scatter.19
  652.2 103.8 reduce-scatter.21

commit v2 on v1

--- a/solution.py
+++ b/solution.py
@@ -1,8 +1,11 @@
+import functools
 import math
 
 import jax
 import jax.numpy as jnp
 from jax import lax
+from jax.experimental import pallas as pl
+from jax.experimental.pallas import tpu as pltpu
 from jax.sharding import Mesh
 from jax.sharding import PartitionSpec as P
 
@@ -71,6 +74,14 @@
 
 def gather_line(rows):
     return lax.all_gather(rows, "z", axis=0, tiled=True)
+
+
+def gather_inputs_plain(attn, egu, sgu, ed, sd, cot):
+    return (gather_all(attn), *gather_weights(egu, sgu, ed, sd), gather_line(cot))
+
+
+def paired():
+    return tuple(lax.axis_size(name) for name in PLANE) == (2, 2, 2)
 
 
 def sum_line(rows):
@@ -97,6 +108,10 @@
 
 def sum_all(parts):
     return lax.psum_scatter(parts, ALL, scatter_dimension=0, tiled=True)
+
+
+def sum_everything_plain(attn, egu, sgu, ed, sd, out):
+    return (sum_all(attn), *sum_weights(egu, sgu, ed, sd), sum_line(out))
 
 
 def units_here(batches, heads):
@@ -123,6 +138,666 @@
     parts = lax.all_to_all(parts, DP, 0, 0, tiled=True)
     parts = parts.reshape(n_dp * here, kinds, HEAD_DIM, rows)[: batches * heads]
     return jnp.transpose(parts, (1, 0, 2, 3)).reshape(kinds, batches, heads * HEAD_DIM, rows)
+
+
+MESH = pl.DeviceIdType.MESH
+
+
+def position():
+    return tuple(lax.axis_index(name) for name in ALL)
+
+
+def remote(src, dst, send, recv, device):
+    return pltpu.make_async_remote_copy(
+        src_ref=src, dst_ref=dst, send_sem=send, recv_sem=recv, device_id=device, device_id_type=MESH
+    )
+
+
+def greet(partners):
+    barrier = pltpu.get_barrier_semaphore()
+    for device in partners:
+        pl.semaphore_signal(barrier, inc=1, device_id=device, device_id_type=MESH)
+    pl.semaphore_wait(barrier, len(partners))
+
+
+def any_specs(count):
+    return [pl.BlockSpec(memory_space=pl.ANY)] * count
+
+
+def params(collective_id, vmem=16 << 20):
+    return pltpu.CompilerParams(collective_id=collective_id, has_side_effects=True, vmem_limit_bytes=vmem)
+
+
+class PlaneItem:
+    def __init__(self, here, index, place, own, x_first):
+        self.here, self.index, self.place, self.own, self.x_first = here, index, place, own, x_first
+
+    def moved(self, along_first, along_second, along_core):
+        z, y, x, c = self.here
+        move_x, move_y = (along_first, along_second) if self.x_first else (along_second, along_first)
+        return (z, 1 - y if move_y else y, 1 - x if move_x else x, 1 - c if along_core else c)
+
+    def ref(self, *moves):
+        return self.place(*self.moved(*moves)[1:])
+
+    COPIES = (
+        ((0, 0, 0), (1, 0, 0)),
+        ((0, 0, 0), (0, 1, 0)),
+        ((1, 0, 0), (0, 1, 0)),
+        ((0, 0, 0), (0, 0, 1)),
+        ((1, 0, 0), (0, 0, 1)),
+        ((0, 1, 0), (0, 0, 1)),
+        ((1, 1, 0), (0, 0, 1)),
+    )
+
+    def copy(self, number, send, recv):
+        source, to = self.COPIES[number]
+        src = self.own if source == (0, 0, 0) else self.ref(*source)
+        return remote(
+            src, self.ref(*source), send.at[self.index, number], recv.at[self.index, number], self.moved(*to)
+        )
+
+    def arrival(self, number, send, recv):
+        source, to = self.COPIES[number]
+        ref = self.ref(*[a ^ b for a, b in zip(source, to)])
+        return remote(ref, ref, send.at[self.index, number], recv.at[self.index, number], self.moved(*to))
+
+
+def gather_kernel(nz, *refs):
+    inputs, outputs = refs[:6], refs[6:12]
+    local, zsend, zrecv, psend, precv = refs[12:]
+    attn_in, egu_in, sgu_in, ed_in, sd_in, cot_in = inputs
+    attn, egu, sgu, ed, sd, cot = outputs
+    here = position()
+    z, y, x, c = here
+    line = [lax.rem(z + d, nz) for d in range(nz)]
+    others = [(line[d], y, x, c) for d in range(1, nz)]
+    greet(others + [(z, 1 - y, x, c), (z, y, 1 - x, c), (z, y, x, 1 - c)])
+
+    def flat(zs, py, px, pc):
+        return ((zs * 2 + py) * 2 + px) * 2 + pc
+
+    half = ed_in.shape[0] // 2
+    places = {
+        "attn": lambda zs: lambda py, px, pc: attn.at[flat(zs, py, px, pc)],
+        "egu": lambda zs: lambda py, px, pc: egu.at[px * 2 + pc, zs * 2 + py],
+        "sgu": lambda zs: lambda py, px, pc: sgu.at[flat(zs, py, px, pc)],
+    }
+    firsts = {"attn": lambda zs: attn_in, "egu": lambda zs: egu_in.at[zs], "sgu": lambda zs: sgu_in.at[zs]}
+    kinds = ("attn", "egu", "sgu")
+
+    def line_copy(kind, d):
+        number = kinds.index(kind)
+        to, frm = line[d], line[(nz - d) % nz]
+        mine = places[kind](z)(y, x, c)
+        src = firsts[kind](to)
+        theirs = places[kind](frm)(y, x, c)
+        sends = remote(src, mine, zsend.at[number, d], zrecv.at[number, d], (to, y, x, c))
+        gets = remote(theirs, theirs, zsend.at[number, d], zrecv.at[number, d], (to, y, x, c))
+        return sends, gets
+
+    def cot_copy(d):
+        to, frm = line[d], line[(nz - d) % nz]
+        sends = remote(cot_in, cot.at[z], zsend.at[3, d], zrecv.at[3, d], (to, y, x, c))
+        gets = remote(cot.at[frm], cot.at[frm], zsend.at[3, d], zrecv.at[3, d], (to, y, x, c))
+        return sends, gets
+
+    items, sums = {}, 0
+    for kind in kinds:
+        for d in range(nz):
+            frm = line[(nz - d) % nz]
+            place = places[kind](frm)
+            own = firsts[kind](z) if d == 0 else place(y, x, c)
+            items[kind, d] = PlaneItem(here, sums, place, own, d % 2 == 1)
+            sums += 1
+    for h in range(2):
+        rows = pl.ds(h * half, half)
+        place = lambda py, px, pc, rows=rows: ed.at[px * 2 + pc, py, rows]
+        items["ed", h] = PlaneItem(here, sums, place, ed_in.at[rows], h == 1)
+        sums += 1
+    items["sd", 0] = PlaneItem(here, sums, lambda py, px, pc: sd.at[(py * 2 + px) * 2 + pc], sd_in, False)
+
+    owns = [
+        (attn_in, attn.at[flat(z, y, x, c)]),
+        (egu_in.at[z], egu.at[x * 2 + c, z * 2 + y]),
+        (sgu_in.at[z], sgu.at[flat(z, y, x, c)]),
+        (ed_in, ed.at[x * 2 + c, y]),
+        (sd_in, sd.at[(y * 2 + x) * 2 + c]),
+        (cot_in, cot.at[z]),
+    ]
+    keeps = [pltpu.make_async_copy(src, dst, local.at[i]) for i, (src, dst) in enumerate(owns)]
+
+    def have_own(item):
+        for number in (0, 1, 3):
+            item.copy(number, psend, precv).start()
+
+    def have_first(item):
+        item.arrival(0, psend, precv).wait_recv()
+        item.copy(2, psend, precv).start()
+        item.copy(4, psend, precv).start()
+
+    def have_second(item):
+        item.arrival(1, psend, precv).wait_recv()
+        item.copy(5, psend, precv).start()
+        item.arrival(2, psend, precv).wait_recv()
+        item.copy(6, psend, precv).start()
+
+    for d in range(1, nz):
+        line_copy("attn", d)[0].start()
+    have_own(items["attn", 0])
+    for kind in ("egu", "sgu"):
+        for d in range(1, nz):
+            line_copy(kind, d)[0].start()
+    for d in range(1, nz):
+        cot_copy(d)[0].start()
+    rest = [items["ed", 0], items["ed", 1], items["sd", 0], items["egu", 0], items["sgu", 0]]
+    for item in rest:
+        have_own(item)
+    for copy in keeps:
+        copy.start()
+    for d in range(1, nz):
+        line_copy("attn", d)[1].wait_recv()
+        have_own(items["attn", d])
+    for d in range(nz):
+        have_first(items["attn", d])
+    for item in rest:
+        have_first(item)
+    for d in range(1, nz):
+        for kind in ("egu", "sgu"):
+            line_copy(kind, d)[1].wait_recv()
+            have_own(items[kind, d])
+    for d in range(nz):
+        have_second(items["attn", d])
+    late = [items[kind, d] for d in range(1, nz) for kind in ("egu", "sgu")]
+    for item in late:
+        have_first(item)
+    for item in rest + late:
+        have_second(item)
+    for d in range(1, nz):
+        cot_copy(d)[1].wait_recv()
+    for item in items.values():
+        for number in range(3, 7):
+            item.arrival(number, psend, precv).wait_recv()
+    for item in items.values():
+        for number in range(7):
+            item.copy(number, psend, precv).wait_send()
+    for d in range(1, nz):
+        for kind in kinds:
+            line_copy(kind, d)[0].wait_send()
+        cot_copy(d)[0].wait_send()
+    for copy in keeps:
+        copy.wait()
+
+
+def gather_inputs_fast(attn, egu, sgu, ed, sd, cot):
+    nz = lax.axis_size("z")
+    all_devices, plane = nz * 8, 8
+    items = 3 * nz + 3
+    shapes = [
+        (all_devices, *attn.shape),
+        (4, nz * 2, *egu.shape[1:]),
+        (all_devices, *sgu.shape[1:]),
+        (4, 2, *ed.shape),
+        (plane, *sd.shape),
+        (nz, *cot.shape),
+    ]
+    attn, egu, sgu, ed, sd, cot = pl.pallas_call(
+        functools.partial(gather_kernel, nz),
+        out_shape=[jax.ShapeDtypeStruct(shape, bf16) for shape in shapes],
+        in_specs=any_specs(6),
+        out_specs=any_specs(6),
+        scratch_shapes=[
+            pltpu.SemaphoreType.DMA((6,)),
+            pltpu.SemaphoreType.DMA((4, nz)),
+            pltpu.SemaphoreType.DMA((4, nz)),
+            pltpu.SemaphoreType.DMA((items, 7)),
+            pltpu.SemaphoreType.DMA((items, 7)),
+        ],
+        compiler_params=params(0),
+        name="gather_inputs",
+    )(attn, egu, sgu, ed, sd, cot)
+    return (
+        attn.reshape(-1, attn.shape[-1]),
+        egu.reshape(4, -1, egu.shape[-1]),
+        sgu.reshape(-1, sgu.shape[-1]),
+        ed.reshape(4, -1, ed.shape[-1]),
+        sd.reshape(-1, sd.shape[-1]),
+        cot.reshape(-1, cot.shape[-1]),
+    )
+
+
+def line_gather_steps(z, nz, own, out, sends, gets, neighbour, pieces):
+    rows = out.shape[1] // pieces
+
+    def copy(way, source, piece, src=None):
+        part = pl.ds(piece * rows, rows)
+        dst = out.at[source, part]
+        src = dst if src is None else src.at[part]
+        return remote(src, dst, sends.at[way, source, piece], gets.at[way, source, piece], neighbour(1 - 2 * way))
+
+    def may_send(way):
+        return z < nz - 1 if way == 0 else z > 0
+
+    def start():
+        for piece in range(pieces):
+            for way in range(2):
+                pl.when(may_send(way))(lambda: copy(way, z, piece, own).start())
+
+    def step(distance, piece):
+        for way in range(2):
+            source = z - distance if way == 0 else z + distance
+
+            @pl.when((source >= 0) & (source < nz))
+            def _():
+                copy(way, source, piece).wait_recv()
+                pl.when(may_send(way))(lambda: copy(way, source, piece).start())
+
+    def end():
+        for distance in range(nz):
+            for piece in range(pieces):
+                for way in range(2):
+                    source = z - distance if way == 0 else z + distance
+
+                    @pl.when((source >= 0) & (source < nz) & may_send(way))
+                    def _():
+                        copy(way, source, piece).wait_send()
+
+    steps = [functools.partial(step, distance, piece) for distance in range(1, nz) for piece in range(pieces)]
+    return start, steps, end
+
+
+def line_partners(here, nz):
+    z, y, x, c = here
+    return lambda way: (jnp.clip(z + way, 0, nz - 1), y, x, c)
+
+
+def greet_line(here, nz):
+    z = here[0]
+    neighbour = line_partners(here, nz)
+    barrier = pltpu.get_barrier_semaphore()
+
+    @pl.when(z > 0)
+    def _():
+        pl.semaphore_signal(barrier, inc=1, device_id=neighbour(-1), device_id_type=MESH)
+
+    @pl.when(z < nz - 1)
+    def _():
+        pl.semaphore_signal(barrier, inc=1, device_id=neighbour(1), device_id_type=MESH)
+
+    pl.semaphore_wait(barrier, jnp.where(z > 0, 1, 0) + jnp.where(z < nz - 1, 1, 0))
+
+
+LINE_PIECES = 2
+
+
+def line_gather_kernel(nz, own, out, local, sends, gets):
+    here = position()
+    z = here[0]
+    greet_line(here, nz)
+    start, steps, end = line_gather_steps(z, nz, own, out, sends, gets, line_partners(here, nz), LINE_PIECES)
+    start()
+    keep = pltpu.make_async_copy(own, out.at[z], local)
+    keep.start()
+    for step in steps:
+        step()
+    end()
+    keep.wait()
+
+
+def gather_line_fast(rows):
+    nz = lax.axis_size("z")
+    sems = pltpu.SemaphoreType.DMA((2, nz, LINE_PIECES))
+    out = pl.pallas_call(
+        functools.partial(line_gather_kernel, nz),
+        out_shape=jax.ShapeDtypeStruct((nz, *rows.shape), bf16),
+        in_specs=any_specs(1),
+        out_specs=pl.BlockSpec(memory_space=pl.ANY),
+        scratch_shapes=[pltpu.SemaphoreType.DMA, sems, sems],
+        compiler_params=params(1),
+        name="gather_line",
+    )(rows)
+    return out.reshape(-1, rows.shape[-1])
+
+
+def line_sum_steps(z, nz, parts, total, up, down, sends, gets, neighbour, pieces):
+    rows = parts.shape[1] // pieces
+    arrived = (up, down)
+
+    def copy(way, target, piece, src):
+        part = pl.ds(piece * rows, rows)
+        dst = arrived[way].at[target, part]
+        return remote(src, dst, sends.at[way, target, piece], gets.at[way, target, piece], neighbour(1 - 2 * way))
+
+    def part_of(ref, target, piece):
+        return ref.at[target, pl.ds(piece * rows, rows)]
+
+    def step(distance, piece):
+        for way in range(2):
+            target = nz - distance if way == 0 else distance - 1
+            ahead = z < target if way == 0 else z > target
+            first = z == 0 if way == 0 else z == nz - 1
+            mine, theirs = part_of(parts, target, piece), part_of(arrived[way], target, piece)
+
+            @pl.when(ahead & first)
+            def _():
+                copy(way, target, piece, mine).start()
+
+            @pl.when(ahead & jnp.logical_not(first))
+            def _():
+                copy(way, target, piece, theirs).wait_recv()
+                mine[...] = (mine[...].astype(f32) + theirs[...].astype(f32)).astype(bf16)
+                copy(way, target, piece, mine).start()
+
+    def end():
+        for piece in range(pieces):
+            part = pl.ds(piece * rows, rows)
+            total[part, :] = parts[z, part, :].astype(f32)
+            for way in range(2):
+                theirs = part_of(arrived[way], z, piece)
+
+                @pl.when(z > 0 if way == 0 else z < nz - 1)
+                def _():
+                    copy(way, z, piece, theirs).wait_recv()
+                    total[part, :] += theirs[...].astype(f32)
+
+        for distance in range(1, nz):
+            for piece in range(pieces):
+                for way in range(2):
+                    target = nz - distance if way == 0 else distance - 1
+
+                    @pl.when(z < target if way == 0 else z > target)
+                    def _():
+                        copy(way, target, piece, part_of(parts, target, piece)).wait_send()
+
+    steps = [functools.partial(step, distance, piece) for distance in range(1, nz) for piece in range(pieces)]
+    return steps, end
+
+
+def line_sum_kernel(nz, parts_in, total, parts, up, down, local, sends, gets):
+    here = position()
+    z = here[0]
+    load = pltpu.make_async_copy(parts_in, parts, local)
+    load.start()
+    greet_line(here, nz)
+    steps, end = line_sum_steps(z, nz, parts, total, up, down, sends, gets, line_partners(here, nz), LINE_PIECES)
+    load.wait()
+    for step in steps:
+        step()
+    end()
+
+
+def sum_line_fast(parts):
+    nz = lax.axis_size("z")
+    parts = parts.reshape(nz, -1, parts.shape[-1])
+    sems = pltpu.SemaphoreType.DMA((2, nz, LINE_PIECES))
+    return pl.pallas_call(
+        functools.partial(line_sum_kernel, nz),
+        out_shape=jax.ShapeDtypeStruct(parts.shape[1:], f32),
+        in_specs=any_specs(1),
+        out_specs=pl.BlockSpec(memory_space=pltpu.VMEM),
+        scratch_shapes=[pltpu.VMEM(parts.shape, bf16)] * 3 + [pltpu.SemaphoreType.DMA, sems, sems],
+        compiler_params=params(2, 32 << 20),
+        name="sum_line",
+    )(parts)
+
+
+class SumItem:
+    def __init__(self, here, index, place, buffers, x_first):
+        self.here, self.index, self.place, self.x_first = here, index, place, x_first
+        self.own, self.sib, self.second, self.first = buffers
+
+    moved = PlaneItem.moved
+
+    def slot(self, a, b):
+        return 2 * a + b
+
+    def begin(self, load, send, recv):
+        for a in range(2):
+            for b in range(2):
+                n = self.slot(a, b)
+                self.sib_copy(a, b, send, recv).start()
+                pltpu.make_async_copy(self.place(*self.moved(a, b, 0)[1:]), self.own.at[n], load.at[self.index, n]).start()
+
+    def sib_copy(self, a, b, send, recv):
+        n = self.slot(a, b)
+        src = self.place(*self.moved(a, b, 1)[1:])
+        return remote(src, self.sib.at[n], send.at[self.index, n], recv.at[self.index, n], self.moved(0, 0, 1))
+
+    def second_copy(self, a, send, recv):
+        n = 4 + a
+        src = self.sib.at[self.slot(a, 1)]
+        return remote(src, self.second.at[a], send.at[self.index, n], recv.at[self.index, n], self.moved(0, 1, 0))
+
+    def first_copy(self, send, recv):
+        src = self.second.at[1]
+        return remote(src, self.first, send.at[self.index, 6], recv.at[self.index, 6], self.moved(1, 0, 0))
+
+    def after_core(self, load, send, recv):
+        for b in (1, 0):
+            for a in range(2):
+                n = self.slot(a, b)
+                pltpu.make_async_copy(self.own.at[n], self.own.at[n], load.at[self.index, n]).wait()
+                self.sib_copy(a, b, send, recv).wait_recv()
+                add_to(self.sib.at[n], self.own.at[n])
+                if b == 1:
+                    self.second_copy(a, send, recv).start()
+
+    def after_second(self, send, recv):
+        for a in (1, 0):
+            self.second_copy(a, send, recv).wait_recv()
+            add_to(self.second.at[a], self.sib.at[self.slot(a, 0)])
+            if a == 1:
+                self.first_copy(send, recv).start()
+
+    def after_first(self, send, recv):
+        self.first_copy(send, recv).wait_recv()
+        add_to(self.first, self.second.at[0])
+
+    def end(self, send, recv):
+        for a in range(2):
+            for b in range(2):
+                self.sib_copy(a, b, send, recv).wait_send()
+            self.second_copy(a, send, recv).wait_send()
+        self.first_copy(send, recv).wait_send()
+
+
+def add_to(total, term):
+    rows, columns = total.shape
+    if rows % 16 == 0:
+
+        @pl.loop(0, rows // 16)
+        def _(i):
+            part = pl.ds(pl.multiple_of(i * 16, 16), 16)
+            total[part, :] = (total[part, :].astype(f32) + term[part, :].astype(f32)).astype(bf16)
+    else:
+        wide = max(w for w in (128, 256, 384, 512, 640) if columns % w == 0)
+
+        @pl.loop(0, columns // wide)
+        def _(i):
+            part = pl.ds(pl.multiple_of(i * wide, 128), wide)
+            total[:, part] = (total[:, part].astype(f32) + term[:, part].astype(f32)).astype(bf16)
+
+
+SUM_LAG = 2
+
+
+def sum_kernel(nz, kinds, extra, *refs):
+    refs = list(refs)
+    take = lambda n: [refs.pop(0) for _ in range(n)]
+    inputs = dict(zip(kinds, take(len(kinds))))
+    out_parts_in = take(1)[0] if extra else None
+    outputs = dict(zip(kinds, take(len(kinds))))
+    out_total = take(1)[0] if extra else None
+    buffers = {kind: take(4) for kind in kinds}
+    zbuf = take(1)[0] if "attn" in kinds else None
+    load, send, recv, zsend, zrecv, store = take(6)
+    if extra:
+        out_parts, up, down, line_load, line_send, line_recv = take(6)
+    here = position()
+    z, y, x, c = here
+    line = [lax.rem(z + d, nz) for d in range(nz)]
+    if extra:
+        out_load = pltpu.make_async_copy(out_parts_in, out_parts, line_load)
+        out_load.start()
+    greet([(line[d], y, x, c) for d in range(1, nz)] + [(z, 1 - y, x, c), (z, y, 1 - x, c), (z, y, x, 1 - c)])
+
+    def flat(zs, py, px, pc):
+        return ((zs * 2 + py) * 2 + px) * 2 + pc
+
+    places = {
+        "attn": lambda zs: lambda py, px, pc: inputs["attn"].at[flat(zs, py, px, pc)],
+        "egu": lambda zs: lambda py, px, pc: inputs["egu"].at[px * 2 + pc, zs * 2 + py],
+        "sgu": lambda zs: lambda py, px, pc: inputs["sgu"].at[flat(zs, py, px, pc)],
+        "ed": lambda h: lambda py, px, pc: inputs["ed"].at[px * 2 + pc, py, pl.ds(h * half, half)],
+        "sd": lambda h: lambda py, px, pc: inputs["sd"].at[(py * 2 + px) * 2 + pc],
+    }
+    if "ed" in kinds:
+        half = inputs["ed"].shape[2] // 2
+    items, finals = [], []
+
+    def line_copy(number, d, src, dst):
+        return remote(src, dst, zsend.at[number, d], zrecv.at[number, d], (line[d], y, x, c))
+
+    def add_item(kind, k):
+        own, sib, second, first = buffers[kind]
+        row = k
+        zs = line[k] if kind in ("attn", "egu", "sgu") else k
+        item = SumItem(
+            here,
+            len(items),
+            places[kind](zs),
+            (own.at[row], sib.at[row], second.at[row], first.at[row]),
+            (k % 2 == 1),
+        )
+        items.append(item)
+        number = ("egu", "sgu", "attn").index(kind) if kind in ("egu", "sgu", "attn") else None
+
+        def finish(wait):
+            result = first.at[row]
+            if kind in ("ed", "sd"):
+                out = outputs[kind]
+                dst = out.at[pl.ds(k * half, half)] if kind == "ed" else out
+                copy = pltpu.make_async_copy(result, dst, store.at[item.index])
+                copy.wait() if wait else copy.start()
+                return
+            dst = zbuf.at[z] if kind == "attn" else outputs[kind].at[z]
+            if k == 0:
+                copy = pltpu.make_async_copy(result, dst, store.at[item.index])
+                copy.wait() if wait else copy.start()
+                return
+            copy = line_copy(number, k, result, dst)
+            if not wait:
+                copy.start()
+                return
+            copy.wait_send()
+            frm = line[(nz - k) % nz]
+            dst = zbuf.at[frm] if kind == "attn" else outputs[kind].at[frm]
+            line_copy(number, k, dst, dst).wait_recv()
+
+        finals.append(finish)
+
+    order = {"ed": range(2), "sd": range(1)}
+    for kind in kinds:
+        steps_of = order.get(kind, [d for d in range(nz - 1, -1, -1)])
+        for k in steps_of:
+            add_item(kind, k)
+
+    line_steps = []
+    if extra:
+        line_steps, line_end = line_sum_steps(
+            z, nz, out_parts, out_total, up, down, line_send, line_recv, line_partners(here, nz), LINE_PIECES
+        )
+        out_load.wait()
+    for item in items:
+        item.begin(load, send, recv)
+    count = len(items)
+    for t in range(count + 2 * SUM_LAG):
+        if t < count:
+            items[t].after_core(load, send, recv)
+        if line_steps:
+            line_steps.pop(0)()
+        if 0 <= t - SUM_LAG < count:
+            items[t - SUM_LAG].after_second(send, recv)
+        if 0 <= t - 2 * SUM_LAG < count:
+            items[t - 2 * SUM_LAG].after_first(send, recv)
+            finals[t - 2 * SUM_LAG](False)
+    for step in line_steps:
+        step()
+    if extra:
+        line_end()
+    for finish in finals:
+        finish(True)
+    if "attn" in kinds:
+        total = outputs["attn"]
+        columns = total.shape[1] // 5
+
+        @pl.loop(0, 5)
+        def _(i):
+            part = pl.ds(pl.multiple_of(i * columns, 128), columns)
+            total[:, part] = sum(zbuf[k, :, part].astype(f32) for k in range(nz))
+
+    for item in items:
+        item.end(send, recv)
+
+
+def sum_fast(arrays, out_parts, collective_id):
+    nz = lax.axis_size("z")
+    kinds = tuple(arrays)
+    shape = {kind: arrays[kind].shape[-2:] for kind in kinds}
+    rows = {kind: nz for kind in kinds} | {"ed": 2, "sd": 1}
+    if "ed" in kinds:
+        shape["ed"] = (shape["ed"][0] // 2, shape["ed"][1])
+    results, specs = [], []
+    for kind in kinds:
+        if kind == "attn":
+            results.append(jax.ShapeDtypeStruct(shape[kind], f32))
+            specs.append(pl.BlockSpec(memory_space=pltpu.VMEM))
+        else:
+            whole = {"ed": arrays[kind].shape[-2:], "sd": arrays[kind].shape[-2:]}.get(kind, (nz, *shape[kind]))
+            results.append(jax.ShapeDtypeStruct(whole, bf16))
+            specs.append(pl.BlockSpec(memory_space=pl.ANY))
+    operands = list(arrays.values())
+    scratch, items = [], 0
+    for kind in kinds:
+        n, block = rows[kind], shape[kind]
+        items += n
+        scratch += [pltpu.VMEM((n, 4, *block), bf16), pltpu.VMEM((n, 4, *block), bf16)]
+        scratch += [pltpu.VMEM((n, 2, *block), bf16), pltpu.VMEM((n, *block), bf16)]
+    if "attn" in kinds:
+        scratch.append(pltpu.VMEM((nz, *shape["attn"]), bf16))
+    dma = pltpu.SemaphoreType.DMA
+    scratch += [dma((items, 4)), dma((items, 7)), dma((items, 7)), dma((3, nz)), dma((3, nz)), dma((items,))]
+    extra = out_parts is not None
+    if extra:
+        out_parts = out_parts.reshape(nz, -1, out_parts.shape[-1])
+        operands.append(out_parts)
+        results.append(jax.ShapeDtypeStruct(out_parts.shape[1:], f32))
+        specs.append(pl.BlockSpec(memory_space=pltpu.VMEM))
+        sems = dma((2, nz, LINE_PIECES))
+        scratch += [pltpu.VMEM(out_parts.shape, bf16)] * 3 + [dma, sems, sems]
+    return pl.pallas_call(
+        functools.partial(sum_kernel, nz, kinds, extra),
+        out_shape=results,
+        in_specs=any_specs(len(operands)),
+        out_specs=specs,
+        scratch_shapes=scratch,
+        compiler_params=params(collective_id, 58 << 20),
+        name="sum_" + "_".join(kinds),
+    )(*operands)
+
+
+def sum_everything_fast(attn, egu, sgu, ed, sd, out_parts):
+    nz = lax.axis_size("z")
+    wide = egu.shape[-1]
+    arrays = {
+        "ed": ed.reshape(4, 2, -1, ed.shape[-1]),
+        "egu": egu.reshape(4, nz * 2, -1, wide),
+        "sd": sd.reshape(8, -1, sd.shape[-1]),
+        "sgu": sgu.reshape(nz * 8, -1, wide),
+        "attn": attn.reshape(nz * 8, -1, attn.shape[-1]),
+    }
+    ed, egu, sd, sgu, attn, out = sum_fast(arrays, out_parts, 3)
+    return attn, egu, sgu, ed, sd, out
 
 
 def visible_units(prefix, heads, here, length):
@@ -206,11 +881,15 @@
     cot_routes = jnp.concatenate(
         [cot, pair_ids.astype(bf16), jnp.zeros((count, MISC - TOP_K), bf16)], axis=1
     )
-    attn_full = gather_all(attn_shard)
-    egu, sgu, ed, sd = gather_weights(
-        slices(expert_gate[0], expert_up[0]), slices(shared_gate, shared_up), expert_down[0], shared_down
+    gather_inputs = gather_inputs_fast if paired() else gather_inputs_plain
+    attn_full, egu, sgu, ed, sd, cot_line = gather_inputs(
+        attn_shard,
+        slices(expert_gate[0], expert_up[0]),
+        slices(shared_gate, shared_up),
+        expert_down[0],
+        shared_down,
+        cot_routes,
     )
-    cot_line = gather_line(cot_routes)
 
     w_qkv = attn_full[:, : 3 * width]
     w_out = attn_full[:, 3 * width : 4 * width]
@@ -236,7 +915,7 @@
     ffn_norm = attended * ffn_scale
     mixed = (ffn_norm * gain_ffn).astype(bf16)
 
-    mixed_line = gather_line(mixed)
+    mixed_line = (gather_line_fast if paired() else gather_line)(mixed)
     cot_rows = cot_line[:, :width]
     ids = cot_line[:, width : width + TOP_K].astype(jnp.int32)
     lines = mixed_line.shape[0]
@@ -309,9 +988,7 @@
     mixed_part = jnp.concatenate(
         [mixed_part.astype(bf16), pair_dot.astype(bf16), jnp.zeros((lines, MISC - TOP_K), bf16)], axis=1
     )
-    mixed_sum = sum_line(mixed_part).astype(f32)
-    out_sum = sum_line(out_part).astype(f32)
-    block_rows = (attended + out_sum).astype(bf16)
+    mixed_sum = (sum_line_fast if paired() else sum_line)(mixed_part).astype(f32)
 
     hot, probs = gates(mixed, pair_ids)
     gate_grads = mixed_sum[:, width : width + TOP_K]
@@ -344,8 +1021,12 @@
         [grad_router, grad_gattn[:, None], grad_gffn[:, None], jnp.zeros((width, MISC - experts - 2), f32)], axis=1
     )
     attn_parts = jnp.concatenate([grad_wqkv, grad_wout, grad_misc], axis=1).astype(bf16)
-    attn_sums = sum_all(attn_parts).astype(f32)
-    egu_sum, sgu_sum, ed_sum, sd_sum = sum_weights(grad_egu, grad_sgu, grad_ed, grad_sd)
+    sum_everything = sum_everything_fast if paired() else sum_everything_plain
+    attn_sums, egu_sum, sgu_sum, ed_sum, sd_sum, out_sum = sum_everything(
+        attn_parts, grad_egu, grad_sgu, grad_ed, grad_sd, out_part
+    )
+    attn_sums = attn_sums.astype(f32)
+    block_rows = (attended + out_sum.astype(f32)).astype(bf16)
 
     def joined(blocks):
         both = jnp.transpose(blocks.reshape(nz, -1, 2, slice_ff), (2, 1, 0, 3)).astype(f32)

time: 776 us -> 586 us (0.76)
  waiting for transfers between devices: 384 us -> 27.5 us
  Pallas kernels: 0 us -> 242 us
  blocking collectives: 82.1 us -> 0 us
  between operations: 15.5 us -> 2.63 us
  matrix products: 120 us -> 132 us
    pallas_call x0 -> x4, Pallas kernels: none -> 242 us  [the longest x1 101 us: sum_fast(): pl.pallas_call(functools.partial(sum_kernel, nz, kinds, extra), out_shape...]
    reduce_scatter x6 -> x0, waiting for transfers between devices: 108 us -> none  [the longest x1 44.9 us: sum_weights(): ed = lax.psum_scatter(ed, PLANE, scatter_dimension=0, tiled=True)[0]]
    unnamed x14 -> x0, waiting for transfers between devices: 99.5 us -> none
    all_gather x6 -> x0, waiting for transfers between devices: 96.7 us -> none  [the longest x2 43.5 us: spread(): lax.all_gather(mine, PLANE, axis=0).reshape(ny, ne, nz, *blocks.shape[1:])]
    all_to_all x4 -> x0, blocking collectives: 70.3 us -> none  [the longest x2 44.1 us: spread(): mine = lax.all_to_all(blocks, 'z', 0, 0, tiled=True)]
    all_to_all x2, waiting for transfers between devices: 55.6 us -> 20 us  [to_units(): units = lax.all_to_all(units, DP, 0, 0, tiled=True)]
    all_to_all x1 -> x2, waiting for transfers between devices: 24.1 us -> 7.6 us  [from_units(): parts = lax.all_to_all(parts, DP, 0, 0, tiled=True)]
    reshape x7 -> x1, local copies, waits for them, and re-layouts: 16.9 us -> 0.66 us  [shards(): pair_ids = routes.reshape(count, TOP_K)]
  transfers between devices with their start and end apart: 17 -> 4, of which waited for: 12 -> 3; matrix products, arithmetic and copies ran while one was open for 24% -> 8% of each run, Pallas kernels for 0% -> 0%
where the time goes in v2:
time: 586 us; the launch traced here: 576 us
  Pallas kernels  242 us (41%)
  matrix products  132 us (23%)
  local copies, waits for them, and re-layouts  95 us (16%)
  other arithmetic  52.9 us (9%)
  waiting for transfers between devices  27.5 us (5%)
  starting transfers between devices  23.4 us (4%)
    dot_general x30, matrix products, dot(): return lax.dot_general(a, b, (dims, batch), preferred_element_type=f32)  128 us
    pallas_call x1, Pallas kernels, sum_fast(): pl.pallas_call(functools.partial(sum_kernel, nz, kinds, extra), out_shape...  101 us
    pallas_call x1, Pallas kernels, gather_inputs_fast(): pl.pallas_call(functools.partial(gather_kernel, nz), out_shape=[jax.Shape...  80.1 us
    pallas_call x1, Pallas kernels, sum_line_fast(): pl.pallas_call(functools.partial(line_sum_kernel, nz), out_shape=jax.Shap...  34.4 us
    pallas_call x1, Pallas kernels, gather_line_fast(): pl.pallas_call(functools.partial(line_gather_kernel, nz), out_shape=jax.S...  26.9 us
    all_to_all x2, waiting for transfers between devices, to_units(): units = lax.all_to_all(units, DP, 0, 0, tiled=True)  20 us
    unnamed x186, local copies, waits for them, and re-layouts  17.1 us
    all_to_all x2, starting transfers between devices, to_units(): units = lax.all_to_all(units, DP, 0, 0, tiled=True)  13.6 us
  transfers between devices with their start and end apart: 4, of which 3 were waited for; matrix products, arithmetic and copies ran while one was open for 8% of the time, Pallas kernels for 0%

profile of v2, /device:TPU:0, one launch (start us, length us, event | category | flops | bytes accessed | tf_op | source)
XLA Modules:
  0.0 575.6 jit_solution(16948656603360244777)
XLA Ops:
  12.5 80.1 %gather_inputs.1 = (bf16[32,24,3200]{2,1,0:T(8,128)(2,1)}, bf16[4,8,96,1024]{3,2,1,0:T(8,128)(2,1)S(1)}, bf16[32,24,1024]{2,1,0:T(8,128)(2,1)S(1)}, bf16[4,2,256...) custom-call(bf16[24,3200]{1,0:T(8,128)(2,1)S(1)} %copy-done.8, ...), custom_call_target="tpu_custom_call" | custom-call | tf_op jit(solution)/shard_map/gather_inputs/pallas_call | solution.py:344
  113.4 7.2 %all-to-all-start = ((bf16[8,3,3,64,128]{4,3,1,2,0:T(8,128)(2,1)}), bf16[8,3,3,64,128]{4,3,1,2,0:T(8,128)(2,1)}, u32[]{:S(2)}, u32[]{:S(2)}) async-start(bf16[8,3,3,64,128]{4,3,1,2,0:T(8,128)(2,1)} %copy.321), calls=%async_computation | async-start | bytes 2359296 | tf_op jit(solution)/shard_map/all_to_all | solution.py:129
  128.6 19.9 %all-to-all-done = bf16[8,3,3,64,128]{4,3,1,2,0:T(8,128)(2,1)} async-done(((bf16[8,3,3,64,128]{4,3,1,2,0:T(8,128)(2,1)}), bf16[8,3,3,64,128]{4,3,1,2,0:T(8,128)(2,1)}, u32[]{:S(2)}, u32[]{:S(2)}) %all-to-all-start) | async-done | bytes 1179680 | tf_op jit(solution)/shard_map/all_to_all | solution.py:129
  150.0 5.0 fusion.4
  155.1 4.6 fusion.1
  159.7 4.5 fusion.26
  182.6 26.9 %gather_line.1 = bf16[4,256,768]{2,1,0:T(8,128)(2,1)S(1)} custom-call(bf16[256,768]{1,0:T(8,128)(2,1)S(1)} %multiply_convert_fusion.8.own), custom_call_target="tpu_custom_call" | custom-call | tf_op jit(solution)/shard_map/gather_line/pallas_call | solution.py:450
  219.1 7.2 %fusion.68 = f32[4,640,1024]{2,1,0:T(8,128)S(1)} fusion(bf16[4,640,768]{2,1,0:T(8,128)(2,1)} %bitcast.301, bf16[4,768,1024]{2,1,0:T(8,128)(2,1)S(1)} %bitcast.278), kind=kOutput, calls=%fused_computation.178 | convolution fusion | flops 4026531840 | bytes 20709376 | tf_op jit(solution)/shard_map/dot_general | solution.py:38
  231.0 5.4 fusion.3
  237.8 8.3 %multiply_convert_fusion.1 = (bf16[4,640,768]{2,1,0:T(8,128)(2,1)S(1)}, bf16[4,640,768]{2,1,0:T(8,128)(2,1)}) fusion(f32[4,640,768]{2,1,0:T(8,128)} %get-tuple-element.166, f32[4,640]{1,0:T(4,128)S(1)} %mul.373, f32[4,8,80,768]{3,2,1,0:T(8,128)} %copy.336), kind=kLoop, calls=%fused_computation.13 | loop fusion | flops 7864320 | bytes 23603200 | tf_op jit(solution)/shard_map/convert_element_type | solution.py:973
  253.3 12.0 %multiply_convert_fusion.3 = (bf16[4,640,512]{2,1,0:T(8,128)(2,1)}, bf16[4,640,512]{2,1,0:T(8,128)(2,1)}) fusion(f32[4,640,1024]{2,1,0:T(8,128)} %copy-done.22, bf16[4,640,768]{2,1,0:T(8,128)(2,1)} %get-tuple-element.157, bf16[4,512,768]{2,1,0:T(8,128)(2,1)} %bitcast.264), kind=kOutput, calls=%fused_computation.20 | convolution fusion | flops 2030305280 | bytes 22806528 | tf_op jit(solution)/shard_map/dot_general | solution.py:38
  265.3 10.5 %fusion.18 = bf16[4,640,768]{2,1,0:T(8,128)(2,1)} fusion(bf16[4,768,1024]{2,1,0:T(8,128)(2,1)} %bitcast.275, bf16[4,640,512]{2,1,0:T(8,128)(2,1)} %get-tuple-element.138, bf16[4,640,512]{2,1,0:T(8,128)(2,1)} %get-tuple-element.137), kind=kOutput, calls=%fused_computation.41 | convolution fusion | flops 4038983680 | bytes 15466496 | tf_op jit(solution)/shard_map/dot_general | solution.py:38
  284.9 5.2 multiply_convert_fusion.6
  299.7 34.4 %sum_line.1 = f32[256,896]{1,0:T(8,128)S(1)} custom-call(bf16[4,256,896]{2,1,0:T(8,128)(2,1)S(1)} %bitcast.263), custom_call_target="tpu_custom_call" | custom-call | tf_op jit(solution)/shard_map/sum_line/pallas_call | solution.py:533
  344.5 6.4 %all-to-all-start.2 = ((bf16[8,3,1,64,128]{4,3,1,2,0:T(8,128)(2,1)}), bf16[8,3,1,64,128]{4,3,1,2,0:T(8,128)(2,1)}, u32[]{:S(2)}, u32[]{:S(2)}) async-start(bf16[8,3,1,64,128]{4,3,1,2,0:T(8,128)(2,1)} %bitcast.315), calls=%async_computation.2 | async-start | bytes 786432 | tf_op jit(solution)/shard_map/all_to_all | solution.py:129
  369.1 10.9 %multiply_reduce_fusion = (f32[3,1024]{1,0:T(4,128)S(1)}, f32[3,1024,1024]{1,2,0:T(8,128)}) fusion(f32[3,1024]{1,0:T(4,128)S(1)} %copy-done.58, f32[3,1024,1024]{1,2,0:T(8,128)} %copy-done.15, pred[3,1024]{1,0:T(4,128)(4,1)S(1)} %iota_compare_fusion.5, pred[1024,1024]{0,1:T(8,128)(4,1)S(1)} %copy-done.26, bf16[3,64,1024]{2,1,0:T(8,128)(2,1)S(1)} %squeeze_reshape.3, ...), kind=kOutput, calls=%fused_computation.2 | convolution fusion | flops 424670208 | bytes 27037696 | tf_op jit(solution)/shard_map/dot_general | solution.py:38
  380.0 10.7 %multiply_convert_fusion = bf16[3,1024,1024]{1,2,0:T(8,128)(2,1)S(1)} fusion(f32[3,1024,1024]{1,2,0:T(8,128)} %get-tuple-element.169, f32[3,1024]{1,0:T(4,128)S(1)} %get-tuple-element.168, f32[3,1024]{1,0:T(4,128)S(1)} %copy-done.58, f32[3,1024,1024]{1,2,0:T(8,128)} %copy-done.15, pred[3,1024]{1,0:T(4,128)(4,1)S(1)} %iota_compare_fusion.5, ...), kind=kLoop, calls=%fused_computation.1 | loop fusion | flops 25165824 | bytes 32533504 | tf_op jit(solution)/shard_map/convert_element_type | solution.py:835
  399.9 6.2 %all-to-all-start.3 = ((bf16[8,3,3,64,128]{4,3,2,1,0:T(8,128)(2,1)}), bf16[8,3,3,64,128]{4,3,2,1,0:T(8,128)(2,1)S(1)}, u32[]{:S(2)}, u32[]{:S(2)}) async-start(bf16[8,3,3,64,128]{4,3,2,1,0:T(8,128)(2,1)} %maximum_bitcast_fusion), calls=%async_computation.3 | async-start | bytes 2359296 | tf_op jit(solution)/shard_map/all_to_all | solution.py:138
  406.2 4.5 fusion.10
  415.5 7.0 %convolution_convert_fusion.1 = bf16[4,768,1024]{2,1,0:T(8,128)(2,1)} fusion(bf16[4,640,768]{2,1,0:T(8,128)(2,1)S(1)} %bitcast.302, bf16[4,640,512]{2,1,0:T(8,128)(2,1)S(1)} %copy-done.78, bf16[4,640,512]{2,1,0:T(8,128)(2,1)S(1)} %copy-done.77), kind=kOutput, calls=%fused_computation.26 | convolution fusion | flops 4040163328 | bytes 15466496 | tf_op jit(solution)/shard_map/dot_general | solution.py:38
  422.5 4.7 all-to-all-done.3
  434.1 4.7 multiply_reduce_fusion.1
  443.9 8.2 %concatenate.50.refs_4_ = bf16[32,24,3200]{2,1,0:T(8,128)(2,1)} concatenate(bf16[32,24,2304]{2,1,0:T(8,128)(2,1)} %convolution_convert_fusion, bf16[32,24,768]{2,1,0:T(8,128)(2,1)S(1)} %copy-done.29, bf16[32,24,4]{2,1,0:T(8,128)(2,1)} %copy.368, bf16[32,24,1]{2,1,0:T(8,128)(2,1)} %concatenate.53, bf16[32,24,1]{2,1,0:T(8,128)(2,1)} %concatenate.54, ...), dimensions={2} | concatenate | bytes 9830400 | tf_op jit(solution)/shard_map/concatenate | solution.py:1023
  452.1 100.9 %sum_ed_egu_sd_sgu_attn.1 = (bf16[256,768]{1,0:T(8,128)(2,1)}, bf16[4,96,1024]{2,1,0:T(8,128)(2,1)}, bf16[64,768]{1,0:T(8,128)(2,1)}, bf16[4,24,1024]{2,1,0:T(8,...) custom-call(bf16[4,2,256,768]{3,2,1,0:T(8,128)(2,1)} %bitcast.307, bf16[4,8,96,1024]{3,2,1,0:T(8,128)(2,1)} %bitcast.291, ...), custom_call_target="tpu_custom_call" | custom-call | tf_op jit(solution)/shard_map/sum_ed_egu_sd_sgu_attn/pallas_call | solution.py:778
  (356 shorter events, 177.7 us)
Async XLA Ops:
  0.6 125.5 %copy-start = (s32[2,1]{0,1:T(1,128)S(1)}, s32[2,1]{0,1:T(1,128)}, u32[]{:S(2)}) copy-start(s32[2,1]{0,1:T(1,128)} %param.19) | copy-start | bytes 28
  96.3 188.6 %copy-start.4 = (bf16[4,256,896]{2,1,0:T(8,128)(2,1)}, bf16[4,256,896]{2,1,0:T(8,128)(2,1)S(1)}, u32[]{:S(2)}) copy-start(bf16[4,256,896]{2,1,0:T(8,128)(2,1)S(1)} %get-tuple-element.28) | copy-start | bytes 5505028
  113.4 35.1 %all-to-all-start = ((bf16[8,3,3,64,128]{4,3,1,2,0:T(8,128)(2,1)}), bf16[8,3,3,64,128]{4,3,1,2,0:T(8,128)(2,1)}, u32[]{:S(2)}, u32[]{:S(2)}) async-start(bf16[8,3,3,64,128]{4,3,1,2,0:T(8,128)(2,1)} %copy.321), calls=%async_computation | async-start | bytes 2359296 | tf_op jit(solution)/shard_map/all_to_all | solution.py:129
  126.1 28.9 %copy-start.56 = (s32[8,128,2]{1,2,0:T(2,128)}, s32[8,128,2]{1,2,0:T(2,128)S(1)}, u32[]{:S(2)}) copy-start(s32[8,128,2]{1,2,0:T(2,128)S(1)} %copy.333) | copy-start | bytes 24580
  127.2 41.6 %copy-start.18 = (bf16[8,128,320]{1,2,0:T(8,128)(2,1)}, bf16[8,128,320]{1,2,0:T(8,128)(2,1)S(1)}, u32[]{:S(2)}) copy-start(bf16[8,128,320]{1,2,0:T(8,128)(2,1)S(1)} %fusion.19) | copy-start | bytes 1966084
  165.1 15.2 %all-to-all-start.1 = ((bf16[8,3,1,64,128]{4,3,1,2,0:T(8,128)(2,1)}), bf16[8,3,1,64,128]{4,3,1,2,0:T(8,128)(2,1)S(1)}, u32[]{:S(2)}, u32[]{:S(2)}) async-start(bf16[8,3,1,64,128]{4,3,1,2,0:T(8,128)(2,1)} %bitcast.257), calls=%async_computation.1 | async-start | bytes 786432 | tf_op jit(solution)/shard_map/all_to_all | solution.py:138
  182.4 31.8 %copy-start.16 = (f32[256,768]{1,0:T(8,128)}, f32[256,768]{1,0:T(8,128)S(1)}, u32[]{:S(2)}) copy-start(f32[256,768]{1,0:T(8,128)S(1)} %get-tuple-element.164) | copy-start | bytes 2359300
  182.4 30.3 %copy-start.65 = (f32[256]{0:T(256)}, f32[256]{0:T(256)S(1)}, u32[]{:S(2)}) copy-start(f32[256]{0:T(256)S(1)} %add_rsqrt_fusion) | copy-start | bytes 3076
  182.6 29.0 %copy-start.33 = (bf16[8,3,1,64,128]{4,3,1,2,0:T(8,128)(2,1)S(1)}, bf16[8,3,1,64,128]{4,3,1,2,0:T(8,128)(2,1)}, u32[]{:S(2)}) copy-start(bf16[8,3,1,64,128]{4,3,1,2,0:T(8,128)(2,1)} %copy-done.32) | copy-start | bytes 1179652
  216.8 14.2 %slice-start.2 = ((s8[7864320]{0:T(1024)(128)(4,1)}), s8[4194304]{0:T(1024)(128)(4,1)S(1)}, s32[]{:S(2)}) async-start(s8[7864320]{0:T(1024)(128)(4,1)} %bitcast.281), calls=%async_computation.6 | async-start | bytes 8388608
  219.1 11.9 %slice-start.3 = ((s8[7864320]{0:T(1024)(128)(4,1)}), s8[3670016]{0:T(1024)(128)(4,1)S(1)}, s32[]{:S(2)}) async-start(s8[7864320]{0:T(1024)(128)(4,1)} %bitcast.281), calls=%async_computation.7 | async-start | bytes 7340032
  252.4 12.8 %copy-start.70 = (f32[256]{0:T(256)}, f32[256]{0:T(256)S(1)}, u32[]{:S(2)}) copy-start(f32[256]{0:T(256)S(1)} %reduce_max.29) | copy-start | bytes 3076
  252.5 12.8 %copy-start.73 = (f32[256]{0:T(256)}, f32[256]{0:T(256)S(1)}, u32[]{:S(2)}) copy-start(f32[256]{0:T(256)S(1)} %fusion.46) | copy-start | bytes 3076
  296.6 40.2 %copy-start.17 = (f32[256,768]{1,0:T(8,128)S(1)}, f32[256,768]{1,0:T(8,128)}, u32[]{:S(2)}) copy-start(f32[256,768]{1,0:T(8,128)} %copy-done.16) | copy-start | bytes 2359300
  296.6 40.2 %copy-start.66 = (f32[256]{0:T(256)S(1)}, f32[256]{0:T(256)}, u32[]{:S(2)}) copy-start(f32[256]{0:T(256)} %copy-done.65) | copy-start | bytes 3076
  339.7 19.2 %copy-start.27 = (f32[256,768]{1,0:T(8,128)}, f32[256,768]{1,0:T(8,128)S(1)}, u32[]{:S(2)}) copy-start(f32[256,768]{1,0:T(8,128)S(1)} %multiply_add_fusion) | copy-start | bytes 2359300
  339.7 19.2 %copy-start.5 = (bf16[4,256,896]{2,1,0:T(8,128)(2,1)S(1)}, bf16[4,256,896]{2,1,0:T(8,128)(2,1)}, u32[]{:S(2)}) copy-start(bf16[4,256,896]{2,1,0:T(8,128)(2,1)} %copy-done.4) | copy-start | bytes 5505028
  344.5 23.1 %all-to-all-start.2 = ((bf16[8,3,1,64,128]{4,3,1,2,0:T(8,128)(2,1)}), bf16[8,3,1,64,128]{4,3,1,2,0:T(8,128)(2,1)}, u32[]{:S(2)}, u32[]{:S(2)}) async-start(bf16[8,3,1,64,128]{4,3,1,2,0:T(8,128)(2,1)} %bitcast.315), calls=%async_computation.2 | async-start | bytes 786432 | tf_op jit(solution)/shard_map/all_to_all | solution.py:129
  369.0 10.9 %copy-start.50 = (bf16[3,64,1024]{2,1,0:T(8,128)(2,1)}, bf16[3,64,1024]{2,1,0:T(8,128)(2,1)S(1)}, u32[]{:S(2)}) copy-start(bf16[3,64,1024]{2,1,0:T(8,128)(2,1)S(1)} %squeeze_reshape.3) | copy-start | bytes 1179652
  369.0 24.9 %slice-start.4 = ((s8[12582912]{0:T(1024)(128)(4,1)}), s8[4194304]{0:T(1024)(128)(4,1)S(1)}, s32[]{:S(2)}) async-start(s8[12582912]{0:T(1024)(128)(4,1)} %bitcast.283), calls=%async_computation.8 | async-start | bytes 8388608
  369.1 24.9 %slice-start.5 = ((s8[12582912]{0:T(1024)(128)(4,1)}), s8[4194304]{0:T(1024)(128)(4,1)S(1)}, s32[]{:S(2)}) async-start(s8[12582912]{0:T(1024)(128)(4,1)} %bitcast.283), calls=%async_computation.9 | async-start | bytes 8388608
  380.0 10.7 %copy-start.37 = (bf16[3,3,64,1024]{3,2,0,1:T(8,128)(2,1)S(1)}, bf16[3,3,64,1024]{3,2,0,1:T(8,128)(2,1)}, u32[]{:S(2)}) copy-start(bf16[3,3,64,1024]{3,2,0,1:T(8,128)(2,1)} %copy-done.36) | copy-start | bytes 3538948
  380.0 14.0 %slice-start.6 = ((s8[12582912]{0:T(1024)(128)(4,1)}), s8[4194304]{0:T(1024)(128)(4,1)S(1)}, s32[]{:S(2)}) async-start(s8[12582912]{0:T(1024)(128)(4,1)} %bitcast.283), calls=%async_computation.10 | async-start | bytes 8388608
  399.9 27.3 %all-to-all-start.3 = ((bf16[8,3,3,64,128]{4,3,2,1,0:T(8,128)(2,1)}), bf16[8,3,3,64,128]{4,3,2,1,0:T(8,128)(2,1)S(1)}, u32[]{:S(2)}, u32[]{:S(2)}) async-start(bf16[8,3,3,64,128]{4,3,2,1,0:T(8,128)(2,1)} %maximum_bitcast_fusion), calls=%async_computation.3 | async-start | bytes 2359296 | tf_op jit(solution)/shard_map/all_to_all | solution.py:138
  (66 other events, 255.7 us)

commit v3 on v1

--- a/solution.py
+++ b/solution.py
@@ -1,8 +1,11 @@
+import functools
 import math
 
 import jax
 import jax.numpy as jnp
 from jax import lax
+from jax.experimental import pallas as pl
+from jax.experimental.pallas import tpu as pltpu
 from jax.sharding import Mesh
 from jax.sharding import PartitionSpec as P
 
@@ -71,6 +74,13 @@
 
 def gather_line(rows):
     return lax.all_gather(rows, "z", axis=0, tiled=True)
+
+
+def paired(batches, heads):
+    n_dp = lax.axis_size(DP)
+    here = batches * heads // n_dp
+    even = here * n_dp == batches * heads and heads % max(1, here) == 0
+    return even and tuple(lax.axis_size(name) for name in PLANE) == (2, 2, 2)
 
 
 def sum_line(rows):
@@ -123,6 +133,975 @@
     parts = lax.all_to_all(parts, DP, 0, 0, tiled=True)
     parts = parts.reshape(n_dp * here, kinds, HEAD_DIM, rows)[: batches * heads]
     return jnp.transpose(parts, (1, 0, 2, 3)).reshape(kinds, batches, heads * HEAD_DIM, rows)
+
+
+MESH = pl.DeviceIdType.MESH
+
+
+def position():
+    return tuple(lax.axis_index(name) for name in ALL)
+
+
+def remote(src, dst, send, recv, device):
+    return pltpu.make_async_remote_copy(
+        src_ref=src, dst_ref=dst, send_sem=send, recv_sem=recv, device_id=device, device_id_type=MESH
+    )
+
+
+def greet(partners):
+    barrier = pltpu.get_barrier_semaphore()
+    for device in partners:
+        pl.semaphore_signal(barrier, inc=1, device_id=device, device_id_type=MESH)
+    pl.semaphore_wait(barrier, len(partners))
+
+
+def any_specs(count):
+    return [pl.BlockSpec(memory_space=pl.ANY)] * count
+
+
+def params(collective_id, vmem=16 << 20):
+    return pltpu.CompilerParams(collective_id=collective_id, has_side_effects=True, vmem_limit_bytes=vmem)
+
+
+class PlaneItem:
+    def __init__(self, here, index, place, own, x_first):
+        self.here, self.index, self.place, self.own, self.x_first = here, index, place, own, x_first
+
+    def moved(self, along_first, along_second, along_core):
+        z, y, x, c = self.here
+        move_x, move_y = (along_first, along_second) if self.x_first else (along_second, along_first)
+        return (z, 1 - y if move_y else y, 1 - x if move_x else x, 1 - c if along_core else c)
+
+    def ref(self, *moves):
+        return self.place(*self.moved(*moves)[1:])
+
+    COPIES = (
+        ((0, 0, 0), (1, 0, 0)),
+        ((0, 0, 0), (0, 1, 0)),
+        ((1, 0, 0), (0, 1, 0)),
+        ((0, 0, 0), (0, 0, 1)),
+        ((1, 0, 0), (0, 0, 1)),
+        ((0, 1, 0), (0, 0, 1)),
+        ((1, 1, 0), (0, 0, 1)),
+    )
+
+    def copy(self, number, send, recv):
+        source, to = self.COPIES[number]
+        src = self.own if source == (0, 0, 0) else self.ref(*source)
+        return remote(
+            src, self.ref(*source), send.at[self.index, number], recv.at[self.index, number], self.moved(*to)
+        )
+
+    def arrival(self, number, send, recv):
+        source, to = self.COPIES[number]
+        ref = self.ref(*[a ^ b for a, b in zip(source, to)])
+        return remote(ref, ref, send.at[self.index, number], recv.at[self.index, number], self.moved(*to))
+
+
+def line_gather_steps(z, nz, own, out, sends, gets, neighbour, pieces):
+    rows = out.shape[1] // pieces
+
+    def copy(way, source, piece, src=None):
+        part = pl.ds(piece * rows, rows)
+        dst = out.at[source, part]
+        src = dst if src is None else src.at[part]
+        return remote(src, dst, sends.at[way, source, piece], gets.at[way, source, piece], neighbour(1 - 2 * way))
+
+    def may_send(way):
+        return z < nz - 1 if way == 0 else z > 0
+
+    def start():
+        for piece in range(pieces):
+            for way in range(2):
+                pl.when(may_send(way))(lambda: copy(way, z, piece, own).start())
+
+    def step(distance, piece):
+        for way in range(2):
+            source = z - distance if way == 0 else z + distance
+
+            @pl.when((source >= 0) & (source < nz))
+            def _():
+                copy(way, source, piece).wait_recv()
+                pl.when(may_send(way))(lambda: copy(way, source, piece).start())
+
+    def end():
+        for distance in range(nz):
+            for piece in range(pieces):
+                for way in range(2):
+                    source = z - distance if way == 0 else z + distance
+
+                    @pl.when((source >= 0) & (source < nz) & may_send(way))
+                    def _():
+                        copy(way, source, piece).wait_send()
+
+    steps = [functools.partial(step, distance, piece) for distance in range(1, nz) for piece in range(pieces)]
+    return start, steps, end
+
+
+def line_partners(here, nz):
+    z, y, x, c = here
+    return lambda way: (jnp.clip(z + way, 0, nz - 1), y, x, c)
+
+
+def greet_line(here, nz):
+    z = here[0]
+    neighbour = line_partners(here, nz)
+    barrier = pltpu.get_barrier_semaphore()
+
+    @pl.when(z > 0)
+    def _():
+        pl.semaphore_signal(barrier, inc=1, device_id=neighbour(-1), device_id_type=MESH)
+
+    @pl.when(z < nz - 1)
+    def _():
+        pl.semaphore_signal(barrier, inc=1, device_id=neighbour(1), device_id_type=MESH)
+
+    pl.semaphore_wait(barrier, jnp.where(z > 0, 1, 0) + jnp.where(z < nz - 1, 1, 0))
+
+
+LINE_PIECES = 2
+
+
+def line_gather_kernel(nz, own, out, local, sends, gets):
+    here = position()
+    z = here[0]
+    greet_line(here, nz)
+    start, steps, end = line_gather_steps(z, nz, own, out, sends, gets, line_partners(here, nz), LINE_PIECES)
+    start()
+    keep = pltpu.make_async_copy(own, out.at[z], local)
+    keep.start()
+    for step in steps:
+        step()
+    end()
+    keep.wait()
+
+
+def gather_line_fast(rows):
+    nz = lax.axis_size("z")
+    sems = pltpu.SemaphoreType.DMA((2, nz, LINE_PIECES))
+    out = pl.pallas_call(
+        functools.partial(line_gather_kernel, nz),
+        out_shape=jax.ShapeDtypeStruct((nz, *rows.shape), bf16),
+        in_specs=any_specs(1),
+        out_specs=pl.BlockSpec(memory_space=pl.ANY),
+        scratch_shapes=[pltpu.SemaphoreType.DMA, sems, sems],
+        compiler_params=params(1),
+        name="gather_line",
+    )(rows)
+    return out.reshape(-1, rows.shape[-1])
+
+
+def line_sum_steps(z, nz, parts, total, up, down, sends, gets, neighbour, pieces):
+    rows = parts.shape[1] // pieces
+    arrived = (up, down)
+
+    def copy(way, target, piece, src):
+        part = pl.ds(piece * rows, rows)
+        dst = arrived[way].at[target, part]
+        return remote(src, dst, sends.at[way, target, piece], gets.at[way, target, piece], neighbour(1 - 2 * way))
+
+    def part_of(ref, target, piece):
+        return ref.at[target, pl.ds(piece * rows, rows)]
+
+    def step(distance, piece):
+        for way in range(2):
+            target = nz - distance if way == 0 else distance - 1
+            ahead = z < target if way == 0 else z > target
+            first = z == 0 if way == 0 else z == nz - 1
+            mine, theirs = part_of(parts, target, piece), part_of(arrived[way], target, piece)
+
+            @pl.when(ahead & first)
+            def _():
+                copy(way, target, piece, mine).start()
+
+            @pl.when(ahead & jnp.logical_not(first))
+            def _():
+                copy(way, target, piece, theirs).wait_recv()
+                mine[...] = (mine[...].astype(f32) + theirs[...].astype(f32)).astype(bf16)
+                copy(way, target, piece, mine).start()
+
+    def end():
+        for piece in range(pieces):
+            part = pl.ds(piece * rows, rows)
+            total[part, :] = parts[z, part, :].astype(f32)
+            for way in range(2):
+                theirs = part_of(arrived[way], z, piece)
+
+                @pl.when(z > 0 if way == 0 else z < nz - 1)
+                def _():
+                    copy(way, z, piece, theirs).wait_recv()
+                    total[part, :] += theirs[...].astype(f32)
+
+        for distance in range(1, nz):
+            for piece in range(pieces):
+                for way in range(2):
+                    target = nz - distance if way == 0 else distance - 1
+
+                    @pl.when(z < target if way == 0 else z > target)
+                    def _():
+                        copy(way, target, piece, part_of(parts, target, piece)).wait_send()
+
+    steps = [functools.partial(step, distance, piece) for distance in range(1, nz) for piece in range(pieces)]
+    return steps, end
+
+
+def line_sum_kernel(nz, parts_in, total, parts, up, down, local, sends, gets):
+    here = position()
+    z = here[0]
+    load = pltpu.make_async_copy(parts_in, parts, local)
+    load.start()
+    greet_line(here, nz)
+    steps, end = line_sum_steps(z, nz, parts, total, up, down, sends, gets, line_partners(here, nz), LINE_PIECES)
+    load.wait()
+    for step in steps:
+        step()
+    end()
+
+
+def sum_line_fast(parts):
+    nz = lax.axis_size("z")
+    parts = parts.reshape(nz, -1, parts.shape[-1])
+    sems = pltpu.SemaphoreType.DMA((2, nz, LINE_PIECES))
+    return pl.pallas_call(
+        functools.partial(line_sum_kernel, nz),
+        out_shape=jax.ShapeDtypeStruct(parts.shape[1:], f32),
+        in_specs=any_specs(1),
+        out_specs=pl.BlockSpec(memory_space=pltpu.VMEM),
+        scratch_shapes=[pltpu.VMEM(parts.shape, bf16)] * 3 + [pltpu.SemaphoreType.DMA, sems, sems],
+        compiler_params=params(2, 32 << 20),
+        name="sum_line",
+    )(parts)
+
+
+class SumItem:
+    def __init__(self, here, index, place, buffers, x_first):
+        self.here, self.index, self.place, self.x_first = here, index, place, x_first
+        self.own, self.sib, self.second, self.first = buffers
+
+    moved = PlaneItem.moved
+
+    def slot(self, a, b):
+        return 2 * a + b
+
+    def begin(self, load, send, recv):
+        for a in range(2):
+            for b in range(2):
+                n = self.slot(a, b)
+                self.sib_copy(a, b, send, recv).start()
+                pltpu.make_async_copy(self.place(*self.moved(a, b, 0)[1:]), self.own.at[n], load.at[self.index, n]).start()
+
+    def sib_copy(self, a, b, send, recv):
+        n = self.slot(a, b)
+        src = self.place(*self.moved(a, b, 1)[1:])
+        return remote(src, self.sib.at[n], send.at[self.index, n], recv.at[self.index, n], self.moved(0, 0, 1))
+
+    def second_copy(self, a, send, recv):
+        n = 4 + a
+        src = self.sib.at[self.slot(a, 1)]
+        return remote(src, self.second.at[a], send.at[self.index, n], recv.at[self.index, n], self.moved(0, 1, 0))
+
+    def first_copy(self, send, recv):
+        src = self.second.at[1]
+        return remote(src, self.first, send.at[self.index, 6], recv.at[self.index, 6], self.moved(1, 0, 0))
+
+    def after_core(self, load, send, recv):
+        for b in (1, 0):
+            for a in range(2):
+                n = self.slot(a, b)
+                pltpu.make_async_copy(self.own.at[n], self.own.at[n], load.at[self.index, n]).wait()
+                self.sib_copy(a, b, send, recv).wait_recv()
+                add_to(self.sib.at[n], self.own.at[n])
+                if b == 1:
+                    self.second_copy(a, send, recv).start()
+
+    def after_second(self, send, recv):
+        for a in (1, 0):
+            self.second_copy(a, send, recv).wait_recv()
+            add_to(self.second.at[a], self.sib.at[self.slot(a, 0)])
+            if a == 1:
+                self.first_copy(send, recv).start()
+
+    def after_first(self, send, recv):
+        self.first_copy(send, recv).wait_recv()
+        add_to(self.first, self.second.at[0])
+
+    def end(self, send, recv):
+        for a in range(2):
+            for b in range(2):
+                self.sib_copy(a, b, send, recv).wait_send()
+            self.second_copy(a, send, recv).wait_send()
+        self.first_copy(send, recv).wait_send()
+
+
+def add_to(total, term):
+    rows, columns = total.shape
+    if rows % 16 == 0:
+
+        @pl.loop(0, rows // 16)
+        def _(i):
+            part = pl.ds(pl.multiple_of(i * 16, 16), 16)
+            total[part, :] = (total[part, :].astype(f32) + term[part, :].astype(f32)).astype(bf16)
+    else:
+        wide = max(w for w in (128, 256, 384, 512, 640) if columns % w == 0)
+
+        @pl.loop(0, columns // wide)
+        def _(i):
+            part = pl.ds(pl.multiple_of(i * wide, 128), wide)
+            total[:, part] = (total[:, part].astype(f32) + term[:, part].astype(f32)).astype(bf16)
+
+
+SUM_LAG = 2
+
+
+def unit_owner(number, batches, heads, here_units):
+    per_batch = heads // here_units
+    return number // per_batch, lax.rem(number, per_batch) * here_units
+
+
+def exchange(me, n_dp, copy):
+    ny = 2
+
+    def device(number):
+        return (number // ny, lax.rem(number, ny))
+
+    far = [lax.rem(me + d, n_dp) for d in range(1, n_dp)]
+    near = [lax.rem(me + n_dp - d, n_dp) for d in range(1, n_dp)]
+
+    def start():
+        for number in far:
+            copy(number, me, device(number)).start()
+
+    def arrive():
+        for number in near:
+            copy(me, number, device(number)).wait_recv()
+
+    def end():
+        for number in far:
+            copy(number, me, device(number)).wait_send()
+
+    return start, arrive, end
+
+
+def tile_spans(length):
+    tile = 256 if length % 512 == 0 else length // 2
+    for start in range(0, length, tile):
+        if start < length // 2:
+            yield start, tile, 0, length // 2
+        else:
+            yield start, tile, start, start + tile
+
+
+def masked(values, start, tile, mask_from, keys, length, fill):
+    key = mask_from + lax.broadcasted_iota(jnp.int32, (keys - mask_from, tile), 0)
+    query = start + lax.broadcasted_iota(jnp.int32, (keys - mask_from, tile), 1)
+    allowed = (key <= query) | ((key < length) & (query < length))
+    tail = jnp.where(allowed, values[mask_from:], fill)
+    return tail if mask_from == 0 else jnp.concatenate([values[:mask_from], tail], axis=0)
+
+
+def plane_items(here, arrays, outs):
+    egu_in, sgu_in, ed_in, sd_in = arrays
+    egu, sgu, ed, sd = outs
+    half = ed_in.shape[0] // 2
+    items = []
+
+    def add(place, own, x_first):
+        items.append(PlaneItem(here, len(items), place, own, x_first))
+
+    for h in range(2):
+        rows = pl.ds(h * half, half)
+        add(lambda py, px, pc, rows=rows: ed.at[px * 2 + pc, py, rows], ed_in.at[rows], h == 1)
+    for zs in range(egu_in.shape[0]):
+        add(lambda py, px, pc, zs=zs: egu.at[px * 2 + pc, zs * 2 + py], egu_in.at[zs], zs % 2 == 1)
+    for zs in range(sgu_in.shape[0]):
+        add(lambda py, px, pc, zs=zs: sgu.at[((zs * 2 + py) * 2 + px) * 2 + pc], sgu_in.at[zs], zs % 2 == 1)
+    add(lambda py, px, pc: sd.at[(py * 2 + px) * 2 + pc], sd_in, False)
+    return items
+
+
+def attend_kernel(nz, *refs):
+    prefix, qkv, egu_in, sgu_in, ed_in, sd_in, cot_in = refs[:7]
+    context, units, lse, egu, sgu, ed, sd, cot = refs[7:15]
+    result, local, send, recv, csend, crecv, psend, precv, lsend, lrecv = refs[15:]
+    here = position()
+    z, y, x, c = here
+    n_dp = nz * 2
+    me = z * 2 + y
+    kinds, batches, width, rows = qkv.shape
+    heads = width // HEAD_DIM
+    count = units.shape[1] // HEAD_DIM
+    span = count * HEAD_DIM
+    length = units.shape[2]
+    greet(
+        [(lax.rem(me + d, n_dp) // 2, lax.rem(me + d, 2), x, c) for d in range(1, n_dp)]
+        + [(z, y, 1 - x, c), (z, y, x, 1 - c)]
+    )
+
+    def columns(number):
+        return pl.ds(pl.multiple_of(number * rows, rows), rows)
+
+    def qkv_block(number):
+        batch, head = unit_owner(number, batches, heads, count)
+        return qkv.at[:, batch, pl.ds(pl.multiple_of(head * HEAD_DIM, HEAD_DIM), span), :]
+
+    def qkv_copy(number, source, device):
+        return remote(
+            qkv_block(number), units.at[:, :, columns(source)], send.at[number], recv.at[source], (*device, x, c)
+        )
+
+    start, arrive, end = exchange(me, n_dp, qkv_copy)
+    start()
+    keep = pltpu.make_async_copy(qkv_block(me), units.at[:, :, columns(me)], local.at[0])
+    keep.start()
+    items = plane_items(here, (egu_in, sgu_in, ed_in, sd_in), (egu, sgu, ed, sd))
+    for item in items:
+        for number in (0, 1, 3):
+            item.copy(number, psend, precv).start()
+    owns = [(cot_in, cot.at[z]), (ed_in, ed.at[x * 2 + c, y]), (sd_in, sd.at[(y * 2 + x) * 2 + c])]
+    owns += [(egu_in.at[zs], egu.at[x * 2 + c, zs * 2 + y]) for zs in range(nz)]
+    owns += [(sgu_in.at[zs], sgu.at[((zs * 2 + y) * 2 + x) * 2 + c]) for zs in range(nz)]
+    keeps = [pltpu.make_async_copy(src, dst, local.at[1 + i]) for i, (src, dst) in enumerate(owns)]
+    for copy in keeps:
+        copy.start()
+
+    def have_first(item):
+        item.arrival(0, psend, precv).wait_recv()
+        item.copy(2, psend, precv).start()
+        item.copy(4, psend, precv).start()
+
+    def have_second(item):
+        item.arrival(1, psend, precv).wait_recv()
+        item.copy(5, psend, precv).start()
+        item.arrival(2, psend, precv).wait_recv()
+        item.copy(6, psend, precv).start()
+
+    early = len(items) // 2
+    for item in items[:early]:
+        have_first(item)
+    arrive()
+    keep.wait()
+    line_start, line_steps, line_end = line_gather_steps(
+        z, nz, cot_in, cot, lsend, lrecv, line_partners(here, nz), LINE_PIECES
+    )
+    line_start()
+
+    my_batch, my_head = unit_owner(me, batches, heads, count)
+    limit = prefix[my_batch, 0]
+
+    def context_copy(head):
+        def copy(number, source, device):
+            _, first_head = unit_owner(source, batches, heads, count)
+            batch, _ = unit_owner(source, batches, heads, count)
+            part = pl.ds(pl.multiple_of((first_head + head) * HEAD_DIM, HEAD_DIM), HEAD_DIM)
+            return remote(
+                result.at[pl.ds(head * HEAD_DIM, HEAD_DIM), columns(number)],
+                context.at[batch, part, :],
+                csend.at[head, number],
+                crecv.at[head, source],
+                (*device, x, c),
+            )
+
+        return copy
+
+    def attend(head):
+        part = pl.ds(head * HEAD_DIM, HEAD_DIM)
+        for first, tile, mask_from, keys in tile_spans(length):
+            queries = units[0, part, pl.ds(first, tile)] * bf16(1.0 / math.sqrt(HEAD_DIM))
+            scores = dot(units[1, part, pl.ds(0, keys)], queries, ((0,), (0,)))
+            scores = masked(scores, first, tile, mask_from, keys, limit, neg_fill)
+            top = jnp.max(scores, axis=0, keepdims=True)
+            weights = jnp.exp(scores - top)
+            total = jnp.sum(weights, axis=0, keepdims=True)
+            lse[head, :, pl.ds(first, tile)] = top + jnp.log(total)
+            mean = dot(units[2, part, pl.ds(0, keys)], weights.astype(bf16), ((1,), (0,))) / total
+            result[part, pl.ds(first, tile)] = mean.astype(bf16)
+
+    exchanges = [exchange(me, n_dp, context_copy(head)) for head in range(count)]
+    own_part = [pl.ds(pl.multiple_of((my_head + head) * HEAD_DIM, HEAD_DIM), HEAD_DIM) for head in range(count)]
+    own_copies = [
+        pltpu.make_async_copy(
+            result.at[pl.ds(head * HEAD_DIM, HEAD_DIM), columns(me)],
+            context.at[my_batch, own_part[head], :],
+            local.at[1 + len(owns) + head],
+        )
+        for head in range(count)
+    ]
+    later = [functools.partial(have_first, item) for item in items[early:]]
+    later += [functools.partial(have_second, item) for item in items]
+    line_steps = list(line_steps)
+    for head in range(count):
+        attend(head)
+        exchanges[head][0]()
+        own_copies[head].start()
+        if head == 0:
+            for step in later[: len(items) - early]:
+                step()
+            later = later[len(items) - early :]
+            for step in line_steps[:LINE_PIECES]:
+                step()
+            line_steps = line_steps[LINE_PIECES:]
+    share = -(-len(later) // max(1, len(line_steps)))
+    while later or line_steps:
+        for step in later[:share]:
+            step()
+        later = later[share:]
+        if line_steps:
+            line_steps.pop(0)()
+    for item in items:
+        for number in range(3, 7):
+            item.arrival(number, psend, precv).wait_recv()
+    for head in range(count):
+        exchanges[head][1]()
+        own_copies[head].wait()
+    for item in items:
+        for number in range(7):
+            item.copy(number, psend, precv).wait_send()
+    end()
+    line_end()
+    for head in range(count):
+        exchanges[head][2]()
+    for copy in keeps:
+        copy.wait()
+
+
+def attend_fast(prefix, qkv, egu, sgu, ed, sd, cot):
+    nz = lax.axis_size("z")
+    n_dp = nz * 2
+    kinds, batches, width, rows = qkv.shape
+    heads = width // HEAD_DIM
+    count = batches * heads // n_dp
+    length = n_dp * rows
+    any_space, vmem = pl.BlockSpec(memory_space=pl.ANY), pl.BlockSpec(memory_space=pltpu.VMEM)
+    shapes = [
+        ((batches, width, rows), bf16),
+        ((kinds, count * HEAD_DIM, length), bf16),
+        ((count, 1, length), f32),
+        ((4, nz * 2, *egu.shape[1:]), bf16),
+        ((nz * 8, *sgu.shape[1:]), bf16),
+        ((4, 2, *ed.shape), bf16),
+        ((8, *sd.shape), bf16),
+        ((nz, *cot.shape), bf16),
+    ]
+    dma = pltpu.SemaphoreType.DMA
+    items = 2 * nz + 3
+    line = dma((2, nz, LINE_PIECES))
+    context, units, lse, egu, sgu, ed, sd, cot = pl.pallas_call(
+        functools.partial(attend_kernel, nz),
+        out_shape=[jax.ShapeDtypeStruct(*shape) for shape in shapes],
+        in_specs=[pl.BlockSpec(memory_space=pltpu.SMEM)] + [any_space] * 6,
+        out_specs=[any_space, vmem, vmem] + [any_space] * 5,
+        scratch_shapes=[
+            pltpu.VMEM((count * HEAD_DIM, length), bf16),
+            dma((4 + 2 * nz + count,)),
+            dma((n_dp,)),
+            dma((n_dp,)),
+            dma((count, n_dp)),
+            dma((count, n_dp)),
+            dma((items, 7)),
+            dma((items, 7)),
+            line,
+            line,
+        ],
+        compiler_params=params(4, 40 << 20),
+        name="attend",
+    )(prefix, qkv, egu, sgu, ed, sd, cot)
+    weights = (
+        egu.reshape(4, -1, egu.shape[-1]),
+        sgu.reshape(-1, sgu.shape[-1]),
+        ed.reshape(4, -1, ed.shape[-1]),
+        sd.reshape(-1, sd.shape[-1]),
+    )
+    return context, (units, lse), weights, cot.reshape(-1, cot.shape[-1])
+
+
+def first_kernel(nz, *refs):
+    attn_in, egu_in, sgu_in, attn, egu, sgu, local, zsend, zrecv, psend, precv = refs
+    here = position()
+    z, y, x, c = here
+    line = [lax.rem(z + d, nz) for d in range(nz)]
+    greet([(line[d], y, x, c) for d in range(1, nz)] + [(z, 1 - y, x, c), (z, y, 1 - x, c), (z, y, x, 1 - c)])
+
+    def flat(zs, py, px, pc):
+        return ((zs * 2 + py) * 2 + px) * 2 + pc
+
+    def line_copy(kind, d, arriving=False):
+        to, frm = line[d], line[(nz - d) % nz]
+        at = frm if arriving else z
+        dst = (attn.at[flat(at, y, x, c)], egu.at[at], sgu.at[at])[kind]
+        src = dst if arriving else (attn_in, egu_in.at[to], sgu_in.at[to])[kind]
+        return remote(src, dst, zsend.at[kind, d], zrecv.at[kind, d], (to, y, x, c))
+
+    for d in (2, 1, 3) if nz == 4 else range(1, nz):
+        line_copy(0, d).start()
+    items = []
+    for d in range(nz):
+        frm = line[(nz - d) % nz]
+        place = lambda py, px, pc, frm=frm: attn.at[flat(frm, py, px, pc)]
+        items.append(PlaneItem(here, d, place, attn_in if d == 0 else place(y, x, c), d % 2 == 1))
+
+    def have_own(item):
+        for number in (0, 1, 3):
+            item.copy(number, psend, precv).start()
+
+    have_own(items[0])
+    for kind in (1, 2):
+        for d in range(1, nz):
+            line_copy(kind, d).start()
+    owns = [(attn_in, attn.at[flat(z, y, x, c)]), (egu_in.at[z], egu.at[z]), (sgu_in.at[z], sgu.at[z])]
+    keeps = [pltpu.make_async_copy(src, dst, local.at[i]) for i, (src, dst) in enumerate(owns)]
+    for copy in keeps:
+        copy.start()
+    for d in range(1, nz):
+        line_copy(0, d, True).wait_recv()
+        have_own(items[d])
+    for item in items:
+        item.arrival(0, psend, precv).wait_recv()
+        item.copy(2, psend, precv).start()
+        item.copy(4, psend, precv).start()
+    for item in items:
+        item.arrival(1, psend, precv).wait_recv()
+        item.copy(5, psend, precv).start()
+    for item in items:
+        item.arrival(2, psend, precv).wait_recv()
+        item.copy(6, psend, precv).start()
+    for item in items:
+        for number in range(3, 7):
+            item.arrival(number, psend, precv).wait_recv()
+    for kind in (1, 2):
+        for d in range(1, nz):
+            line_copy(kind, d, True).wait_recv()
+    for item in items:
+        for number in range(7):
+            item.copy(number, psend, precv).wait_send()
+    for kind in range(3):
+        for d in range(1, nz):
+            line_copy(kind, d).wait_send()
+    for copy in keeps:
+        copy.wait()
+
+
+def first_fast(attn, egu, sgu):
+    nz = lax.axis_size("z")
+    dma = pltpu.SemaphoreType.DMA
+    shapes = [(nz * 8, *attn.shape), egu.shape, sgu.shape]
+    attn, egu, sgu = pl.pallas_call(
+        functools.partial(first_kernel, nz),
+        out_shape=[jax.ShapeDtypeStruct(shape, bf16) for shape in shapes],
+        in_specs=any_specs(3),
+        out_specs=any_specs(3),
+        scratch_shapes=[dma((3,)), dma((3, nz)), dma((3, nz)), dma((nz, 7)), dma((nz, 7))],
+        compiler_params=params(0),
+        name="first",
+    )(attn, egu, sgu)
+    return attn.reshape(-1, attn.shape[-1]), egu, sgu
+
+
+def backward_kernel(nz, kinds, *refs):
+    refs = list(refs)
+    take = lambda n: [refs.pop(0) for _ in range(n)]
+    prefix, grad_in, units, lse = take(4)
+    inputs = dict(zip(kinds, take(len(kinds))))
+    (rows_in,) = take(1)
+    (grads,) = take(1)
+    outputs = dict(zip(kinds, take(len(kinds))))
+    (rows_total,) = take(1)
+    grad, dkey, dvalue, result = take(4)
+    buffers = {kind: take(4) for kind in kinds}
+    local, send, recv, csend, crecv, load, psend, precv, store = take(9)
+    rows_parts, up, down, lload, lsend, lrecv = take(6)
+    here = position()
+    z, y, x, c = here
+    n_dp = nz * 2
+    me = z * 2 + y
+    batches, width, rows = grad_in.shape
+    heads = width // HEAD_DIM
+    span, length = grad.shape
+    count = span // HEAD_DIM
+    row_load = pltpu.make_async_copy(rows_in, rows_parts, lload)
+    row_load.start()
+    greet(
+        [(lax.rem(me + d, n_dp) // 2, lax.rem(me + d, 2), x, c) for d in range(1, n_dp)]
+        + [(z, y, 1 - x, c), (z, y, x, 1 - c)]
+    )
+
+    def columns(number):
+        return pl.ds(pl.multiple_of(number * rows, rows), rows)
+
+    def grad_block(number):
+        batch, head = unit_owner(number, batches, heads, count)
+        return grad_in.at[batch, pl.ds(pl.multiple_of(head * HEAD_DIM, HEAD_DIM), span), :]
+
+    def grad_copy(number, source, device):
+        return remote(
+            grad_block(number), grad.at[:, columns(source)], send.at[number], recv.at[source], (*device, x, c)
+        )
+
+    start, arrive, end = exchange(me, n_dp, grad_copy)
+    start()
+    keep = pltpu.make_async_copy(grad_block(me), grad.at[:, columns(me)], local.at[0])
+    keep.start()
+
+    half = inputs["ed"].shape[2] // 2
+    places = {
+        "egu": lambda zs: lambda py, px, pc: inputs["egu"].at[px * 2 + pc, zs * 2 + py],
+        "sgu": lambda zs: lambda py, px, pc: inputs["sgu"].at[((zs * 2 + py) * 2 + px) * 2 + pc],
+        "ed": lambda h: lambda py, px, pc: inputs["ed"].at[px * 2 + pc, py, pl.ds(h * half, half)],
+        "sd": lambda h: lambda py, px, pc: inputs["sd"].at[(py * 2 + px) * 2 + pc],
+    }
+    targets = {
+        "egu": lambda k: outputs["egu"].at[k],
+        "sgu": lambda k: outputs["sgu"].at[k],
+        "ed": lambda k: outputs["ed"].at[pl.ds(k * half, half)],
+        "sd": lambda k: outputs["sd"],
+    }
+    number_of = {"egu": nz, "sgu": nz, "ed": 2, "sd": 1}
+    items, finals = [], []
+    for kind in kinds:
+        for k in range(number_of[kind]):
+            parts = tuple(buffer.at[k] for buffer in buffers[kind])
+            item = SumItem(here, len(items), places[kind](k), parts, k % 2 == 1)
+            finals.append(pltpu.make_async_copy(item.first, targets[kind](k), store.at[item.index]))
+            items.append(item)
+    for item in items:
+        item.begin(load, psend, precv)
+    row_load.wait()
+    row_steps, row_end = line_sum_steps(
+        z, nz, rows_parts, rows_total, up, down, lsend, lrecv, line_partners(here, nz), LINE_PIECES
+    )
+
+    def stage(t):
+        if t < len(items):
+            items[t].after_core(load, psend, precv)
+        if 0 <= t - SUM_LAG < len(items):
+            items[t - SUM_LAG].after_second(psend, precv)
+        if 0 <= t - 2 * SUM_LAG < len(items):
+            items[t - 2 * SUM_LAG].after_first(psend, precv)
+            finals[t - 2 * SUM_LAG].start()
+
+    steps = [functools.partial(stage, t) for t in range(len(items) + 2 * SUM_LAG)]
+    for step in steps[:2]:
+        step()
+    steps = steps[2:]
+    arrive()
+    keep.wait()
+
+    my_batch, my_head = unit_owner(me, batches, heads, count)
+    limit = prefix[my_batch, 0]
+    inv = 1.0 / math.sqrt(HEAD_DIM)
+
+    def head_rows(source, head):
+        _, first_head = unit_owner(source, batches, heads, count)
+        return pl.ds(pl.multiple_of((first_head + head) * HEAD_DIM, HEAD_DIM), HEAD_DIM)
+
+    def grads_copy(head):
+        def copy(number, source, device):
+            batch, _ = unit_owner(source, batches, heads, count)
+            return remote(
+                result.at[:, pl.ds(head * HEAD_DIM, HEAD_DIM), columns(number)],
+                grads.at[:, batch, head_rows(source, head), :],
+                csend.at[head, number],
+                crecv.at[head, source],
+                (*device, x, c),
+            )
+
+        return copy
+
+    def attend(head):
+        part = pl.ds(head * HEAD_DIM, HEAD_DIM)
+        dkey[...] = jnp.zeros_like(dkey)
+        dvalue[...] = jnp.zeros_like(dvalue)
+        for first, tile, mask_from, keys in tile_spans(length):
+            here_q, upto = pl.ds(first, tile), pl.ds(0, keys)
+            queries = units[0, part, here_q] * bf16(inv)
+            key, value, out_grad = units[1, part, upto], units[2, part, upto], grad[part, here_q]
+            scores = dot(key, queries, ((0,), (0,)))
+            probs = jnp.exp(scores - lse[head, :, here_q])
+            probs = masked(probs, first, tile, mask_from, keys, limit, 0.0)
+            prob_grad = dot(value, out_grad, ((0,), (0,)))
+            delta = jnp.sum(probs * prob_grad, axis=0, keepdims=True)
+            score_grad = (probs * (prob_grad - delta)).astype(bf16)
+            result[0, part, here_q] = (dot(key, score_grad, ((1,), (0,))) * inv).astype(bf16)
+            dkey[:, upto] += dot(queries, score_grad, ((1,), (1,)))
+            dvalue[:, upto] += dot(out_grad, probs.astype(bf16), ((1,), (1,)))
+        result[1, part, :] = dkey[...].astype(bf16)
+        result[2, part, :] = dvalue[...].astype(bf16)
+
+    exchanges = [exchange(me, n_dp, grads_copy(head)) for head in range(count)]
+    own_copies = [
+        pltpu.make_async_copy(
+            result.at[:, pl.ds(head * HEAD_DIM, HEAD_DIM), columns(me)],
+            grads.at[:, my_batch, head_rows(me, head), :],
+            local.at[1 + head],
+        )
+        for head in range(count)
+    ]
+    for head in range(count):
+        attend(head)
+        exchanges[head][0]()
+        own_copies[head].start()
+        for step in steps[:3]:
+            step()
+        steps = steps[3:]
+        for step in row_steps[:LINE_PIECES]:
+            step()
+        row_steps = row_steps[LINE_PIECES:]
+    for step in steps + row_steps:
+        step()
+    row_end()
+    for head in range(count):
+        exchanges[head][1]()
+        own_copies[head].wait()
+    for item in items:
+        item.end(psend, precv)
+    for final in finals:
+        final.wait()
+    end()
+    for head in range(count):
+        exchanges[head][2]()
+
+
+def backward_fast(prefix, grad, saved, egu, sgu, ed, sd, rows):
+    nz = lax.axis_size("z")
+    n_dp = nz * 2
+    units, lse = saved
+    batches, width, count_rows = grad.shape
+    span, length = units.shape[1:]
+    count = span // HEAD_DIM
+    wide = egu.shape[-1]
+    arrays = {
+        "ed": ed.reshape(4, 2, -1, ed.shape[-1]),
+        "egu": egu.reshape(4, nz * 2, -1, wide),
+        "sgu": sgu.reshape(nz * 8, -1, wide),
+        "sd": sd.reshape(8, -1, sd.shape[-1]),
+    }
+    kinds = tuple(arrays)
+    rows = rows.reshape(nz, -1, rows.shape[-1])
+    any_space, vmem = pl.BlockSpec(memory_space=pl.ANY), pl.BlockSpec(memory_space=pltpu.VMEM)
+    block = {kind: arrays[kind].shape[-2:] for kind in kinds}
+    number_of = {"egu": nz, "sgu": nz, "ed": 2, "sd": 1}
+    wholes = {"ed": block["ed"], "sd": block["sd"], "egu": (nz, *block["egu"]), "sgu": (nz, *block["sgu"])}
+    block["ed"] = (block["ed"][0] // 2, block["ed"][1])
+    results = [((3, batches, width, count_rows), bf16)] + [(wholes[kind], bf16) for kind in kinds]
+    results += [(rows.shape[1:], f32)]
+    scratch = [
+        pltpu.VMEM((span, length), bf16),
+        pltpu.VMEM((HEAD_DIM, length), f32),
+        pltpu.VMEM((HEAD_DIM, length), f32),
+        pltpu.VMEM((3, span, length), bf16),
+    ]
+    items = sum(number_of.values())
+    for kind in kinds:
+        n = number_of[kind]
+        scratch += [pltpu.VMEM((n, 4, *block[kind]), bf16), pltpu.VMEM((n, 4, *block[kind]), bf16)]
+        scratch += [pltpu.VMEM((n, 2, *block[kind]), bf16), pltpu.VMEM((n, *block[kind]), bf16)]
+    dma = pltpu.SemaphoreType.DMA
+    scratch += [dma((1 + count,)), dma((n_dp,)), dma((n_dp,)), dma((count, n_dp)), dma((count, n_dp))]
+    scratch += [dma((items, 4)), dma((items, 7)), dma((items, 7)), dma((items,))]
+    line = dma((2, nz, LINE_PIECES))
+    scratch += [pltpu.VMEM(rows.shape, bf16)] * 3 + [dma, line, line]
+    outs = pl.pallas_call(
+        functools.partial(backward_kernel, nz, kinds),
+        out_shape=[jax.ShapeDtypeStruct(*result) for result in results],
+        in_specs=[pl.BlockSpec(memory_space=pltpu.SMEM), any_space, vmem, vmem] + [any_space] * 5,
+        out_specs=[any_space] * 5 + [vmem],
+        scratch_shapes=scratch,
+        compiler_params=params(5, 56 << 20),
+        name="attend_backward",
+    )(prefix, grad, units, lse, *arrays.values(), rows)
+    grads, ed, egu, sgu, sd, total = outs
+    return grads, (egu, sgu, ed, sd), total
+
+
+def last_kernel(nz, *refs):
+    attn_in, egu_in, sgu_in, attn, egu, sgu, own, sib, second, first, zbuf = refs[:11]
+    local, load, zsend, zrecv, psend, precv, store = refs[11:]
+    here = position()
+    z, y, x, c = here
+    line = [lax.rem(z + d, nz) for d in range(nz)]
+    greet([(line[d], y, x, c) for d in range(1, nz)] + [(z, 1 - y, x, c), (z, y, 1 - x, c), (z, y, x, 1 - c)])
+    items = []
+    for d in (3, 2, 1, 0) if nz == 4 else range(nz - 1, -1, -1):
+        place = lambda py, px, pc, zs=line[d]: attn_in.at[((zs * 2 + py) * 2 + px) * 2 + pc]
+        items.append((d, SumItem(here, d, place, (own.at[d], sib.at[d], second.at[d], first.at[d]), d % 2 == 1)))
+    for _, item in items:
+        item.begin(load, psend, precv)
+
+    def line_copy(kind, d, arriving=False):
+        to, frm = line[d], line[(nz - d) % nz]
+        at = frm if arriving else z
+        dst = (zbuf, egu, sgu)[kind].at[at]
+        src = dst if arriving else (first.at[d], egu_in.at[to], sgu_in.at[to])[kind]
+        return remote(src, dst, zsend.at[kind, d], zrecv.at[kind, d], (to, y, x, c))
+
+    for kind in (1, 2):
+        for d in range(1, nz):
+            line_copy(kind, d).start()
+    keeps = [pltpu.make_async_copy(src.at[z], dst.at[z], local.at[i]) for i, (src, dst) in enumerate(((egu_in, egu), (sgu_in, sgu)))]
+    for copy in keeps:
+        copy.start()
+    mine = pltpu.make_async_copy(first.at[0], zbuf.at[z], store)
+    for _, item in items:
+        item.after_core(load, psend, precv)
+    for _, item in items:
+        item.after_second(psend, precv)
+    for d, item in items:
+        item.after_first(psend, precv)
+        if d == 0:
+            mine.start()
+        else:
+            line_copy(0, d).start()
+    mine.wait()
+    for kind in range(3):
+        for d in range(1, nz):
+            line_copy(kind, d, True).wait_recv()
+    columns = attn.shape[1] // 5
+
+    @pl.loop(0, 5)
+    def _(i):
+        part = pl.ds(pl.multiple_of(i * columns, 128), columns)
+        attn[:, part] = sum(zbuf[k, :, part].astype(f32) for k in range(nz))
+
+    for _, item in items:
+        item.end(psend, precv)
+    for kind in range(3):
+        for d in range(1, nz):
+            line_copy(kind, d).wait_send()
+    for copy in keeps:
+        copy.wait()
+
+
+def last_fast(attn, egu, sgu):
+    nz = lax.axis_size("z")
+    dma = pltpu.SemaphoreType.DMA
+    attn = attn.reshape(nz * 8, -1, attn.shape[-1])
+    block = attn.shape[1:]
+    any_space = pl.BlockSpec(memory_space=pl.ANY)
+    return pl.pallas_call(
+        functools.partial(last_kernel, nz),
+        out_shape=[
+            jax.ShapeDtypeStruct(block, f32),
+            jax.ShapeDtypeStruct(egu.shape, bf16),
+            jax.ShapeDtypeStruct(sgu.shape, bf16),
+        ],
+        in_specs=any_specs(3),
+        out_specs=[pl.BlockSpec(memory_space=pltpu.VMEM), any_space, any_space],
+        scratch_shapes=[
+            pltpu.VMEM((nz, 4, *block), bf16),
+            pltpu.VMEM((nz, 4, *block), bf16),
+            pltpu.VMEM((nz, 2, *block), bf16),
+            pltpu.VMEM((nz, *block), bf16),
+            pltpu.VMEM((nz, *block), bf16),
+            dma((2,)),
+            dma((nz, 4)),
+            dma((3, nz)),
+            dma((3, nz)),
+            dma((nz, 7)),
+            dma((nz, 7)),
+            dma,
+        ],
+        compiler_params=params(3, 32 << 20),
+        name="last",
+    )(attn, egu, sgu)
 
 
 def visible_units(prefix, heads, here, length):
@@ -206,11 +1185,12 @@
     cot_routes = jnp.concatenate(
         [cot, pair_ids.astype(bf16), jnp.zeros((count, MISC - TOP_K), bf16)], axis=1
     )
-    attn_full = gather_all(attn_shard)
-    egu, sgu, ed, sd = gather_weights(
-        slices(expert_gate[0], expert_up[0]), slices(shared_gate, shared_up), expert_down[0], shared_down
-    )
-    cot_line = gather_line(cot_routes)
+    parts = (slices(expert_gate[0], expert_up[0]), slices(shared_gate, shared_up), expert_down[0], shared_down)
+    fast = paired(batches, heads)
+    if fast:
+        attn_full, *lined = first_fast(attn_shard, *parts[:2])
+    else:
+        attn_full = gather_all(attn_shard)
 
     w_qkv = attn_full[:, : 3 * width]
     w_out = attn_full[:, 3 * width : 4 * width]
@@ -229,14 +1209,19 @@
     turned = rotate_t(projected[: 2 * width], cosine, sine, 1.0)
     qkv = jnp.concatenate([turned, projected[2 * width :]], axis=0).astype(bf16)
     qkv = jnp.transpose(qkv.reshape(3, width, batches, rows), (0, 2, 1, 3))
-    context, saved = attention_forward(qkv, batches, heads, prefix)
+    if fast:
+        context, saved, ffn, cot_line = attend_fast(prefix, qkv, *lined, *parts[2:], cot_routes)
+    else:
+        context, saved = attention_forward(qkv, batches, heads, prefix)
+        ffn, cot_line = gather_weights(*parts), gather_line(cot_routes)
+    egu, sgu, ed, sd = ffn
     context = jnp.transpose(context, (1, 0, 2)).reshape(width, count)
     attended = x_in + dot(context, w_out, ((0,), (0,)))
     ffn_scale = rms_scale(attended)
     ffn_norm = attended * ffn_scale
     mixed = (ffn_norm * gain_ffn).astype(bf16)
 
-    mixed_line = gather_line(mixed)
+    mixed_line = (gather_line_fast if fast else gather_line)(mixed)
     cot_rows = cot_line[:, :width]
     ids = cot_line[:, width : width + TOP_K].astype(jnp.int32)
     lines = mixed_line.shape[0]
@@ -309,9 +1294,7 @@
     mixed_part = jnp.concatenate(
         [mixed_part.astype(bf16), pair_dot.astype(bf16), jnp.zeros((lines, MISC - TOP_K), bf16)], axis=1
     )
-    mixed_sum = sum_line(mixed_part).astype(f32)
-    out_sum = sum_line(out_part).astype(f32)
-    block_rows = (attended + out_sum).astype(bf16)
+    mixed_sum = (sum_line_fast if fast else sum_line)(mixed_part).astype(f32)
 
     hot, probs = gates(mixed, pair_ids)
     gate_grads = mixed_sum[:, width : width + TOP_K]
@@ -328,7 +1311,13 @@
     context_grad = dot(w_out, out_grad, ((1,), (1,))).astype(bf16)
     context_grad = jnp.transpose(context_grad.reshape(width, batches, rows), (1, 0, 2))
 
-    rot_grad = attention_backward(context_grad, saved, batches, heads, prefix)
+    ffn_grads = (grad_egu, grad_sgu, grad_ed, grad_sd)
+    if fast:
+        rot_grad, (*lined, ed_sum, sd_sum), out_sum = backward_fast(prefix, context_grad, saved, *ffn_grads, out_part)
+    else:
+        rot_grad = attention_backward(context_grad, saved, batches, heads, prefix)
+        egu_sum, sgu_sum, ed_sum, sd_sum = sum_weights(*ffn_grads)
+        out_sum = sum_line(out_part)
     rot_grad = jnp.transpose(rot_grad, (0, 2, 1, 3)).reshape(3 * width, count).astype(f32)
     turned = rotate_t(rot_grad[: 2 * width], cosine, sine, -1.0)
     qkv_grad = jnp.concatenate([turned, rot_grad[2 * width :]], axis=0).astype(bf16)
@@ -344,8 +1333,12 @@
         [grad_router, grad_gattn[:, None], grad_gffn[:, None], jnp.zeros((width, MISC - experts - 2), f32)], axis=1
     )
     attn_parts = jnp.concatenate([grad_wqkv, grad_wout, grad_misc], axis=1).astype(bf16)
-    attn_sums = sum_all(attn_parts).astype(f32)
-    egu_sum, sgu_sum, ed_sum, sd_sum = sum_weights(grad_egu, grad_sgu, grad_ed, grad_sd)
+    if fast:
+        attn_sums, egu_sum, sgu_sum = last_fast(attn_parts, *lined)
+    else:
+        attn_sums = sum_all(attn_parts)
+    attn_sums = attn_sums.astype(f32)
+    block_rows = (attended + out_sum.astype(f32)).astype(bf16)
 
     def joined(blocks):
         both = jnp.transpose(blocks.reshape(nz, -1, 2, slice_ff), (2, 1, 0, 3)).astype(f32)

time: 776 us -> 543 us (0.70)
  waiting for transfers between devices: 384 us -> 0 us
  Pallas kernels: 0 us -> 315 us
  blocking collectives: 82.1 us -> 0 us
  matrix products: 120 us -> 102 us
  starting transfers between devices: 17.5 us -> 0 us
  other arithmetic: 51.7 us -> 34.5 us
  between operations: 15.5 us -> 2.04 us
  local copies, waits for them, and re-layouts: 96.6 us -> 84 us
    pallas_call x0 -> x6, Pallas kernels: none -> 315 us  [the longest x1 87.9 us: backward_fast(): pl.pallas_call(functools.partial(backward_kernel, nz, kinds), out_shape=[...]
    reduce_scatter x6 -> x0, waiting for transfers between devices: 108 us -> none  [the longest x1 44.9 us: sum_weights(): ed = lax.psum_scatter(ed, PLANE, scatter_dimension=0, tiled=True)[0]]
    unnamed x14 -> x0, waiting for transfers between devices: 99.5 us -> none
    all_gather x6 -> x0, waiting for transfers between devices: 96.7 us -> none  [the longest x2 43.5 us: spread(): lax.all_gather(mine, PLANE, axis=0).reshape(ny, ne, nz, *blocks.shape[1:])]
    all_to_all x4 -> x0, waiting for transfers between devices: 79.7 us -> none  [the longest x2 55.6 us: to_units(): units = lax.all_to_all(units, DP, 0, 0, tiled=True)]
    all_to_all x4 -> x0, blocking collectives: 70.3 us -> none  [the longest x2 44.1 us: spread(): mine = lax.all_to_all(blocks, 'z', 0, 0, tiled=True)]
    dot_general x30 -> x24, matrix products: 117 us -> 97.8 us  [dot(): return lax.dot_general(a, b, (dims, batch), preferred_element_type=f32)]
    reshape x8 -> x1, local copies, waits for them, and re-layouts: 17.1 us -> 1.04 us  [shards(): pair_ids = routes.reshape(count, TOP_K)]
  transfers between devices with their start and end apart: 17 -> 0, of which waited for: 12 -> 0; matrix products, arithmetic and copies ran while one was open for 24% -> 0% of each run, Pallas kernels for 0% -> 0%
where the time goes in v3:
time: 543 us; the launch traced here: 537 us
  Pallas kernels  315 us (58%)
  matrix products  102 us (19%)
  local copies, waits for them, and re-layouts  84 us (15%)
  other arithmetic  34.5 us (6%)
    dot_general x24, matrix products, dot(): return lax.dot_general(a, b, (dims, batch), preferred_element_type=f32)  97.8 us
    pallas_call x1, Pallas kernels, backward_fast(): pl.pallas_call(functools.partial(backward_kernel, nz, kinds), out_shape=[...  87.9 us
    pallas_call x1, Pallas kernels, attend_fast(): pl.pallas_call(functools.partial(attend_kernel, nz), out_shape=[jax.Shape...  77.5 us
    pallas_call x1, Pallas kernels, last_fast(): pl.pallas_call(functools.partial(last_kernel, nz), out_shape=[jax.ShapeDt...  47.5 us
    pallas_call x1, Pallas kernels, first_fast(): pl.pallas_call(functools.partial(first_kernel, nz), out_shape=[jax.ShapeD...  40.6 us
    pallas_call x1, Pallas kernels, sum_line_fast(): pl.pallas_call(functools.partial(line_sum_kernel, nz), out_shape=jax.Shap...  34.1 us
    pallas_call x1, Pallas kernels, gather_line_fast(): pl.pallas_call(functools.partial(line_gather_kernel, nz), out_shape=jax.S...  27.6 us
    unnamed x140, local copies, waits for them, and re-layouts  24.1 us

profile of v3, /device:TPU:0, one launch (start us, length us, event | category | flops | bytes accessed | tf_op | source)
XLA Modules:
  0.0 537.4 jit_solution(17364400047593712292)
XLA Ops:
  11.7 40.6 %first.1 = (bf16[32,24,3200]{2,1,0:T(8,128)(2,1)S(1)}, bf16[4,96,1024]{2,1,0:T(8,128)(2,1)S(1)}, bf16[4,24,1024]{2,1,0:T(8,128)(2,1)S(1)}) custom-call(bf16[24,3200]{1,0:T(8,128)(2,1)S(1)} %concatenate.34.refs_0_, bf16[4,96,1024]{2,1,0:T(8,128)(2,1)S(1)} %bitcast.191, bf16[4,24,1024]{2,1,0:T(8,128)(2,1)S(1)} %bitcast.200), custom_call_target="tpu_custom_call" | custom-call | tf_op jit(solution)/shard_map/first/pallas_call | solution.py:787
  57.5 3.3 fusion.7
  66.9 77.5 %attend.1 = (bf16[2,768,128]{2,1,0:T(8,128)(2,1)S(1)}, bf16[3,192,1024]{2,1,0:T(8,128)(2,1)S(1)}, f32[3,1,1024]{2,1,0:T(1,128)S(1)}, bf16[4,8,96,1024]{3,2,1,0:T...) custom-call(s32[2,1]{1,0:T(2,128)S(1)} %copy.296.refs_0_, ...), custom_call_target="tpu_custom_call" | custom-call | tf_op jit(solution)/shard_map/attend/pallas_call | solution.py:688
  153.9 27.6 %gather_line.1 = bf16[4,256,768]{2,1,0:T(8,128)(2,1)S(1)} custom-call(bf16[256,768]{1,0:T(8,128)(2,1)S(1)} %multiply_convert_fusion.7.own), custom_call_target="tpu_custom_call" | custom-call | tf_op jit(solution)/shard_map/gather_line/pallas_call | solution.py:282
  203.4 10.7 %fusion.48 = f32[4,640,1024]{1,2,0:T(8,128)} fusion(bf16[4,640,768]{2,1,0:T(8,128)(2,1)} %bitcast.223, bf16[4,768,1024]{2,1,0:T(8,128)(2,1)} %bitcast.261), kind=kOutput, calls=%fused_computation.140 | convolution fusion | flops 4026531840 | bytes 20709376 | tf_op jit(solution)/shard_map/dot_general | solution.py:38
  214.2 5.2 multiply_convert_fusion.1
  219.4 5.7 %fusion.1 = (f32[4,640]{1,0:T(4,128)S(1)}, f32[4,640,768]{2,1,0:T(8,128)}) fusion(f32[4,8,80,768]{3,2,1,0:T(8,128)S(1)} %copy.306, bf16[4,640,512]{1,2,0:T(8,128)(2,1)S(1)} %multiply_convert_fusion.1, bf16[4,512,768]{2,1,0:T(8,128)(2,1)S(1)} %bitcast.189), kind=kOutput, calls=%fused_computation.3 | convolution fusion | flops 2017195520 | bytes 21506048 | tf_op jit(solution)/shard_map/dot_general | solution.py:38
  226.6 8.2 %multiply_convert_fusion = (bf16[4,640,768]{2,1,0:T(8,128)(2,1)}, bf16[4,640,768]{2,1,0:T(8,128)(2,1)S(1)}) fusion(f32[4,640,768]{2,1,0:T(8,128)} %get-tuple-element.180, f32[4,640]{1,0:T(4,128)S(1)} %mul.347, f32[4,8,80,768]{3,2,1,0:T(8,128)} %copy-done.27), kind=kLoop, calls=%fused_computation.4 | loop fusion | flops 7864320 | bytes 23603200 | tf_op jit(solution)/shard_map/convert_element_type | solution.py:1279
  234.8 9.5 %multiply_convert_fusion.3 = (bf16[4,640,512]{1,2,0:T(8,128)(2,1)}, bf16[4,640,512]{1,2,0:T(8,128)(2,1)}) fusion(f32[4,640,1024]{1,2,0:T(8,128)} %fusion.48, bf16[4,640,768]{2,1,0:T(8,128)(2,1)S(1)} %get-tuple-element.173, bf16[4,512,768]{2,1,0:T(8,128)(2,1)S(1)} %bitcast.190), kind=kOutput, calls=%fused_computation.8 | convolution fusion | flops 2030305280 | bytes 22806528 | tf_op jit(solution)/shard_map/dot_general | solution.py:38
  244.3 10.9 %fusion.12 = bf16[4,640,768]{2,1,0:T(8,128)(2,1)} fusion(bf16[4,768,1024]{2,1,0:T(8,128)(2,1)} %bitcast.262, bf16[4,640,512]{1,2,0:T(8,128)(2,1)} %get-tuple-element.154, bf16[4,640,512]{1,2,0:T(8,128)(2,1)} %get-tuple-element.153), kind=kOutput, calls=%fused_computation.27 | convolution fusion | flops 4038983680 | bytes 15466496 | tf_op jit(solution)/shard_map/dot_general | solution.py:38
  260.4 3.9 copy.315
  264.3 3.4 fusion.50
  267.7 2.7 multiply_convert_fusion.6
  273.9 3.1 copy.318
  277.0 34.1 %sum_line.1 = f32[256,896]{1,0:T(8,128)S(1)} custom-call(bf16[4,256,896]{2,1,0:T(8,128)(2,1)S(1)} %bitcast.187), custom_call_target="tpu_custom_call" | custom-call | tf_op jit(solution)/shard_map/sum_line/pallas_call | solution.py:365
  316.8 2.7 multiply_reduce_fusion
  322.5 7.2 %convolution_convert_fusion.3 = bf16[4,512,768]{2,1,0:T(8,128)(2,1)} fusion(bf16[4,640,512]{1,2,0:T(8,128)(2,1)} %copy-done.34, bf16[4,640,768]{2,1,0:T(8,128)(2,1)} %copy-done.36), kind=kOutput, calls=%fused_computation.30 | convolution fusion | flops 2014838784 | bytes 9699328 | tf_op jit(solution)/shard_map/dot_general | solution.py:38
  329.8 11.7 %convolution_convert_fusion.1 = bf16[4,768,1024]{2,1,0:T(8,128)(2,1)} fusion(bf16[4,640,768]{2,1,0:T(8,128)(2,1)} %bitcast.224, bf16[4,640,512]{1,2,0:T(8,128)(2,1)} %get-tuple-element.154, bf16[4,640,512]{1,2,0:T(8,128)(2,1)} %get-tuple-element.153), kind=kOutput, calls=%fused_computation.12 | convolution fusion | flops 4040163328 | bytes 15466496 | tf_op jit(solution)/shard_map/dot_general | solution.py:38
  341.5 4.7 convolution_convert_fusion.4
  353.0 87.9 %attend_backward.1 = (bf16[3,2,768,128]{3,2,1,0:T(8,128)(2,1)}, bf16[256,768]{1,0:T(8,128)(2,1)}, bf16[4,96,1024]{2,1,0:T(8,128)(2,1)}, bf16[4,24,1024]{2,1,0:T(...) custom-call(s32[2,1]{1,0:T(2,128)} %copy-done.24, bf16[2,768,128]{2,1,0:T(8,128)(2,1)} %bitcast.238, ...), custom_call_target="tpu_custom_call" | custom-call | tf_op jit(solution)/shard_map/attend_backward/pallas_call | solution.py:1002
  452.5 3.9 multiply_reduce_fusion.1
  457.6 3.9 convolution_convert_fusion
  466.2 8.3 %concatenate.43.refs_0_ = bf16[32,24,3200]{2,1,0:T(8,128)(2,1)} concatenate(bf16[32,24,2304]{2,1,0:T(8,128)(2,1)} %convolution_convert_fusion, bf16[32,24,768]{2,1,0:T(8,128)(2,1)S(1)} %copy-done.35, bf16[32,24,4]{2,1,0:T(8,128)(2,1)S(1)} %copy.336, bf16[32,24,1]{2,1,0:T(8,128)(2,1)S(1)} %concatenate.44, bf16[32,24,1]{2,1,0:T(8,128)(2,1)S(1)} %concatenate.45, ...), dimensions={2} | concatenate | bytes 9830400 | tf_op jit(solution)/shard_map/concatenate | solution.py:1335
  476.9 47.5 %last.1 = (f32[24,3200]{1,0:T(8,128)S(1)}, bf16[4,96,1024]{2,1,0:T(8,128)(2,1)S(1)}, bf16[4,24,1024]{2,1,0:T(8,128)(2,1)S(1)}) custom-call(bf16[32,24,3200]{2,1,0:T(8,128)(2,1)S(1)} %copy-done, bf16[4,96,1024]{2,1,0:T(8,128)(2,1)S(1)} %copy-done.16, bf16[4,24,1024]{2,1,0:T(8,128)(2,1)S(1)} %copy-done.18), custom_call_target="tpu_custom_call" | custom-call | tf_op jit(solution)/shard_map/last/pallas_call | solution.py:1079
  (279 shorter events, 111.1 us)
Async XLA Ops:
  1.4 62.4 %copy-start.24 = (s32[2,1]{1,0:T(2,128)}, s32[2,1]{1,0:T(2,128)S(1)}, u32[]{:S(2)}) copy-start(s32[2,1]{1,0:T(2,128)S(1)} %copy.296.refs_0_) | copy-start | bytes 28
  6.5 4.2 copy-start.50
  6.5 4.4 copy-start.51
  10.1 47.0 %copy-start.37 = (bf16[2,1,128,768]{3,2,1,0:T(8,128)(2,1)S(1)}, bf16[2,1,128,768]{3,2,1,0:T(8,128)(2,1)}, u32[]{:S(2)}) copy-start(bf16[2,1,128,768]{3,2,1,0:T(8,128)(2,1)} %param.17) | copy-start | bytes 1179652
  63.7 89.1 %copy-start.56 = (bf16[896]{0:T(1024)(128)(2,1)}, bf16[896]{0:T(1024)(128)(2,1)S(1)}, u32[]{:S(2)}) copy-start(bf16[896]{0:T(1024)(128)(2,1)S(1)} %pad.13.clone) | copy-start | bytes 5380
  149.8 117.9 %copy-start.6 = (bf16[4,256,896]{2,1,0:T(8,128)(2,1)}, bf16[4,256,896]{2,1,0:T(8,128)(2,1)S(1)}, u32[]{:S(2)}) copy-start(bf16[4,256,896]{2,1,0:T(8,128)(2,1)S(1)} %get-tuple-element.39) | copy-start | bytes 5505028
  152.9 32.6 %copy-start.54 = (f32[256]{0:T(256)}, f32[256]{0:T(256)S(1)}, u32[]{:S(2)}) copy-start(f32[256]{0:T(256)S(1)} %add_rsqrt_fusion) | copy-start | bytes 3076
  199.6 19.8 %copy-start.27 = (f32[4,8,80,768]{3,2,1,0:T(8,128)}, f32[4,8,80,768]{3,2,1,0:T(8,128)S(1)}, u32[]{:S(2)}) copy-start(f32[4,8,80,768]{3,2,1,0:T(8,128)S(1)} %copy.306) | copy-start | bytes 23592964
  214.2 5.2 copy-start.4
  219.3 5.8 %copy-start.34 = (bf16[4,640,512]{1,2,0:T(8,128)(2,1)}, bf16[4,640,512]{1,2,0:T(8,128)(2,1)S(1)}, u32[]{:S(2)}) copy-start(bf16[4,640,512]{1,2,0:T(8,128)(2,1)S(1)} %multiply_convert_fusion.1) | copy-start | bytes 7864324
  219.4 5.9 %copy-start.53 = (f32[8,128,2]{1,2,0:T(2,128)S(1)}, f32[8,128,2]{1,2,0:T(2,128)}, u32[]{:S(2)}) copy-start(f32[8,128,2]{1,2,0:T(2,128)} %copy.308) | copy-start | bytes 24580
  226.6 8.2 %copy-start.5 = (bf16[4,2,256,768]{3,2,1,0:T(8,128)(2,1)S(1)}, bf16[4,2,256,768]{3,2,1,0:T(8,128)(2,1)}, u32[]{:S(2)}) copy-start(bf16[4,2,256,768]{3,2,1,0:T(8,128)(2,1)} %copy-done.3) | copy-start | bytes 9437188
  234.8 9.5 %copy-start.36 = (bf16[4,640,768]{2,1,0:T(8,128)(2,1)}, bf16[4,640,768]{2,1,0:T(8,128)(2,1)S(1)}, u32[]{:S(2)}) copy-start(bf16[4,640,768]{2,1,0:T(8,128)(2,1)S(1)} %get-tuple-element.173) | copy-start | bytes 11796484
  273.9 42.9 %copy-start.55 = (f32[256]{0:T(256)S(1)}, f32[256]{0:T(256)}, u32[]{:S(2)}) copy-start(f32[256]{0:T(256)} %copy-done.54) | copy-start | bytes 3076
  312.1 7.5 %copy-start.29 = (f32[256,768]{1,0:T(8,128)S(1)}, f32[256,768]{1,0:T(8,128)}, u32[]{:S(2)}) copy-start(f32[256,768]{1,0:T(8,128)} %copy-done.28) | copy-start | bytes 2359300
  312.1 7.5 %copy-start.41 = (bf16[2,1,128,768]{3,2,1,0:T(8,128)(2,1)S(1)}, bf16[2,1,128,768]{3,2,1,0:T(8,128)(2,1)}, u32[]{:S(2)}) copy-start(bf16[2,1,128,768]{3,2,1,0:T(8,128)(2,1)} %param.20) | copy-start | bytes 1179652
  341.5 4.7 copy-start.7
  341.5 4.7 copy-start.46
  452.4 4.9 copy-start.43
  457.4 4.1 copy-start.9
  461.5 3.9 copy-start.62
  466.2 8.3 %copy-start.16 = (bf16[4,96,1024]{2,1,0:T(8,128)(2,1)S(1)}, bf16[4,96,1024]{2,1,0:T(8,128)(2,1)}, u32[]{:S(2)}) copy-start(bf16[4,96,1024]{2,1,0:T(8,128)(2,1)} %get-tuple-element.48.refs_1_) | copy-start | bytes 2359300
  466.2 8.3 %copy-start.18 = (bf16[4,24,1024]{2,1,0:T(8,128)(2,1)S(1)}, bf16[4,24,1024]{2,1,0:T(8,128)(2,1)}, u32[]{:S(2)}) copy-start(bf16[4,24,1024]{2,1,0:T(8,128)(2,1)} %get-tuple-element.49.refs_2_) | copy-start | bytes 589828
  524.4 4.5 copy-start.52
  (41 other events, 75.2 us)

commit v4 on v3

--- a/solution.py
+++ b/solution.py
@@ -80,7 +80,7 @@
     n_dp = lax.axis_size(DP)
     here = batches * heads // n_dp
     even = here * n_dp == batches * heads and heads % max(1, here) == 0
-    return even and tuple(lax.axis_size(name) for name in PLANE) == (2, 2, 2)
+    return even and tuple(lax.axis_size(name) for name in ALL) == (4, 2, 2, 2)
 
 
 def sum_line(rows):
@@ -262,35 +262,6 @@
 LINE_PIECES = 2
 
 
-def line_gather_kernel(nz, own, out, local, sends, gets):
-    here = position()
-    z = here[0]
-    greet_line(here, nz)
-    start, steps, end = line_gather_steps(z, nz, own, out, sends, gets, line_partners(here, nz), LINE_PIECES)
-    start()
-    keep = pltpu.make_async_copy(own, out.at[z], local)
-    keep.start()
-    for step in steps:
-        step()
-    end()
-    keep.wait()
-
-
-def gather_line_fast(rows):
-    nz = lax.axis_size("z")
-    sems = pltpu.SemaphoreType.DMA((2, nz, LINE_PIECES))
-    out = pl.pallas_call(
-        functools.partial(line_gather_kernel, nz),
-        out_shape=jax.ShapeDtypeStruct((nz, *rows.shape), bf16),
-        in_specs=any_specs(1),
-        out_specs=pl.BlockSpec(memory_space=pl.ANY),
-        scratch_shapes=[pltpu.SemaphoreType.DMA, sems, sems],
-        compiler_params=params(1),
-        name="gather_line",
-    )(rows)
-    return out.reshape(-1, rows.shape[-1])
-
-
 def line_sum_steps(z, nz, parts, total, up, down, sends, gets, neighbour, pieces):
     rows = parts.shape[1] // pieces
     arrived = (up, down)
@@ -343,34 +314,6 @@
 
     steps = [functools.partial(step, distance, piece) for distance in range(1, nz) for piece in range(pieces)]
     return steps, end
-
-
-def line_sum_kernel(nz, parts_in, total, parts, up, down, local, sends, gets):
-    here = position()
-    z = here[0]
-    load = pltpu.make_async_copy(parts_in, parts, local)
-    load.start()
-    greet_line(here, nz)
-    steps, end = line_sum_steps(z, nz, parts, total, up, down, sends, gets, line_partners(here, nz), LINE_PIECES)
-    load.wait()
-    for step in steps:
-        step()
-    end()
-
-
-def sum_line_fast(parts):
-    nz = lax.axis_size("z")
-    parts = parts.reshape(nz, -1, parts.shape[-1])
-    sems = pltpu.SemaphoreType.DMA((2, nz, LINE_PIECES))
-    return pl.pallas_call(
-        functools.partial(line_sum_kernel, nz),
-        out_shape=jax.ShapeDtypeStruct(parts.shape[1:], f32),
-        in_specs=any_specs(1),
-        out_specs=pl.BlockSpec(memory_space=pltpu.VMEM),
-        scratch_shapes=[pltpu.VMEM(parts.shape, bf16)] * 3 + [pltpu.SemaphoreType.DMA, sems, sems],
-        compiler_params=params(2, 32 << 20),
-        name="sum_line",
-    )(parts)
 
 
 class SumItem:
@@ -1104,6 +1047,329 @@
     )(attn, egu, sgu)
 
 
+ORDER = ((0, 1, 2, 3), (1, 0, 2, 3), (2, 3, 1, 0), (3, 2, 1, 0))
+EXTRA = 16
+
+
+def by_distance(z, index):
+    code = jnp.int32(0)
+    for plane, order in enumerate(ORDER):
+        code = jnp.where(z == plane, sum(p * 4**i for i, p in enumerate(order)), code)
+    for _ in range(3):
+        code = jnp.where(index > 0, code // 4, code)
+        index = index - 1
+    return lax.rem(code, 4)
+
+
+def ffn_kernel(capacity, *refs):
+    refs = list(refs)
+    take = lambda n: [refs.pop(0) for _ in range(n)]
+    mixed_in, cot_in, router_in, *weights_in = take(7)
+    out_part, total, *grads = take(6)
+    weights = take(4)
+    egu, sgu, ed, sd = weights
+    mixed, cot, router, arrived, pair_grad, expert_hidden, act_grad, s_hidden, s_grad = take(9)
+    slot_out, slot_grad, hots, gate_dot, outs, parts, up, down, wide_stage, deep_stage = take(10)
+    local, loads, gsend, grecv, ssend, srecv, stores = take(7)
+    here = position()
+    z, y, x, c = here
+    nz = 4
+    neighbour = line_partners(here, nz)
+    experts = egu.shape[0]
+    rows, width = mixed_in.shape
+    group = 128
+    groups = rows // group
+    slots = groups * capacity
+    ff = ed.shape[1]
+
+    loading = [pltpu.make_async_copy(router_in, router, local.at[0])]
+    loading += [pltpu.make_async_copy(mixed_in, mixed.at[z], local.at[1])]
+    loading += [pltpu.make_async_copy(cot_in, cot, local.at[2])]
+    shared_loads = [
+        pltpu.make_async_copy(weights_in[1], sgu, local.at[3]),
+        pltpu.make_async_copy(weights_in[3], sd, local.at[4]),
+    ]
+    for copy in loading:
+        copy.start()
+
+    def expert_loads(e):
+        return [
+            pltpu.make_async_copy(weights_in[0].at[e], egu.at[e], loads.at[0, e]),
+            pltpu.make_async_copy(weights_in[2].at[e], ed.at[e], loads.at[1, e]),
+        ]
+
+    for e in range(experts):
+        for copy in expert_loads(e):
+            copy.start()
+    for copy in shared_loads:
+        copy.start()
+    greet_line(here, nz)
+
+    def may_send(way):
+        return z < nz - 1 if way == 0 else z > 0
+
+    def chunk_copy(way, source, src=None):
+        dst = mixed.at[source]
+        return remote(dst if src is None else src, dst, gsend.at[way, source], grecv.at[way, source], neighbour(1 - 2 * way))
+
+    for way in range(2):
+        pl.when(may_send(way))(lambda: chunk_copy(way, z, mixed_in).start())
+
+    def receive(source):
+        for way in range(2):
+
+            @pl.when(source < z if way == 0 else source > z)
+            def _():
+                chunk_copy(way, source).wait_recv()
+                pl.when(may_send(way))(lambda: chunk_copy(way, source).start())
+
+    piece_rows = (pl.ds(0, group), pl.ds(group, parts.shape[1] - group))
+    came = (up, down)
+
+    def part_copy(way, target, piece):
+        part = piece_rows[piece]
+        return remote(
+            parts.at[target, part],
+            came[way].at[target, part],
+            ssend.at[way, target, piece],
+            srecv.at[way, target, piece],
+            neighbour(1 - 2 * way),
+        )
+
+    def relay(target, piece):
+        part = piece_rows[piece]
+        for way in range(2):
+            ahead = z < target if way == 0 else z > target
+            inner = z > 0 if way == 0 else z < nz - 1
+
+            @pl.when(ahead & inner)
+            def _():
+                part_copy(way, target, piece).wait_recv()
+                mine, theirs = parts.at[target, part], came[way].at[target, part]
+                mine[...] = (mine[...].astype(f32) + theirs[...].astype(f32)).astype(bf16)
+
+            pl.when(ahead)(lambda: part_copy(way, target, piece).start())
+
+    for copy in loading:
+        copy.wait()
+
+    sub = lax.broadcasted_iota(jnp.int32, (8, group), 0).astype(f32)
+    before = lax.broadcasted_iota(jnp.int32, (group, group), 0) < lax.broadcasted_iota(jnp.int32, (group, group), 1)
+    before = jnp.where(before, 1.0, 0.0).astype(bf16)
+    slot_iota = lax.broadcasted_iota(jnp.int32, (capacity, group), 0).astype(f32)
+
+    def chunk(index, source):
+        tokens = mixed.at[source]
+        named, ranks, probs = [], [], []
+        for g in range(groups):
+            lanes = pl.ds(g * group, group)
+            ids = cot[source, pl.ds(rows, EXTRA), lanes].astype(f32)
+            hot = jnp.where((sub == ids[0:1]) | (sub == ids[1:2]), 1.0, 0.0)
+            logits = dot(router[...], mixed[source, lanes, :], ((1,), (1,)))[:8]
+            top = jnp.max(jnp.where(hot > 0, logits, neg_fill), axis=0, keepdims=True)
+            powers = jnp.where(hot > 0, jnp.exp(logits - top), 0.0)
+            probs.append(powers / jnp.sum(powers, axis=0, keepdims=True))
+            rank = dot(jnp.concatenate([hot, hot], axis=0).astype(bf16), before, ((1,), (0,)))[:8]
+            ranks.append(jnp.where(hot > 0, rank, float(group * TOP_K)))
+        gate_dot[...] = jnp.zeros_like(gate_dot)
+
+        def row_of(table, e):
+            return jnp.sum(jnp.where(sub == e.astype(f32), table, 0.0), axis=0, keepdims=True)
+
+        @pl.loop(0, experts)
+        def _(e):
+            @pl.when(index == 0)
+            def _():
+                for copy in expert_loads(e):
+                    copy.wait()
+
+            here_slots = pl.ds(pl.multiple_of(source * slots, 16), slots)
+            hot_of, prob_of, cot_of = [], [], []
+            for g in range(groups):
+                lanes = pl.ds(g * group, group)
+                hot = jnp.where(slot_iota == row_of(ranks[g], e), 1.0, 0.0)
+                prob_of.append(jnp.sum(hot * row_of(probs[g], e), axis=1, keepdims=True))
+                low_hot = hot.astype(bf16)
+                hots[g, pl.ds(pl.multiple_of(e * capacity, 16), capacity), :] = low_hot
+                hot_of.append(hot)
+                mine = pl.ds(pl.multiple_of(source * slots + g * capacity, 16), capacity)
+                arrived[e, mine, :] = dot(low_hot, mixed[source, lanes, :], ((1,), (0,))).astype(bf16)
+                picked = dot(low_hot, cot[source, lanes, :], ((1,), (0,)))
+                cot_of.append(picked)
+                pair_grad[e, mine, :] = (picked * prob_of[g]).astype(bf16)
+            act = dot(arrived[e, here_slots, :], egu[e], ((1,), (0,)))
+            hidden_grad = dot(pair_grad[e, here_slots, :], ed[e], ((1,), (1,)))
+            gate_act, up_act = act[:, :ff], act[:, ff:]
+            sig = jax.nn.sigmoid(gate_act)
+            silu = gate_act * sig
+            hidden = (silu * up_act).astype(bf16)
+            expert_hidden[e, here_slots, :] = hidden
+            gate_grad = (hidden_grad * up_act * (sig * (1.0 + gate_act * (1.0 - sig)))).astype(bf16)
+            up_grad = (hidden_grad * silu).astype(bf16)
+            act_grad[e, here_slots, pl.ds(0, ff)] = gate_grad
+            act_grad[e, here_slots, pl.ds(ff, ff)] = up_grad
+            out = dot(hidden, ed[e], ((1,), (0,)))
+            back = dot(act_grad[e, here_slots, :], egu[e], ((1,), (1,)))
+            for g in range(groups):
+                mine, stack = slice(g * capacity, (g + 1) * capacity), pl.ds(pl.multiple_of(e * capacity, 16), capacity)
+                lanes = pl.ds(g * group, group)
+                slot_out[g, stack, :] = (out[mine] * prob_of[g]).astype(bf16)
+                slot_grad[g, stack, :] = back[mine].astype(bf16)
+                dots = jnp.sum(out[mine] * cot_of[g], axis=1, keepdims=True)
+                dots = jnp.sum(hot_of[g] * dots, axis=0, keepdims=True)
+                gate_dot[:, lanes] += jnp.where(sub == e.astype(f32), dots, 0.0)
+
+        @pl.when(index == 0)
+        def _():
+            for copy in shared_loads:
+                copy.wait()
+
+        act = dot(tokens[...], sgu[...], ((1,), (0,)))
+        hidden_grad = dot(cot[source, pl.ds(0, rows), :], sd[...], ((1,), (1,)))
+        gate_act, up_act = act[:, :ff], act[:, ff:]
+        sig = jax.nn.sigmoid(gate_act)
+        silu = gate_act * sig
+        hidden = (silu * up_act).astype(bf16)
+        mine = pl.ds(pl.multiple_of(source * rows, 16), rows)
+        s_hidden[mine, :] = hidden
+        s_grad[mine, pl.ds(0, ff)] = (hidden_grad * up_act * (sig * (1.0 + gate_act * (1.0 - sig)))).astype(bf16)
+        s_grad[mine, pl.ds(ff, ff)] = (hidden_grad * silu).astype(bf16)
+        out = dot(hidden, sd[...], ((1,), (0,)))
+        back = dot(s_grad[mine, :], sgu[...], ((1,), (1,)))
+        for g in range(groups):
+            lanes = pl.ds(g * group, group)
+            span = slice(g * group, (g + 1) * group)
+            outs[source, lanes, :] = (out[span] + dot(hots[g], slot_out[g], ((0,), (0,)))).astype(bf16)
+            parts[source, lanes, :] = (back[span] + dot(hots[g], slot_grad[g], ((0,), (0,)))).astype(bf16)
+        dots = jnp.concatenate([gate_dot[...], jnp.zeros((EXTRA - 8, rows), f32)], axis=0)
+        parts[source, pl.ds(rows, EXTRA), :] = jnp.concatenate(
+            [dots, jnp.zeros((EXTRA, width - rows), f32)], axis=1
+        ).astype(bf16)
+
+    inner = (z > 0) & (z < nz - 1)
+
+    @pl.loop(0, nz)
+    def _(index):
+        source = by_distance(z, index)
+        pl.when((index == 1) | (index == 3) | ((index == 2) & jnp.logical_not(inner)))(lambda: receive(source))
+        pl.when((index == 1) & inner)(lambda: receive(by_distance(z, jnp.int32(2))))
+        chunk(index, source)
+
+        @pl.when(jnp.logical_not(inner) & (index > 0))
+        def _():
+            for piece in range(2):
+                relay(source, piece)
+
+        @pl.when(inner & (index == 3))
+        def _():
+            for piece in range(2):
+                relay(by_distance(z, jnp.int32(2)), piece)
+
+    out_copy = pltpu.make_async_copy(outs, out_part, local.at[5])
+    out_copy.start()
+    far, near = by_distance(z, jnp.int32(3)), by_distance(z, jnp.int32(1))
+
+    def stage_copies(e, slot):
+        return [
+            pltpu.make_async_copy(wide_stage.at[slot], grads[0].at[e], stores.at[0, slot]),
+            pltpu.make_async_copy(deep_stage.at[slot], grads[2].at[e], stores.at[1, slot]),
+        ]
+
+    def weight_grads(slot, rows_in, wide, hidden, deep):
+        for k in range(0, wide.shape[1], 512):
+            span = pl.ds(k, 512)
+            wide_stage[slot, :, span] = dot(rows_in[...], wide[:, span], ((0,), (0,))).astype(bf16)
+        deep_stage[slot] = dot(hidden[...], deep[...], ((0,), (0,))).astype(bf16)
+
+    @pl.loop(0, experts)
+    def _(e):
+        slot = lax.rem(e, 2)
+
+        @pl.when(e >= 2)
+        def _():
+            for copy in stage_copies(e - 2, slot):
+                copy.wait()
+
+        weight_grads(slot, arrived.at[e], act_grad.at[e], expert_hidden.at[e], pair_grad.at[e])
+        for copy in stage_copies(e, slot):
+            copy.start()
+        pl.when(inner & (e == 1))(lambda: relay(far, 0))
+        pl.when(inner & (e == 2))(lambda: relay(far, 1))
+        pl.when(inner & (e == 3))(lambda: relay(near, 0))
+
+    for copy in stage_copies(experts - 2, 0):
+        copy.wait()
+    tokens = mixed.reshape(nz * rows, width)
+    for k in range(0, 2 * ff, 512):
+        span = pl.ds(k, 512)
+        wide_stage[0, :, span] = dot(tokens[...], s_grad[:, span], ((0,), (0,))).astype(bf16)
+    cots = jnp.concatenate([cot[k, pl.ds(0, rows), :] for k in range(nz)], axis=0)
+    deep_stage[0] = dot(s_hidden[...], cots, ((0,), (0,))).astype(bf16)
+    shared_stores = [
+        pltpu.make_async_copy(wide_stage.at[0], grads[1], stores.at[0, 0]),
+        pltpu.make_async_copy(deep_stage.at[0], grads[3], stores.at[1, 0]),
+    ]
+    for copy in shared_stores:
+        copy.start()
+    pl.when(inner)(lambda: relay(near, 1))
+    total[...] = parts[z].astype(f32)
+    for way in range(2):
+
+        @pl.when(z > 0 if way == 0 else z < nz - 1)
+        def _():
+            for piece in range(2):
+                part_copy(way, z, piece).wait_recv()
+            total[...] += came[way][z].astype(f32)
+
+    for copy in stage_copies(experts - 1, 1) + shared_stores + [out_copy]:
+        copy.wait()
+    for way in range(2):
+        for plane in range(nz):
+            sent = (plane <= z if way == 0 else plane >= z) & may_send(way)
+            pl.when(sent)(lambda: chunk_copy(way, plane).wait_send())
+
+            @pl.when(z < plane if way == 0 else z > plane)
+            def _():
+                for piece in range(2):
+                    part_copy(way, plane, piece).wait_send()
+
+
+def ffn_fast(mixed, cot, router, weights, capacity):
+    nz = lax.axis_size("z")
+    egu, sgu, ed, sd = weights
+    rows, width = mixed.shape
+    experts, ff = ed.shape[:2]
+    cot = cot.reshape(nz, -1, width)
+    slots = nz * rows // 128 * capacity
+    groups = rows // 128
+    vmem, dma = pltpu.VMEM, pltpu.SemaphoreType.DMA
+    low = lambda *shape: vmem(shape, bf16)
+    scratch = [low(*w.shape) for w in weights]
+    scratch += [low(nz, rows, width), low(*cot.shape), low(*router.shape)]
+    scratch += [low(experts, slots, width), low(experts, slots, width)]
+    scratch += [low(experts, slots, ff), low(experts, slots, 2 * ff), low(nz * rows, ff), low(nz * rows, 2 * ff)]
+    stack = experts * capacity
+    scratch += [low(groups, stack, width), low(groups, stack, width), low(groups, stack, 128), vmem((8, rows), f32)]
+    scratch += [low(nz, rows, width)] + [low(*cot.shape)] * 3
+    scratch += [low(2, width, 2 * ff), low(2, ff, width)]
+    scratch += [dma((6,)), dma((2, experts)), dma((2, nz)), dma((2, nz)), dma((2, nz, 2)), dma((2, nz, 2)), dma((2, 2))]
+    any_space = pl.BlockSpec(memory_space=pl.ANY)
+    out_part, total, *grads = pl.pallas_call(
+        functools.partial(ffn_kernel, capacity),
+        out_shape=[
+            jax.ShapeDtypeStruct((nz, rows, width), bf16),
+            jax.ShapeDtypeStruct((rows + EXTRA, width), f32),
+        ]
+        + [jax.ShapeDtypeStruct(w.shape, bf16) for w in weights],
+        in_specs=any_specs(7),
+        out_specs=[any_space, pl.BlockSpec(memory_space=pltpu.VMEM)] + [any_space] * 4,
+        scratch_shapes=scratch,
+        compiler_params=params(1, 60 << 20),
+        name="feed_forward",
+    )(mixed, cot, router, *weights)
+    return out_part, total, grads
+
+
 def visible_units(prefix, heads, here, length):
     unit = lax.axis_index(DP) * here + jnp.arange(here)
     lengths = prefix[jnp.minimum(unit // heads, prefix.shape[0] - 1), 0]
@@ -1141,6 +1407,89 @@
     dk = dot(q, score_grad, ((2,), (1,)), ((0,), (0,))) * inv
     dv = dot(grad, probs.astype(bf16), ((2,), (1,)), ((0,), (0,)))
     return from_units(jnp.stack([dq, dk, dv], axis=1).astype(bf16), batches, heads)
+
+
+def gates(mixed_rows, pair_ids, router_w):
+    hot = (pair_ids[..., None] == jnp.arange(router_w.shape[1], dtype=jnp.int32)).astype(f32)
+    logits = dot(mixed_rows, router_w, ((1,), (0,)))
+    return hot, jax.nn.softmax(jnp.sum(hot * logits[:, None, :], axis=-1), axis=-1)
+
+
+def ffn_plain(mixed, cot_line, router_w, weights, capacity, rows):
+    nz, (count, width), experts = lax.axis_size("z"), mixed.shape, router_w.shape[1]
+    egu, sgu, ed, sd = weights
+    slice_ff = sd.shape[0]
+    cot_line = cot_line.reshape(nz, -1, width)
+    mixed_line = gather_line(mixed)
+    cot_rows = cot_line[:, :count].reshape(nz * count, width)
+    ids = jnp.transpose(cot_line[:, count : count + TOP_K, :count], (0, 2, 1)).reshape(-1, TOP_K).astype(jnp.int32)
+    lines = mixed_line.shape[0]
+    groups = lines // rows
+
+    hot, probs = gates(mixed_line, ids, router_w)
+    hot_int = hot.astype(jnp.int32).reshape(groups, rows * TOP_K, experts)
+    earlier = jnp.cumsum(hot_int, axis=1) - hot_int
+    rank = jnp.sum(earlier * hot_int, axis=-1).reshape(groups, rows, TOP_K)
+    group_ids = ids.reshape(groups, rows, TOP_K)
+    slot = jnp.where(rank < capacity, group_ids * capacity + rank, experts * capacity)
+    slot_hot = (slot[..., None] == jnp.arange(experts * capacity, dtype=jnp.int32)).astype(bf16)
+    token_hot = jnp.sum(slot_hot, axis=2)
+    slot_probs = jnp.sum(slot_hot.astype(f32) * probs.reshape(groups, rows, TOP_K, 1), axis=(1, 2))
+
+    def dispatch(values):
+        per_group = dot(token_hot, values.reshape(groups, rows, width), ((1,), (1,)), ((0,), (0,)))
+        per_group = per_group.reshape(groups, experts, capacity, width)
+        return jnp.transpose(per_group, (1, 0, 2, 3)).reshape(experts, groups * capacity, width)
+
+    def per_slot(values):
+        return jnp.transpose(values.reshape(groups, experts, capacity), (1, 0, 2)).reshape(experts, -1, 1)
+
+    def combine(slots):
+        per_group = jnp.transpose(slots.reshape(experts, groups, capacity, width), (1, 0, 2, 3))
+        per_group = per_group.reshape(groups, experts * capacity, width)
+        return dot(token_hot, per_group, ((2,), (1,)), ((0,), (0,))).reshape(lines, width)
+
+    slot_p = per_slot(slot_probs)
+    arrived = dispatch(mixed_line).astype(bf16)
+    cot_slots = dispatch(cot_rows)
+    pair_grad = (cot_slots * slot_p).astype(bf16)
+    batch = ((0,), (0,))
+    act = dot(arrived, egu, ((2,), (1,)), batch)
+    gate_act, up_act = act[..., :slice_ff], act[..., slice_ff:]
+    sig = jax.nn.sigmoid(gate_act)
+    silu_act = gate_act * sig
+    expert_hidden = (silu_act * up_act).astype(bf16)
+    expert_out = dot(expert_hidden, ed, ((2,), (1,)), batch)
+    hidden_grad = dot(pair_grad, ed, ((2,), (2,)), batch)
+    gate_up_grad = jnp.concatenate(
+        [hidden_grad * up_act * sig * (1.0 + gate_act * (1.0 - sig)), hidden_grad * silu_act], axis=-1
+    ).astype(bf16)
+    grad_egu = dot(arrived, gate_up_grad, ((1,), (1,)), batch).astype(bf16)
+    grad_ed = dot(expert_hidden, pair_grad, ((1,), (1,)), batch).astype(bf16)
+    slot_grad = dot(gate_up_grad, egu, ((2,), (2,)), batch).astype(bf16)
+    gate_dot = jnp.sum(cot_slots * expert_out, axis=-1)
+    gate_dot = jnp.transpose(gate_dot.reshape(experts, groups, capacity), (1, 0, 2)).reshape(groups, 1, 1, -1)
+    pair_dot = jnp.sum(slot_hot.astype(f32) * gate_dot, axis=-1).reshape(lines, TOP_K)
+    expert_sum = combine((expert_out * slot_p).astype(bf16))
+
+    s_act = dot(mixed_line, sgu, ((1,), (0,)))
+    s_in, s_lift = s_act[:, :slice_ff], s_act[:, slice_ff:]
+    s_sig = jax.nn.sigmoid(s_in)
+    s_silu = s_in * s_sig
+    s_hidden = (s_silu * s_lift).astype(bf16)
+    s_hidden_grad = dot(cot_rows, sd, ((1,), (1,)))
+    s_grad = jnp.concatenate(
+        [s_hidden_grad * s_lift * s_sig * (1.0 + s_in * (1.0 - s_sig)), s_hidden_grad * s_silu], axis=-1
+    ).astype(bf16)
+    grad_sgu = dot(mixed_line, s_grad, ((0,), (0,))).astype(bf16)
+    grad_sd = dot(s_hidden, cot_rows, ((0,), (0,))).astype(bf16)
+    out_part = (dot(s_hidden, sd, ((1,), (0,))) + expert_sum).astype(bf16)
+    mixed_part = combine(slot_grad) + dot(s_grad, sgu, ((1,), (1,)))
+    pair_dot = jnp.sum(hot * pair_dot[..., None], axis=1).reshape(nz, count, experts)
+    pair_dot = jnp.pad(jnp.transpose(pair_dot, (0, 2, 1)), ((0, 0), (0, EXTRA - experts), (0, width - count)))
+    mixed_part = jnp.concatenate([mixed_part.reshape(nz, count, width), pair_dot], axis=1).astype(bf16)
+    mixed_sum = sum_line(mixed_part.reshape(-1, width)).astype(f32)
+    return out_part, mixed_sum, (grad_egu, grad_sgu, grad_ed, grad_sd)
 
 
 def shards(
@@ -1182,9 +1531,8 @@
 
     cot = cotangent.reshape(count, width)
     pair_ids = routes.reshape(count, TOP_K)
-    cot_routes = jnp.concatenate(
-        [cot, pair_ids.astype(bf16), jnp.zeros((count, MISC - TOP_K), bf16)], axis=1
-    )
+    ids_rows = jnp.pad(pair_ids.T.astype(bf16), ((0, EXTRA - TOP_K), (0, width - count)))
+    cot_routes = jnp.concatenate([cot, ids_rows], axis=0)
     parts = (slices(expert_gate[0], expert_up[0]), slices(shared_gate, shared_up), expert_down[0], shared_down)
     fast = paired(batches, heads)
     if fast:
@@ -1214,94 +1562,24 @@
     else:
         context, saved = attention_forward(qkv, batches, heads, prefix)
         ffn, cot_line = gather_weights(*parts), gather_line(cot_routes)
-    egu, sgu, ed, sd = ffn
     context = jnp.transpose(context, (1, 0, 2)).reshape(width, count)
     attended = x_in + dot(context, w_out, ((0,), (0,)))
     ffn_scale = rms_scale(attended)
     ffn_norm = attended * ffn_scale
     mixed = (ffn_norm * gain_ffn).astype(bf16)
 
-    mixed_line = (gather_line_fast if fast else gather_line)(mixed)
-    cot_rows = cot_line[:, :width]
-    ids = cot_line[:, width : width + TOP_K].astype(jnp.int32)
-    lines = mixed_line.shape[0]
-    groups = lines // rows
-
-    def gates(mixed_rows, pair_ids):
-        hot = (pair_ids[..., None] == jnp.arange(experts, dtype=jnp.int32)).astype(f32)
-        logits = dot(mixed_rows, router_w, ((1,), (0,)))
-        return hot, jax.nn.softmax(jnp.sum(hot * logits[:, None, :], axis=-1), axis=-1)
-
-    hot, probs = gates(mixed_line, ids)
-    hot_int = hot.astype(jnp.int32).reshape(groups, rows * TOP_K, experts)
-    earlier = jnp.cumsum(hot_int, axis=1) - hot_int
-    rank = jnp.sum(earlier * hot_int, axis=-1).reshape(groups, rows, TOP_K)
-    group_ids = ids.reshape(groups, rows, TOP_K)
-    slot = jnp.where(rank < capacity, group_ids * capacity + rank, experts * capacity)
-    slot_hot = (slot[..., None] == jnp.arange(experts * capacity, dtype=jnp.int32)).astype(bf16)
-    token_hot = jnp.sum(slot_hot, axis=2)
-    slot_probs = jnp.sum(slot_hot.astype(f32) * probs.reshape(groups, rows, TOP_K, 1), axis=(1, 2))
-
-    def dispatch(values):
-        per_group = dot(token_hot, values.reshape(groups, rows, width), ((1,), (1,)), ((0,), (0,)))
-        per_group = per_group.reshape(groups, experts, capacity, width)
-        return jnp.transpose(per_group, (1, 0, 2, 3)).reshape(experts, groups * capacity, width)
-
-    def per_slot(values):
-        return jnp.transpose(values.reshape(groups, experts, capacity), (1, 0, 2)).reshape(experts, -1, 1)
-
-    def combine(slots):
-        per_group = jnp.transpose(slots.reshape(experts, groups, capacity, width), (1, 0, 2, 3))
-        per_group = per_group.reshape(groups, experts * capacity, width)
-        return dot(token_hot, per_group, ((2,), (1,)), ((0,), (0,))).reshape(lines, width)
-
-    slot_p = per_slot(slot_probs)
-    arrived = dispatch(mixed_line).astype(bf16)
-    cot_slots = dispatch(cot_rows)
-    pair_grad = (cot_slots * slot_p).astype(bf16)
-    batch = ((0,), (0,))
-    act = dot(arrived, egu, ((2,), (1,)), batch)
-    gate_act, up_act = act[..., :slice_ff], act[..., slice_ff:]
-    sig = jax.nn.sigmoid(gate_act)
-    silu_act = gate_act * sig
-    expert_hidden = (silu_act * up_act).astype(bf16)
-    expert_out = dot(expert_hidden, ed, ((2,), (1,)), batch)
-    hidden_grad = dot(pair_grad, ed, ((2,), (2,)), batch)
-    gate_up_grad = jnp.concatenate(
-        [hidden_grad * up_act * sig * (1.0 + gate_act * (1.0 - sig)), hidden_grad * silu_act], axis=-1
-    ).astype(bf16)
-    grad_egu = dot(arrived, gate_up_grad, ((1,), (1,)), batch).astype(bf16)
-    grad_ed = dot(expert_hidden, pair_grad, ((1,), (1,)), batch).astype(bf16)
-    slot_grad = dot(gate_up_grad, egu, ((2,), (2,)), batch).astype(bf16)
-    gate_dot = jnp.sum(cot_slots * expert_out, axis=-1)
-    gate_dot = jnp.transpose(gate_dot.reshape(experts, groups, capacity), (1, 0, 2)).reshape(groups, 1, 1, -1)
-    pair_dot = jnp.sum(slot_hot.astype(f32) * gate_dot, axis=-1).reshape(lines, TOP_K)
-    expert_sum = combine((expert_out * slot_p).astype(bf16))
-
-    s_act = dot(mixed_line, sgu, ((1,), (0,)))
-    s_in, s_lift = s_act[:, :slice_ff], s_act[:, slice_ff:]
-    s_sig = jax.nn.sigmoid(s_in)
-    s_silu = s_in * s_sig
-    s_hidden = (s_silu * s_lift).astype(bf16)
-    s_hidden_grad = dot(cot_rows, sd, ((1,), (1,)))
-    s_grad = jnp.concatenate(
-        [s_hidden_grad * s_lift * s_sig * (1.0 + s_in * (1.0 - s_sig)), s_hidden_grad * s_silu], axis=-1
-    ).astype(bf16)
-    grad_sgu = dot(mixed_line, s_grad, ((0,), (0,))).astype(bf16)
-    grad_sd = dot(s_hidden, cot_rows, ((0,), (0,))).astype(bf16)
-    out_part = (dot(s_hidden, sd, ((1,), (0,))) + expert_sum).astype(bf16)
-    mixed_part = combine(slot_grad) + dot(s_grad, sgu, ((1,), (1,)))
-    mixed_part = jnp.concatenate(
-        [mixed_part.astype(bf16), pair_dot.astype(bf16), jnp.zeros((lines, MISC - TOP_K), bf16)], axis=1
-    )
-    mixed_sum = (sum_line_fast if fast else sum_line)(mixed_part).astype(f32)
-
-    hot, probs = gates(mixed, pair_ids)
-    gate_grads = mixed_sum[:, width : width + TOP_K]
+    if fast:
+        router_rows = jnp.pad(router_w.T, ((0, 16 - experts), (0, 0)))
+        out_part, mixed_sum, ffn_grads = ffn_fast(mixed, cot_line, router_rows, ffn, capacity)
+    else:
+        out_part, mixed_sum, ffn_grads = ffn_plain(mixed, cot_line, router_w, ffn, capacity, rows)
+
+    hot, probs = gates(mixed, pair_ids, router_w)
+    gate_grads = jnp.sum(hot * mixed_sum[count : count + experts, :count].T[:, None, :], axis=-1)
     picked = probs * (gate_grads - jnp.sum(probs * gate_grads, axis=-1, keepdims=True))
     logit_grad = jnp.sum(hot * picked[..., None], axis=1)
     grad_router = jnp.dot(mixed.astype(f32).T, logit_grad, precision=highest)
-    mixed_grad = mixed_sum[:, :width] + jnp.dot(logit_grad, router_w.astype(f32).T, precision=highest)
+    mixed_grad = mixed_sum[:count] + jnp.dot(logit_grad, router_w.astype(f32).T, precision=highest)
     cot_wide = cot.astype(f32)
     inner = mixed_grad * gain_ffn
     grad_gffn = jnp.sum(mixed_grad * ffn_norm, axis=0)
@@ -1311,7 +1589,6 @@
     context_grad = dot(w_out, out_grad, ((1,), (1,))).astype(bf16)
     context_grad = jnp.transpose(context_grad.reshape(width, batches, rows), (1, 0, 2))
 
-    ffn_grads = (grad_egu, grad_sgu, grad_ed, grad_sd)
     if fast:
         rot_grad, (*lined, ed_sum, sd_sum), out_sum = backward_fast(prefix, context_grad, saved, *ffn_grads, out_part)
     else:

time: 543 us -> 410 us (0.76)
  matrix products: 102 us -> 17.8 us
  local copies, waits for them, and re-layouts: 84 us -> 53.8 us
  other arithmetic: 34.5 us -> 12.4 us
    dot_general x24 -> x7, matrix products: 97.8 us -> 14.1 us  [dot(): return lax.dot_general(a, b, (dims, batch), preferred_element_type=f32)]
    convert_element_type x6 -> x1, other arithmetic: 13.4 us -> 0.01 us  [shards(): pair_ids.T.astype(bf16)]
    unnamed x140 -> x71, local copies, waits for them, and re-layouts: 24.1 us -> 14.7 us
    pallas_call x2 -> x1, Pallas kernels: 61.7 us -> 70.9 us  [ffn_fast(): pl.pallas_call(functools.partial(ffn_kernel, capacity), out_shape=[jax.Sh...]
where the time goes in v4:
time: 410 us; the launch traced here: 405 us
  Pallas kernels  320 us (78%)
  local copies, waits for them, and re-layouts  53.8 us (13%)
  matrix products  17.8 us (4%)
  other arithmetic  12.4 us (3%)
    pallas_call x1, Pallas kernels, backward_fast(): pl.pallas_call(functools.partial(backward_kernel, nz, kinds), out_shape=[...  86.1 us
    pallas_call x1, Pallas kernels, attend_fast(): pl.pallas_call(functools.partial(attend_kernel, nz), out_shape=[jax.Shape...  75.6 us
    pallas_call x1, Pallas kernels, ffn_fast(): pl.pallas_call(functools.partial(ffn_kernel, capacity), out_shape=[jax.Sh...  70.9 us
    pallas_call x1, Pallas kernels, last_fast(): pl.pallas_call(functools.partial(last_kernel, nz), out_shape=[jax.ShapeDt...  46.8 us
    pallas_call x1, Pallas kernels, first_fast(): pl.pallas_call(functools.partial(first_kernel, nz), out_shape=[jax.ShapeD...  40.6 us
    unnamed x71, local copies, waits for them, and re-layouts  14.7 us
    dot_general x7, matrix products, dot(): return lax.dot_general(a, b, (dims, batch), preferred_element_type=f32)  14.1 us
    concatenate x3, local copies, waits for them, and re-layouts, shards(): jnp.concatenate([grad_wqkv, grad_wout, grad_misc], axis=1).astype(bf16)  8.99 us

profile of v4, /device:TPU:0, one launch (start us, length us, event | category | flops | bytes accessed | tf_op | source)
XLA Modules:
  0.0 405.4 jit_solution(4855906228449751228)
XLA Ops:
  4.6 1.3 stack_reshape_squeeze.7
  7.5 1.6 pad_maximum_fusion.2
  10.7 40.6 %first.1 = (bf16[32,24,3200]{2,1,0:T(8,128)(2,1)S(1)}, bf16[4,96,1024]{2,1,0:T(8,128)(2,1)S(1)}, bf16[4,24,1024]{2,1,0:T(8,128)(2,1)S(1)}) custom-call(bf16[24,3200]{1,0:T(8,128)(2,1)S(1)} %concatenate.23.refs_0_, bf16[4,96,1024]{2,1,0:T(8,128)(2,1)S(1)} %bitcast.93, bf16[4,24,1024]{2,1,0:T(8,128)(2,1)S(1)} %bitcast.99), custom_call_target="tpu_custom_call" | custom-call | tf_op jit(solution)/shard_map/first/pallas_call | solution.py:730
  56.6 1.5 copy.187
  58.2 75.6 %attend.1 = (bf16[2,768,128]{2,1,0:T(8,128)(2,1)S(1)}, bf16[3,192,1024]{2,1,0:T(8,128)(2,1)S(1)}, f32[3,1,1024]{2,1,0:T(1,128)S(1)}, bf16[4,8,96,1024]{3,2,1,0:T...) custom-call(s32[2,1]{1,0:T(2,128)S(1)} %copy.161.refs_0_, ...), custom_call_target="tpu_custom_call" | custom-call | tf_op jit(solution)/shard_map/attend/pallas_call | solution.py:631
  133.8 1.7 copy-done.1
  136.7 1.2 copy-done.3
  140.6 1.8 multiply_reduce_fusion.4
  145.0 70.9 %feed_forward.1 = (bf16[4,256,768]{2,1,0:T(8,128)(2,1)}, f32[272,768]{1,0:T(8,128)}, bf16[4,768,1024]{2,1,0:T(8,128)(2,1)}, bf16[768,1024]{1,0:T(8,128)(2,1)}, b...) custom-call(bf16[256,768]{1,0:T(8,128)(2,1)} %multiply_convert_fusion.refs_0_, bf16[4,272,768]{2,1,0:T(8,128)(2,1)} %copy-done.2, ...), custom_call_target="tpu_custom_call" | custom-call | tf_op jit(solution)/shard_map/feed_forward/pallas_call | solution.py:1357
  217.9 2.6 multiply_reduce_fusion
  220.7 1.8 convolution_convert_fusion.2
  223.4 86.1 %attend_backward.1 = (bf16[3,2,768,128]{3,2,1,0:T(8,128)(2,1)}, bf16[256,768]{1,0:T(8,128)(2,1)}, bf16[4,96,1024]{2,1,0:T(8,128)(2,1)}, bf16[4,24,1024]{2,1,0:T(...) custom-call(s32[2,1]{1,0:T(2,128)} %copy-done.12, bf16[2,768,128]{2,1,0:T(8,128)(2,1)} %bitcast.125, ...), custom_call_target="tpu_custom_call" | custom-call | tf_op jit(solution)/shard_map/attend_backward/pallas_call | solution.py:945
  309.6 2.0 add_convert_fusion.2
  313.7 1.2 slice_convert_fusion
  314.9 2.4 copy.166
  317.3 2.9 reshape.341
  321.5 3.9 multiply_reduce_fusion.1
  327.3 3.9 convolution_convert_fusion
  334.9 8.3 %concatenate.29.refs_0_ = bf16[32,24,3200]{2,1,0:T(8,128)(2,1)} concatenate(bf16[32,24,2304]{2,1,0:T(8,128)(2,1)} %convolution_convert_fusion, bf16[32,24,768]{2,1,0:T(8,128)(2,1)S(1)} %convolution_convert_fusion.1, bf16[32,24,4]{2,1,0:T(8,128)(2,1)S(1)} %copy.173, bf16[32,24,1]{2,1,0:T(8,128)(2,1)S(1)} %concatenate.30, bf16[32,24,1]{2,1,0:T(8,128)(2,1)S(1)} %concatenate.31, ...), dimensions={2} | concatenate | bytes 9830400 | tf_op jit(solution)/shard_map/concatenate | solution.py:1612
  343.2 2.4 copy-done
  345.6 46.8 %last.1 = (f32[24,3200]{1,0:T(8,128)S(1)}, bf16[4,96,1024]{2,1,0:T(8,128)(2,1)S(1)}, bf16[4,24,1024]{2,1,0:T(8,128)(2,1)S(1)}) custom-call(bf16[32,24,3200]{2,1,0:T(8,128)(2,1)S(1)} %copy-done, bf16[4,96,1024]{2,1,0:T(8,128)(2,1)S(1)} %copy-done.6, bf16[4,24,1024]{2,1,0:T(8,128)(2,1)S(1)} %copy-done.8), custom_call_target="tpu_custom_call" | custom-call | tf_op jit(solution)/shard_map/last/pallas_call | solution.py:1022
  397.6 1.5 reshape.344
  400.9 1.4 slice.123
  402.8 1.4 slice.125
  (145 shorter events, 39.0 us)
Async XLA Ops:
  0.6 5.9 %copy-start.21 = (bf16[1,96,2048]{2,1,0:T(8,128)(2,1)S(1)}, bf16[1,96,2048]{2,1,0:T(8,128)(2,1)}, u32[]{:S(2)}) copy-start(bf16[1,96,2048]{2,1,0:T(8,128)(2,1)} %param.31) | copy-start | bytes 1179652
  1.4 56.7 %copy-start.12 = (s32[2,1]{1,0:T(2,128)}, s32[2,1]{1,0:T(2,128)S(1)}, u32[]{:S(2)}) copy-start(s32[2,1]{1,0:T(2,128)S(1)} %copy.161.refs_0_) | copy-start | bytes 28
  7.4 2.2 copy-start.24
  7.5 2.5 copy-start.25
  9.7 41.9 %copy-start.14 = (bf16[2,1,128,768]{3,2,1,0:T(8,128)(2,1)S(1)}, bf16[2,1,128,768]{3,2,1,0:T(8,128)(2,1)}, u32[]{:S(2)}) copy-start(bf16[2,1,128,768]{3,2,1,0:T(8,128)(2,1)} %param.17) | copy-start | bytes 1179652
  51.3 2.1 copy-start.9
  51.8 1.7 copy-start.28
  52.0 1.7 copy-start.17
  56.6 1.5 copy-start.27
  56.6 1.5 copy-start.16
  56.6 1.6 copy-start.7
  56.6 1.6 copy-start.10
  133.8 1.7 copy-start.1
  135.4 1.2 copy-start.2
  136.7 1.2 copy-start.3
  145.0 71.6 %copy-start.13 = (bf16[256,768]{1,0:T(8,128)(2,1)S(1)}, bf16[256,768]{1,0:T(8,128)(2,1)}, u32[]{:S(2)}) copy-start(bf16[256,768]{1,0:T(8,128)(2,1)} %multiply_convert_fusion.refs_0_) | copy-start | bytes 1179652
  325.3 1.9 copy-start.20
  332.3 1.8 copy-start.31
  332.4 2.1 copy-start.30
  334.9 8.3 %copy-start.6 = (bf16[4,96,1024]{2,1,0:T(8,128)(2,1)S(1)}, bf16[4,96,1024]{2,1,0:T(8,128)(2,1)}, u32[]{:S(2)}) copy-start(bf16[4,96,1024]{2,1,0:T(8,128)(2,1)} %get-tuple-element.60.refs_1_) | copy-start | bytes 2359300
  334.9 8.3 %copy-start.8 = (bf16[4,24,1024]{2,1,0:T(8,128)(2,1)S(1)}, bf16[4,24,1024]{2,1,0:T(8,128)(2,1)}, u32[]{:S(2)}) copy-start(bf16[4,24,1024]{2,1,0:T(8,128)(2,1)} %get-tuple-element.61.refs_2_) | copy-start | bytes 589828
  343.2 2.4 copy-start
  393.1 3.8 copy-start.26
  402.3 1.9 copy-start.22
  (8 other events, 7.8 us)
